TPU v7x, 128 devices: a whole 4x4x4 slice. The times are simulated.
128 devices in a mesh: spec: 4 (over x_lo, core), tile: 32 (over z, y, x_hi).
Axes of the slice: x: 4 (x_hi: 2, x_lo: 2; x = x_hi * 2 + x_lo), y: 4, z: 4, core: 2. Of those that a mesh axis runs over, the one named last changes fastest.
Arguments:
- tracers: float32 [288, 8, 512, 128], P('spec', None, 'tile'), may hold values from -6 to 6
- courant: float32 [4, 512, 128], P(None, 'tile'), may hold values from 0.02 to 0.22
- neighbours: int32 [2, 512, 128], P(None, 'tile'), may hold values from 0 to 127, as said below
- owner_map: int32 [32, 128], P('tile'), may hold values from 0 to 127, each once within a row
- gain: float32 [288], replicated, may hold values from 0.25 to 1.75
- w_in: bfloat16 [288, 1024], replicated, may hold values from -0.375 to 0.375
- b_in: float32 [1024], replicated, may hold values from -3 to 3
- w_mid: bfloat16 [1024, 1024], replicated, may hold values from -0.1875 to 0.1875
- b_mid: float32 [1024], replicated, may hold values from -3 to 3
- w_out: bfloat16 [1024, 288], replicated, may hold values from -0.1875 to 0.1875
Outputs:
- tracers_out: float32 [288, 8, 512, 128], P('spec', None, 'tile')
- owned_tend: bfloat16 [128, 288, 4096], P(('spec', 'tile'))
Inputs may be any that keep to these rules, and one draw needn't show every extreme that they name: `neighbours`: for each cell, the y-index of its neighbour in the column before (first entry) and after (second), at most 3 rows away with wrap-around over 128. `owner_map`: each row names every owner once.
All inputs are finite; a program needn't handle non-finite values.
Results may differ from a plain program's by a relative error of at most 0.0065.
Values may be sent and summed in bfloat16 or wider, within the bound.
No kernel may reach another device: no remote copies, remote signals or barrier semaphores. Data moves between devices by JAX's collectives and lax.ppermute only.
A program may use at most 256 MiB of HBM per device.

v0:
```python
import jax
import jax.numpy as jnp
from jax import lax
from jax.sharding import PartitionSpec as P

STEPS = 2


def padded_2(cells, sides, width):
    for axis, dim in sides:
        count = lax.axis_size(axis)
        ends = count - 1
        head = lax.slice_in_dim(cells, 0, width, axis=dim)
        tail = lax.slice_in_dim(cells, cells.shape[dim] - width, cells.shape[dim], axis=dim)
        cells = jnp.concatenate(
            [
                lax.ppermute(tail, axis, [(i, (i + 1) % count) for i in range(ends)]),
                cells,
                lax.ppermute(head, axis, [((i + 1) % count, i) for i in range(ends)]),
            ],
            axis=dim,
        )
    return cells


def offset_masks(index_table):
    cols_y = index_table.shape[1]
    column = jnp.arange(cols_y, dtype=jnp.int32)[None, :]
    offset = (index_table - column) % cols_y
    return [(shift_by, offset == shift_by % cols_y) for shift_by in range(-3, 4)]


def pick_rows(field, masks):
    picked = jnp.zeros_like(field)
    for shift_by, mask in masks:
        picked = jnp.where(mask[None, None], jnp.roll(field, -shift_by, axis=3), picked)
    return picked


def advect(tracer_field, courant, west_masks, east_masks):
    padded = padded_2(tracer_field, (("tile", 2),), 1)
    west_side = pick_rows(padded[:, :, :-2, :], west_masks)
    east_side = pick_rows(padded[:, :, 2:, :], east_masks)
    north_side = jnp.roll(tracer_field, -1, axis=3)
    south_side = jnp.roll(tracer_field, 1, axis=3)
    return (
        tracer_field
        + courant[0] * (west_side - tracer_field)
        + courant[1] * (east_side - tracer_field)
        + courant[2] * (north_side - tracer_field)
        + courant[3] * (south_side - tracer_field)
    )


def surrogate(features, gain, w_in, b_in, w_mid, b_mid, w_out):
    values = features.astype(jnp.float32)
    inv_rms = lax.rsqrt(jnp.mean(values * values, axis=0, keepdims=True) + 1e-06)
    normed = (values * inv_rms * gain[:, None]).astype(jnp.bfloat16)
    contract = (((0,), (0,)), ((), ()))
    first_sum = lax.dot_general(w_in, normed, contract, preferred_element_type=jnp.float32)
    hidden_one = jax.nn.silu(first_sum + b_in[:, None]).astype(jnp.bfloat16)
    second = lax.dot_general(w_mid, hidden_one, contract, preferred_element_type=jnp.float32)
    hidden_two = jax.nn.silu(second + b_mid[:, None]).astype(jnp.bfloat16)
    return lax.dot_general(w_out, hidden_two, contract, preferred_element_type=jnp.float32).astype(
        jnp.bfloat16
    )


def shards(tracers, courant, neighbours, owner_map, gain, w_in, b_in, w_mid, b_mid, w_out):
    spec_dev, levels, rows_x, cols_y = tracers.shape
    n_spec = lax.axis_size("spec")
    n_tile = lax.axis_size("tile")
    devices = n_spec * n_tile
    block_cells = rows_x * cols_y // devices
    level_cells = levels * block_cells
    west_masks = offset_masks(neighbours[0])
    east_masks = offset_masks(neighbours[1])
    advected = tracers
    for substep in range(STEPS):
        advected = advect(advected, courant, west_masks, east_masks)
    owners = owner_map[0]
    inverse = jnp.zeros((devices,), jnp.int32).at[owners].set(jnp.arange(devices, dtype=jnp.int32))
    chem_in = advected.astype(jnp.bfloat16)
    blocks = chem_in.reshape(spec_dev, levels, devices, block_cells)
    by_owner = jnp.take(blocks, inverse, axis=2)
    arriving = lax.all_to_all(
        by_owner.transpose(2, 0, 1, 3).reshape(devices, spec_dev, level_cells),
        ("spec", "tile"),
        split_axis=0,
        concat_axis=0,
        tiled=True,
    )
    item_width = arriving.shape[2]
    group_item_width = arriving.shape[2]
    grouped = arriving.reshape(n_spec, n_tile, spec_dev, group_item_width).transpose(0, 2, 1, 3)
    owner_tend = surrogate(
        grouped.reshape(n_spec * spec_dev, n_tile * group_item_width),
        gain,
        w_in,
        b_in,
        w_mid,
        b_mid,
        w_out,
    )
    owner_tend = owner_tend.reshape(n_spec * spec_dev, n_tile, item_width)
    item_width = owner_tend.shape[2]
    sending = owner_tend.reshape(n_spec, spec_dev, n_tile, item_width).transpose(0, 2, 1, 3)
    returned_piece = lax.all_to_all(
        sending.reshape(devices, spec_dev, item_width),
        ("spec", "tile"),
        split_axis=0,
        concat_axis=0,
        tiled=True,
    )
    owned_tend = owner_tend.reshape(1, n_spec * spec_dev, n_tile * level_cells)
    back_blocks = jnp.take(returned_piece, owners, axis=0)
    tendency = back_blocks.reshape(devices, spec_dev, levels, block_cells).transpose(1, 2, 0, 3)
    tendency = tendency.reshape(spec_dev, levels, rows_x, cols_y)
    return (advected + tendency.astype(jnp.float32), owned_tend)


def solution(mesh):
    return jax.shard_map(
        shards,
        mesh=mesh,
        in_specs=(
            P("spec", None, "tile", None),
            P(None, "tile", None),
            P(None, "tile", None),
            P("tile", None),
            P(),
            P(),
            P(),
            P(),
            P(),
            P(),
        ),
        out_specs=(P("spec", None, "tile", None), P(("spec", "tile"), None, None)),
        check_vma=False,
    )
```

profile of v0, /device:TPU:1, one launch (start us, length us, event | category | flops | bytes accessed | tf_op | source)
XLA Modules:
  0.0 469.3 jit_solution(3567763449786395668)
XLA Ops:
  0.7 8.1 %copy.78 = f32[72,8,16,128]{0,3,2,1:T(8,128)} copy(f32[72,8,16,128]{3,2,1,0:T(8,128)} %param.10) | data formatting | bytes 9437184 | tf_op args[0]
  11.1 5.5 %collective-permute-start = (f32[72,8,1,128]{0,3,2,1:T(8,128)}, f32[72,8,1,128]{0,3,2,1:T(8,128)S(1)}, u32[]{:S(2)}, u32[]{:S(2)}) collective-permute-start(f32[72,8,1,128]{0,3,2,1:T(8,128)} %get-tuple-element.90), channel_id=1, source_target_pairs={{0,1},{1,2},{2,3},{3,4},{4,5},{5,6},{6,7},{7,8},{8,9},{9,10},{10,1... | collective-permute-start | bytes 884744 | tf_op jit(solution)/shard_map/ppermute | solution.py:17
  19.1 8.3 %collective-permute-done = f32[72,8,1,128]{0,3,2,1:T(8,128)S(1)} collective-permute-done((f32[72,8,1,128]{0,3,2,1:T(8,128)}, f32[72,8,1,128]{0,3,2,1:T(8,128)S(1)}, u32[]{:S(2)}, u32[]{:S(2)}) %collective-permute-start) | collective-permute-done | bytes 294944 | tf_op jit(solution)/shard_map/ppermute | solution.py:17
  27.4 13.1 %collective-permute-done.1 = f32[72,8,1,128]{0,3,2,1:T(8,128)S(1)} collective-permute-done((f32[72,8,1,128]{0,3,2,1:T(8,128)}, f32[72,8,1,128]{0,3,2,1:T(8,128)S(1)}, u32[]{:S(2)}, u32[]{:S(2)}) %collective-permute-start.1) | collective-permute-done | bytes 294944 | tf_op jit(solution)/shard_map/ppermute | solution.py:19
  40.5 32.6 %fusion.49 = (f32[72,8,16,127]{0,3,2,1:T(8,128)}, f32[72,8,16,127]{0,3,2,1:T(8,128)}, f32[72,8,16,127]{0,3,2,1:T(8,128)}, f32[72,8,16,127]{0,3,2,1:T(8,128)}, f3...) fusion(f32[72,8,1,128]{0,3,2,1:T(8,128)S(1)} %collective-permute-done.1, f32[72,8,16,128]{0,3,2,1:T(8,128)} %copy.78, ...), kind=kLoop, calls=%fused_computation.104 | loop fusion | flops 4681728 | bytes 53846016 | tf_op jit(solution)/shard_map/concatenate | solution.py:15
  77.5 11.2 %fusion.50 = (f32[72,8,16,126]{0,3,2,1:T(8,128)}, f32[72,8,16,126]{0,3,2,1:T(8,128)}, f32[72,8,16,126]{0,3,2,1:T(8,128)}, f32[72,8,16,126]{0,3,2,1:T(8,128)}) fusion(f32[72,8,1,128]{0,3,2,1:T(8,128)S(1)} %collective-permute-done.1, f32[72,8,16,128]{0,3,2,1:T(8,128)S(1)} %copy-done.1, f32[72,8,1,128]{0,3,2,1:T(8,128)S(1)} %collective-permute-done), kind=kLoop, calls=%fused_computation.105 | loop fusion | flops 4644864 | bytes 23887872 | tf_op jit(solution)/shard_map/concatenate | solution.py:15
  89.0 7.3 %fusion.36 = (f32[72,8,16,125]{0,3,2,1:T(8,128)}, f32[72,8,16,125]{0,3,2,1:T(8,128)}) fusion(f32[72,8,1,128]{0,3,2,1:T(8,128)S(1)} %collective-permute-done.1, f32[72,8,16,128]{0,3,2,1:T(8,128)S(1)} %copy-done.1, f32[72,8,1,128]{0,3,2,1:T(8,128)S(1)} %collective-permute-done), kind=kLoop, calls=%fused_computation.91 | loop fusion | flops 2304000 | bytes 14524416 | tf_op jit(solution)/shard_map/concatenate | solution.py:15
  96.5 51.9 %fusion.48 = f32[72,8,16,128]{0,3,2,1:T(8,128)} fusion(f32[72,8,16,128]{0,3,2,1:T(8,128)} %copy.78, f32[72,8,1,128]{0,3,2,1:T(8,128)S(1)} %collective-permute-done.1, f32[72,8,1,128]{0,3,2,1:T(8,128)S(1)} %collective-permute-done, f32[72,8,16,3]{0,3,2,1:T(4,128)S(1)} %get-tuple-element.78, f32[72,8,16,125]{0,3,2,1:T(8,128)} %get-tuple-element.89, ...), kind=kLoop, calls=%fused_computation.103 | loop fusion | flops 51904512 | bytes 66932736 | tf_op jit(solution)/shard_map/add | solution.py:47
  157.0 6.9 %collective-permute-done.2 = f32[72,8,1,128]{0,3,2,1:T(8,128)S(1)} collective-permute-done((f32[72,8,1,128]{0,3,2,1:T(8,128)S(1)}, f32[72,8,1,128]{0,3,2,1:T(8,128)S(1)}, u32[]{:S(2)}, u32[]{:S(2)}) %collective-permute-start.2) | collective-permute-done | bytes 294944 | tf_op jit(solution)/shard_map/ppermute | solution.py:17
  163.9 13.2 %collective-permute-done.3 = f32[72,8,1,128]{0,3,2,1:T(8,128)S(1)} collective-permute-done((f32[72,8,1,128]{0,3,2,1:T(8,128)S(1)}, f32[72,8,1,128]{0,3,2,1:T(8,128)S(1)}, u32[]{:S(2)}, u32[]{:S(2)}) %collective-permute-start.3) | collective-permute-done | bytes 294944 | tf_op jit(solution)/shard_map/ppermute | solution.py:19
  177.1 10.6 %fusion.23 = (f32[72,8,16,125]{0,3,2,1:T(8,128)}, f32[72,8,16,125]{0,3,2,1:T(8,128)}) fusion(f32[72,8,1,128]{0,3,2,1:T(8,128)S(1)} %collective-permute-done.2, f32[72,8,16,128]{0,3,2,1:T(8,128)} %fusion.48, f32[72,8,1,128]{0,3,2,1:T(8,128)S(1)} %collective-permute-done.3), kind=kLoop, calls=%fused_computation.78 | loop fusion | flops 2304000 | bytes 14524416 | tf_op jit(solution)/shard_map/concatenate | solution.py:15
  187.9 11.1 %fusion.24 = (f32[72,8,16,126]{0,3,2,1:T(8,128)}, f32[72,8,16,126]{0,3,2,1:T(8,128)}, f32[72,8,16,126]{0,3,2,1:T(8,128)}, f32[72,8,16,126]{0,3,2,1:T(8,128)}) fusion(f32[72,8,1,128]{0,3,2,1:T(8,128)S(1)} %collective-permute-done.2, f32[72,8,16,128]{0,3,2,1:T(8,128)S(1)} %bitcast.101, f32[72,8,1,128]{0,3,2,1:T(8,128)S(1)} %collective-permute-done.3), kind=kLoop, calls=%fused_computation.79 | loop fusion | flops 4644864 | bytes 23887872 | tf_op jit(solution)/shard_map/concatenate | solution.py:15
  199.4 34.5 %fusion.25 = (f32[72,8,16,127]{0,3,2,1:T(8,128)}, f32[72,8,16,127]{0,3,2,1:T(8,128)}, f32[72,8,16,127]{0,3,2,1:T(8,128)}, f32[72,8,16,127]{0,3,2,1:T(8,128)}, f3...) fusion(f32[72,8,1,128]{0,3,2,1:T(8,128)S(1)} %collective-permute-done.2, f32[72,8,16,128]{0,3,2,1:T(8,128)} %fusion.48, ...), kind=kLoop, calls=%fused_computation.80 | loop fusion | flops 4681728 | bytes 53846016 | tf_op jit(solution)/shard_map/concatenate | solution.py:15
  233.9 53.5 %fusion.134 = (bf16[72,8,16,128]{0,3,2,1:T(8,128)(2,1)}, f32[72,8,16,128]{0,3,2,1:T(8,128)}) fusion(f32[72,8,16,128]{0,3,2,1:T(8,128)} %fusion.48, f32[72,8,16,127]{0,3,2,1:T(8,128)} %get-tuple-element.67, f32[72,8,16,1]{0,3,2,1:T(1,128)S(1)} %get-tuple-element.71, f32[16,128]{1,0:T(8,128)S(1)} %get-tuple-element.94, ...), kind=kLoop, calls=%fused_computation.248 | loop fusion | flops 53084160 | bytes 69292032 | tf_op jit(solution)/shard_map/convert_element_type | solution.py:83
  287.4 5.6 %gather_fusion = bf16[128,72,8,16]{1,3,2,0:T(8,128)(2,1)} fusion(bf16[72,8,128,16]{0,3,2,1:T(8,128)(2,1)} %bitcast.102, s32[1024]{0:T(1024)} %pad_clamp_fusion.1), kind=kCustom, calls=%fused_computation | custom fusion | bytes 4719104 | tf_op jit(solution)/shard_map/jit(_take)/gather | solution.py:85
  297.7 5.7 %copy.89 = bf16[128,72,128]{2,1,0:T(8,128)(2,1)} copy(bf16[128,72,128]{1,2,0:T(8,128)(2,1)} %bitcast.106) | data formatting | bytes 4718592 | tf_op jit(solution)/shard_map/reshape | solution.py:87
  303.3 45.9 %all_to_all.10 = bf16[128,72,128]{2,1,0:T(8,128)(2,1)S(1)} all-to-all(bf16[128,72,128]{2,1,0:T(8,128)(2,1)} %copy.89), channel_id=1, replica_groups=mesh['spec'=4,'tile'=32] {'spec','tile'}, dimensions={0} | all-to-all | bytes 4718592 | tf_op jit(solution)/shard_map/all_to_all | solution.py:86
  353.4 17.8 %fusion.99 = f32[4096,1024]{1,0:T(8,128)} fusion(bf16[288,1024]{1,0:T(8,128)(2,1)S(1)} %copy-done.2, f32[36,8,32,128]{3,2,1,0:T(8,128)} %bitcast.104, f32[288]{0:T(512)S(1)} %copy-done.19, f32[4096]{0:T(1024)S(1)} %rsqrt_bitcast_fusion), kind=kOutput, calls=%fused_computation.181 | convolution fusion | flops 2419458048 | bytes 22103168 | tf_op jit(solution)/shard_map/dot_general | solution.py:60
  371.2 18.8 %fusion.92 = bf16[4096,288]{0,1:T(8,128)(2,1)} fusion(bf16[1024,288]{0,1:T(8,128)(2,1)S(1)} %copy-done.23, f32[1024]{0:T(1024)S(1)} %copy-done.24, bf16[1024,1024]{1,0:T(8,128)(2,1)S(1)} %copy-done, f32[4096,1024]{1,0:T(8,128)} %fusion.99, f32[1024]{0:T(1024)S(1)} %copy-done.25), kind=kOutput, calls=%fused_computation.175 | convolution fusion | flops 11057364992 | bytes 21831680 | tf_op jit(solution)/shard_map/dot_general | solution.py:64
  394.6 5.2 %all-to-all-start.1 = ((bf16[128,72,128]{2,1,0:T(8,128)(2,1)}), bf16[128,72,128]{2,1,0:T(8,128)(2,1)}, u32[]{:S(2)}, u32[]{:S(2)}) async-start(bf16[128,72,128]{2,1,0:T(8,128)(2,1)} %bitcast.108), calls=%async_computation.1 | async-start | bytes 4718592 | tf_op jit(solution)/shard_map/all_to_all | solution.py:108
  399.8 33.1 %all-to-all-done.1 = bf16[128,72,128]{2,1,0:T(8,128)(2,1)} async-done(((bf16[128,72,128]{2,1,0:T(8,128)(2,1)}), bf16[128,72,128]{2,1,0:T(8,128)(2,1)}, u32[]{:S(2)}, u32[]{:S(2)}) %all-to-all-start.1) | async-done | bytes 2359328 | tf_op jit(solution)/shard_map/all_to_all | solution.py:108
  437.0 5.6 %copy.100 = bf16[128,72,128]{1,2,0:T(8,128)(2,1)} copy(bf16[128,72,128]{2,1,0:T(8,128)(2,1)} %gather_fusion.1) | data formatting | bytes 4718592 | tf_op jit(solution)/shard_map/jit(_take)/gather | solution.py:116
  449.3 11.7 %bitcast_add_fusion = f32[72,8,16,128]{0,3,2,1:T(8,128)} fusion(f32[72,8,16,128]{0,3,2,1:T(8,128)} %get-tuple-element.11, f32[72,8,16,128]{0,3,2,1:T(8,128)} %bitcast.103), kind=kLoop, calls=%fused_computation.147 | loop fusion | flops 1179648 | bytes 14155776 | tf_op jit(solution)/shard_map/add | solution.py:119
  461.1 8.0 %copy.97 = f32[72,8,16,128]{3,2,1,0:T(8,128)} copy(f32[72,8,16,128]{0,3,2,1:T(8,128)} %bitcast_add_fusion) | data formatting | bytes 9437184
  (94 shorter events, 42.8 us)
Async XLA Ops:
  0.6 370.6 %copy-start = (bf16[1024,1024]{1,0:T(8,128)(2,1)S(1)}, bf16[1024,1024]{1,0:T(8,128)(2,1)}, u32[]{:S(2)}) copy-start(bf16[1024,1024]{1,0:T(8,128)(2,1)} %param.17) | copy-start | bytes 6291460
  11.1 16.4 %collective-permute-start = (f32[72,8,1,128]{0,3,2,1:T(8,128)}, f32[72,8,1,128]{0,3,2,1:T(8,128)S(1)}, u32[]{:S(2)}, u32[]{:S(2)}) collective-permute-start(f32[72,8,1,128]{0,3,2,1:T(8,128)} %get-tuple-element.90), channel_id=1, source_target_pairs={{0,1},{1,2},{2,3},{3,4},{4,5},{5,6},{6,7},{7,8},{8,9},{9,10},{10,1... | collective-permute-start | bytes 884744 | tf_op jit(solution)/shard_map/ppermute | solution.py:17
  16.6 24.0 %collective-permute-start.1 = (f32[72,8,1,128]{0,3,2,1:T(8,128)}, f32[72,8,1,128]{0,3,2,1:T(8,128)S(1)}, u32[]{:S(2)}, u32[]{:S(2)}) collective-permute-start(f32[72,8,1,128]{0,3,2,1:T(8,128)} %get-tuple-element.91), channel_id=1, source_target_pairs={{1,0},{2,1},{3,2},{4,3},{5,4},{6,5},{7,6},{8,7},{9,8},{10,9},{11,1... | collective-permute-start | bytes 884744 | tf_op jit(solution)/shard_map/ppermute | solution.py:19
  17.9 78.4 %copy-start.5 = (pred[16,128]{1,0:T(8,128)(4,1)}, pred[16,128]{1,0:T(8,128)(4,1)S(1)}, u32[]{:S(2)}) copy-start(pred[16,128]{1,0:T(8,128)(4,1)S(1)} %get-tuple-element.96) | copy-start | bytes 6148
  17.9 78.4 %copy-start.3 = (f32[16,128]{1,0:T(8,128)}, f32[16,128]{1,0:T(8,128)S(1)}, u32[]{:S(2)}) copy-start(f32[16,128]{1,0:T(8,128)S(1)} %get-tuple-element.95) | copy-start | bytes 24580
  19.0 77.3 %copy-start.6 = (pred[16,128]{1,0:T(8,128)(4,1)}, pred[16,128]{1,0:T(8,128)(4,1)S(1)}, u32[]{:S(2)}) copy-start(pred[16,128]{1,0:T(8,128)(4,1)S(1)} %get-tuple-element.104) | copy-start | bytes 6148
  19.0 77.3 %copy-start.7 = (pred[16,128]{1,0:T(8,128)(4,1)}, pred[16,128]{1,0:T(8,128)(4,1)S(1)}, u32[]{:S(2)}) copy-start(pred[16,128]{1,0:T(8,128)(4,1)S(1)} %get-tuple-element.105) | copy-start | bytes 6148
  19.0 77.3 %copy-start.8 = (pred[16,128]{1,0:T(8,128)(4,1)}, pred[16,128]{1,0:T(8,128)(4,1)S(1)}, u32[]{:S(2)}) copy-start(pred[16,128]{1,0:T(8,128)(4,1)S(1)} %get-tuple-element.106) | copy-start | bytes 6148
  19.1 77.3 %copy-start.9 = (pred[16,128]{1,0:T(8,128)(4,1)}, pred[16,128]{1,0:T(8,128)(4,1)S(1)}, u32[]{:S(2)}) copy-start(pred[16,128]{1,0:T(8,128)(4,1)S(1)} %get-tuple-element.107) | copy-start | bytes 6148
  19.1 77.3 %copy-start.10 = (pred[16,128]{1,0:T(8,128)(4,1)}, pred[16,128]{1,0:T(8,128)(4,1)S(1)}, u32[]{:S(2)}) copy-start(pred[16,128]{1,0:T(8,128)(4,1)S(1)} %get-tuple-element.108) | copy-start | bytes 6148
  19.1 77.3 %copy-start.11 = (pred[16,128]{1,0:T(8,128)(4,1)}, pred[16,128]{1,0:T(8,128)(4,1)S(1)}, u32[]{:S(2)}) copy-start(pred[16,128]{1,0:T(8,128)(4,1)S(1)} %get-tuple-element.109) | copy-start | bytes 6148
  19.1 77.3 %copy-start.12 = (pred[16,128]{1,0:T(8,128)(4,1)}, pred[16,128]{1,0:T(8,128)(4,1)S(1)}, u32[]{:S(2)}) copy-start(pred[16,128]{1,0:T(8,128)(4,1)S(1)} %get-tuple-element.110) | copy-start | bytes 6148
  19.1 77.3 %copy-start.13 = (pred[16,128]{1,0:T(8,128)(4,1)}, pred[16,128]{1,0:T(8,128)(4,1)S(1)}, u32[]{:S(2)}) copy-start(pred[16,128]{1,0:T(8,128)(4,1)S(1)} %get-tuple-element.111) | copy-start | bytes 6148
  19.1 77.3 %copy-start.14 = (pred[16,128]{1,0:T(8,128)(4,1)}, pred[16,128]{1,0:T(8,128)(4,1)S(1)}, u32[]{:S(2)}) copy-start(pred[16,128]{1,0:T(8,128)(4,1)S(1)} %get-tuple-element.112) | copy-start | bytes 6148
  19.1 77.3 %copy-start.15 = (pred[16,128]{1,0:T(8,128)(4,1)}, pred[16,128]{1,0:T(8,128)(4,1)S(1)}, u32[]{:S(2)}) copy-start(pred[16,128]{1,0:T(8,128)(4,1)S(1)} %get-tuple-element.113) | copy-start | bytes 6148
  19.1 77.3 %copy-start.16 = (pred[16,128]{1,0:T(8,128)(4,1)}, pred[16,128]{1,0:T(8,128)(4,1)S(1)}, u32[]{:S(2)}) copy-start(pred[16,128]{1,0:T(8,128)(4,1)S(1)} %get-tuple-element.114) | copy-start | bytes 6148
  19.1 77.3 %copy-start.17 = (pred[16,128]{1,0:T(8,128)(4,1)}, pred[16,128]{1,0:T(8,128)(4,1)S(1)}, u32[]{:S(2)}) copy-start(pred[16,128]{1,0:T(8,128)(4,1)S(1)} %get-tuple-element.115) | copy-start | bytes 6148
  149.6 14.3 %collective-permute-start.2 = (f32[72,8,1,128]{0,3,2,1:T(8,128)S(1)}, f32[72,8,1,128]{0,3,2,1:T(8,128)S(1)}, u32[]{:S(2)}, u32[]{:S(2)}) collective-permute-start(f32[72,8,1,128]{0,3,2,1:T(8,128)S(1)} %get-tuple-element.72), channel_id=1, source_target_pairs={{0,1},{1,2},{2,3},{3,4},{4,5},{5,6},{6,7},{7,8},{8,9},{9,10},{10,1... | collective-permute-start | bytes 884744 | tf_op jit(solution)/shard_map/ppermute | solution.py:17
  154.3 22.8 %collective-permute-start.3 = (f32[72,8,1,128]{0,3,2,1:T(8,128)S(1)}, f32[72,8,1,128]{0,3,2,1:T(8,128)S(1)}, u32[]{:S(2)}, u32[]{:S(2)}) collective-permute-start(f32[72,8,1,128]{0,3,2,1:T(8,128)S(1)} %get-tuple-element.73), channel_id=1, source_target_pairs={{1,0},{2,1},{3,2},{4,3},{5,4},{6,5},{7,6},{8,7},{9,8},{10,9},{11,1... | collective-permute-start | bytes 884744 | tf_op jit(solution)/shard_map/ppermute | solution.py:19
  156.5 31.2 %slice-start = ((s8[8388608]{0:T(1024)(128)(4,1)}), s8[4194304]{0:T(1024)(128)(4,1)S(1)}, s32[]{:S(2)}) async-start(s8[8388608]{0:T(1024)(128)(4,1)} %bitcast.100), calls=%async_computation.2 | async-start | bytes 8388608
  157.0 30.7 %slice-start.1 = ((s8[8388608]{0:T(1024)(128)(4,1)}), s8[4194304]{0:T(1024)(128)(4,1)S(1)}, s32[]{:S(2)}) async-start(s8[8388608]{0:T(1024)(128)(4,1)} %bitcast.100), calls=%async_computation.3 | async-start | bytes 8388608
  353.4 17.8 %copy-start.23 = (bf16[1024,288]{0,1:T(8,128)(2,1)S(1)}, bf16[1024,288]{0,1:T(8,128)(2,1)}, u32[]{:S(2)}) copy-start(bf16[1024,288]{0,1:T(8,128)(2,1)} %param.19) | copy-start | bytes 1769476
  353.4 17.8 %copy-start.24 = (f32[1024]{0:T(1024)S(1)}, f32[1024]{0:T(1024)}, u32[]{:S(2)}) copy-start(f32[1024]{0:T(1024)} %param.18) | copy-start | bytes 12292
  394.6 38.4 %all-to-all-start.1 = ((bf16[128,72,128]{2,1,0:T(8,128)(2,1)}), bf16[128,72,128]{2,1,0:T(8,128)(2,1)}, u32[]{:S(2)}, u32[]{:S(2)}) async-start(bf16[128,72,128]{2,1,0:T(8,128)(2,1)} %bitcast.108), calls=%async_computation.1 | async-start | bytes 4718592 | tf_op jit(solution)/shard_map/all_to_all | solution.py:108
  (11 other events, 108.4 us)
where the time goes:
time: 477 us; the launch traced here: 469 us
  other arithmetic  237 us (50%)
  waiting for transfers between devices  74.6 us (16%)
  local copies, waits for them, and re-layouts  55 us (12%)
  blocking collectives  45.9 us (10%)
  matrix products  36.6 us (8%)
  starting transfers between devices  18.2 us (4%)
    concatenate x12, other arithmetic, padded_2(): jnp.concatenate([lax.ppermute(tail, axis, [(i, (i + 1) % count) for i in...  111 us
    convert_element_type x1, other arithmetic, shards(): chem_in = advected.astype(jnp.bfloat16)  53.5 us
    add x1, other arithmetic, advect(): tracer_field + courant[0] * (west_side - tracer_field)  51.9 us
    all_to_all x1, blocking collectives, shards(): lax.all_to_all(by_owner.transpose(2, 0, 1, 3).reshape(devices, spec_dev,...  45.9 us
    all_to_all x1, waiting for transfers between devices, shards(): lax.all_to_all(sending.reshape(devices, spec_dev, item_width), ('spec', '...  33.1 us
    ppermute x2, waiting for transfers between devices, padded_2(): lax.ppermute(head, axis, [((i + 1) % count, i) for i in range(ends)])  26.3 us
    unnamed x63, local copies, waits for them, and re-layouts  20.3 us
    dot_general x1, matrix products, surrogate(): lax.dot_general(w_out, hidden_two, contract, preferred_element_type=jnp.f...  18.8 us
  transfers between devices with their start and end apart: 5, of which 5 were waited for; matrix products, arithmetic and copies ran while one was open for 0% of the time, Pallas kernels for 0%

commit v1 on v0

v1 whole, which is shorter than its diff:
```python
import functools

import jax
import jax.numpy as jnp
from jax import lax
from jax.experimental import pallas as pl
from jax.experimental.pallas import tpu as pltpu
from jax.sharding import PartitionSpec as P

LEV = 8
COLS = 16
CY = 128
BLOCK = 16
GROUP = 8
EXTRA = 16
MIB = 1024 * 1024
AXES = ("spec", "tile")
f32, bf16, i32 = jnp.float32, jnp.bfloat16, jnp.int32


def whole(shape):
    return pl.BlockSpec(shape, lambda *_: (0,) * len(shape))


def smem():
    return pl.BlockSpec(memory_space=pltpu.SMEM)


def pack_kernel(tr, courant, nbr, west, east, edge, extra):
    step = pl.program_id(0)
    species = 72
    for side, cols in ((0, (14, 15)), (1, (0, 1))):
        for j, x in enumerate(cols):
            for l in range(LEV):
                rows = tr[pl.ds(l * COLS + x, GROUP, stride=LEV * COLS), :]
                at = pl.multiple_of((j * LEV + l) * species + step * GROUP, GROUP)
                edge[side, pl.ds(at, GROUP), :] = rows

    @pl.when(step == pl.num_programs(0) - 1)
    def _():
        for side, x, out in ((0, 15, west), (1, 0, east)):
            n = 2 * LEV * species
            extra[...] = jnp.zeros_like(extra)
            for i in range(4):
                c = courant[i, x : x + 1, :]
                high = c.astype(bf16).astype(f32)
                extra[i : i + 1, :] = high
                extra[4 + i : 5 + i, :] = c - high
            for i in range(2):
                extra[8 + i : 9 + i, :] = nbr[i, x : x + 1, :].astype(f32)
            out[0:n, :] = edge[side].astype(bf16)
            out[n : n + EXTRA, :] = extra[...].astype(bf16)


def pack_halo(rows, courant, nbr):
    n = rows.shape[0] // (LEV * COLS)
    total = 2 * LEV * n + EXTRA
    out = jax.ShapeDtypeStruct((total, CY), bf16)
    return pl.pallas_call(
        pack_kernel,
        grid=(n // GROUP,),
        in_specs=[
            pl.BlockSpec((GROUP * LEV * COLS, CY), lambda c: (c, 0)),
            whole(courant.shape),
            whole(nbr.shape),
        ],
        out_specs=[whole((total, CY))] * 2,
        out_shape=[out, out],
        scratch_shapes=[pltpu.VMEM((2, 2 * LEV * n, CY), f32), pltpu.VMEM((EXTRA, CY), f32)],
        compiler_params=pltpu.CompilerParams(vmem_limit_bytes=32 * MIB),
        cost_estimate=pl.CostEstimate(flops=0, bytes_accessed=6 * MIB, transcendentals=0),
        name="pack_halo",
    )(rows, courant, nbr)


def lane_block():
    return lax.broadcasted_iota(i32, (GROUP, CY), 1) // BLOCK


def swap_blocks(tiles):
    place = lane_block()
    n = len(tiles)
    cur = [t if a == 0 else pltpu.roll(t, a * BLOCK, 1) for a, t in enumerate(tiles)]
    for bit in (1, 2, 4):
        mask = (place & bit) != 0
        cur = [jnp.where(mask, cur[(i + bit) % n], cur[i]) for i in range(n)]
    out = []
    for k in range(n):
        v = cur[(-k) % n]
        out.append(v if k == 0 else pltpu.roll(v, CY - k * BLOCK, 1))
    return out


def transport_kernel(place, tr, courant, nbr, west, east, adv, m0, m1, m2, m3, halo, coef, index, field, mid, msg):
    step = pl.program_id(0)
    species = 72
    n = 2 * LEV * species

    @pl.when(step == 0)
    def _():
        for side, src in ((0, west), (1, east)):
            halo[side] = src[...].astype(f32)
        for x in range(-1, COLS + 1):
            if x < 0 or x == COLS:
                side = 0 if x < 0 else 1
                c = [halo[side, n + i : n + i + 1, :] + halo[side, n + 4 + i : n + 5 + i, :] for i in range(4)]
                ind = [halo[side, n + 8 + i : n + 9 + i, :].astype(i32) for i in range(2)]
            else:
                c = [courant[i, x : x + 1, :] for i in range(4)]
                ind = [nbr[i, x : x + 1, :] for i in range(2)]
            c = c + [1.0 - (c[0] + c[1] + c[2] + c[3])]
            for i in range(5):
                coef[x + 1, i] = jnp.broadcast_to(c[i], (GROUP, CY))
            for i in range(2):
                index[x + 1, i] = jnp.broadcast_to(ind[i], (GROUP, CY))

    for l in range(LEV):
        for j in range(2):
            at = pl.multiple_of((j * LEV + l) * species + step * GROUP, GROUP)
            field[j, l] = halo[0, pl.ds(at, GROUP), :]
            field[COLS + 2 + j, l] = halo[1, pl.ds(at, GROUP), :]
        for x in range(COLS):
            field[x + 2, l] = tr[pl.ds(l * COLS + x, GROUP, stride=LEV * COLS), :]

    def move(src, at, l, c, ind):
        here = src[at, l]
        w = jnp.take_along_axis(src[at - 1, l], ind[0], axis=1, mode="promise_in_bounds")
        e = jnp.take_along_axis(src[at + 1, l], ind[1], axis=1, mode="promise_in_bounds")
        up = pltpu.roll(here, CY - 1, 1)
        down = pltpu.roll(here, 1, 1)
        return c[0] * w + c[1] * e + c[2] * up + c[3] * down + c[4] * here

    def first(x, _):
        c = [coef[x, i] for i in range(5)]
        ind = [index[x, i] for i in range(2)]
        for l in range(LEV):
            mid[x, l] = move(field, x + 1, l, c, ind)
        return 0

    lax.fori_loop(0, COLS + 2, first, 0)

    def second(x, _):
        c = [coef[x + 1, i] for i in range(5)]
        ind = [index[x + 1, i] for i in range(2)]
        tiles = [move(mid, x + 1, l, c, ind) for l in range(LEV)]
        for l in range(LEV):
            adv[0, x, l] = tiles[l]
        at = pl.multiple_of(step * GROUP, GROUP)
        for b, v in enumerate(swap_blocks(tiles)):
            msg[place[x * 8 + b], pl.ds(at, GROUP), :] = v
        return 0

    lax.fori_loop(0, COLS, second, 0)

    @pl.when(step == pl.num_programs(0) - 1)
    def _():
        for k, out in enumerate((m0, m1, m2, m3)):
            def put(i, _, k=k, out=out):
                pair = jnp.concatenate([msg[k * 32 + 2 * i], msg[k * 32 + 2 * i + 1]], axis=0)
                out[pl.ds(pl.multiple_of(i * 2 * species, 16), 2 * species), :] = pair.astype(bf16)
                return 0

            lax.fori_loop(0, 16, put, 0)


def transport(place, rows, courant, nbr, west, east):
    n = rows.shape[0] // (LEV * COLS)
    msg = jax.ShapeDtypeStruct((32 * n, CY), bf16)
    return pl.pallas_call(
        transport_kernel,
        grid=(n // GROUP,),
        in_specs=[
            smem(),
            pl.BlockSpec((GROUP * LEV * COLS, CY), lambda c: (c, 0)),
            whole(courant.shape),
            whole(nbr.shape),
            whole(west.shape),
            whole(east.shape),
        ],
        out_specs=[pl.BlockSpec((1, COLS, LEV, GROUP, CY), lambda c: (c, 0, 0, 0, 0))] + [whole((32 * n, CY))] * 4,
        out_shape=[jax.ShapeDtypeStruct((n // GROUP, COLS, LEV, GROUP, CY), f32)] + [msg] * 4,
        scratch_shapes=[
            pltpu.VMEM((2,) + west.shape, f32),
            pltpu.VMEM((COLS + 2, 5, GROUP, CY), f32),
            pltpu.VMEM((COLS + 2, 2, GROUP, CY), i32),
            pltpu.VMEM((COLS + 4, LEV, GROUP, CY), f32),
            pltpu.VMEM((COLS + 2, LEV, GROUP, CY), f32),
            pltpu.VMEM((128, n, CY), f32),
        ],
        compiler_params=pltpu.CompilerParams(vmem_limit_bytes=48 * MIB),
        cost_estimate=pl.CostEstimate(flops=40 * MIB, bytes_accessed=13 * MIB, transcendentals=0),
        name="transport",
    )(place, rows, courant, nbr, west, east)


def chem_kernel(slots, group, gain, w1, b1, w2, b2, w3, p0, p1, p2, p3, own, r0, r1, r2, r3, x, xn, h1, h2, y, bias, gains):
    species = 72
    total = 4 * species
    cells = slots * CY

    @pl.when(pl.program_id(0) == 0)
    def _():
        bias[0] = jnp.broadcast_to(b1[...], bias.shape[1:])
        bias[1] = jnp.broadcast_to(b2[...], bias.shape[1:])
        gains[...] = jnp.broadcast_to(gain[...], gains.shape)

    for k, piece in enumerate((p0, p1, p2, p3)):
        at = pl.multiple_of(group[k] * species, GROUP)
        for i in range(slots // 2):
            pair = piece[2 * i * species : 2 * (i + 1) * species, :].astype(f32)
            x[pl.ds(at, species), 2 * i * CY : (2 * i + 1) * CY] = pair[:species]
            x[pl.ds(at, species), (2 * i + 1) * CY : (2 * i + 2) * CY] = pair[species:]
    for i in range(slots):
        lanes = slice(i * CY, (i + 1) * CY)
        v = x[:, lanes]
        scale = lax.rsqrt(jnp.sum(v * v, axis=0, keepdims=True) * (1.0 / total) + 1e-6)
        xn[:, lanes] = (v * scale * gains[...]).astype(bf16)

    def layer(w, src, dst, b):
        hidden = w.shape[0]
        part = 256
        for m in range(0, hidden, part):
            u = jnp.dot(w[m : m + part, :], src[...], preferred_element_type=f32)
            for i in range(slots):
                lanes = slice(i * CY, (i + 1) * CY)
                v = u[:, lanes] + bias[b, m : m + part, :]
                dst[m : m + part, lanes] = (v + v * jnp.tanh(v)).astype(bf16)

    layer(w1, xn, h1, 0)
    layer(w2, h1, h2, 1)
    y[...] = jnp.dot(w3[...], h2[...], preferred_element_type=f32)
    for i in range(slots):
        own[i] = y[:, i * CY : (i + 1) * CY].astype(bf16)
    for k, piece in enumerate((r0, r1, r2, r3)):
        at = pl.multiple_of(group[k] * species, GROUP)
        for i in range(slots // 2):
            a = y[pl.ds(at, species), 2 * i * CY : (2 * i + 1) * CY]
            b = y[pl.ds(at, species), (2 * i + 1) * CY : (2 * i + 2) * CY]
            piece[2 * i * species : 2 * (i + 1) * species, :] = jnp.concatenate([a, b], axis=0).astype(bf16)


def chemistry(group, gain, w1, b1, w2, b2, w3, pieces, slots=4):
    rows = pieces[0].shape[0]
    species = 72
    total = 4 * species
    count = rows // species
    hidden = w1.shape[0]
    cells = slots * CY
    piece = pl.BlockSpec((slots * species, CY), lambda c: (c, 0))
    flops = 2 * count * CY * (hidden * hidden + 2 * hidden * total)
    return pl.pallas_call(
        functools.partial(chem_kernel, slots),
        grid=(count // slots,),
        in_specs=[smem(), whole(gain.shape), whole(w1.shape), whole(b1.shape), whole(w2.shape), whole(b2.shape), whole(w3.shape)]
        + [piece] * 4,
        out_specs=[pl.BlockSpec((slots, total, CY), lambda c: (c, 0, 0))] + [piece] * 4,
        out_shape=[jax.ShapeDtypeStruct((count, total, CY), bf16)] + [jax.ShapeDtypeStruct((rows, CY), bf16)] * 4,
        scratch_shapes=[
            pltpu.VMEM((total, cells), f32),
            pltpu.VMEM((total, cells), bf16),
            pltpu.VMEM((hidden, cells), bf16),
            pltpu.VMEM((hidden, cells), bf16),
            pltpu.VMEM((total, cells), f32),
            pltpu.VMEM((2, hidden, CY), f32),
            pltpu.VMEM((total, CY), f32),
        ],
        compiler_params=pltpu.CompilerParams(vmem_limit_bytes=48 * MIB),
        cost_estimate=pl.CostEstimate(flops=flops, bytes_accessed=11 * MIB, transcendentals=2 * hidden * count * CY),
        name="chemistry",
    )(group, gain, w1, b1, w2, b2, w3, *pieces)


def finish_kernel(place, adv, r0, r1, r2, r3, out, tend):
    step = pl.program_id(0)
    species = 72

    @pl.when(step == 0)
    def _():
        for k, piece in enumerate((r0, r1, r2, r3)):
            def take(i, _, k=k, piece=piece):
                pair = piece[pl.ds(pl.multiple_of(i * 2 * species, 16), 2 * species), :].astype(f32)
                tend[k * 32 + 2 * i] = pair[:species]
                tend[k * 32 + 2 * i + 1] = pair[species:]
                return 0

            lax.fori_loop(0, 16, take, 0)

    def column(x, _):
        at = pl.multiple_of(step * GROUP, GROUP)
        tiles = [tend[place[x * 8 + b], pl.ds(at, GROUP), :] for b in range(8)]
        for l, v in enumerate(swap_blocks(tiles)):
            out[pl.ds(l * COLS + x, GROUP, stride=LEV * COLS), :] = adv[0, x, l] + v
        return 0

    lax.fori_loop(0, COLS, column, 0)


def finish(place, adv, pieces):
    groups = adv.shape[0]
    n = groups * GROUP
    return pl.pallas_call(
        finish_kernel,
        grid=(groups,),
        in_specs=[smem(), pl.BlockSpec((1, COLS, LEV, GROUP, CY), lambda c: (c, 0, 0, 0, 0))]
        + [whole(pieces[0].shape)] * 4,
        out_specs=pl.BlockSpec((GROUP * LEV * COLS, CY), lambda c: (c, 0)),
        out_shape=jax.ShapeDtypeStruct((n * LEV * COLS, CY), f32),
        scratch_shapes=[pltpu.VMEM((128, n, CY), f32)],
        compiler_params=pltpu.CompilerParams(vmem_limit_bytes=48 * MIB),
        cost_estimate=pl.CostEstimate(flops=4 * MIB, bytes_accessed=13 * MIB, transcendentals=0),
        name="finish",
    )(place, adv, *pieces)


def sides():
    groups = []
    for core in range(2):
        for side in range(2):
            groups.append([(((t % 2) ^ side) * 2 + core) * 32 + t for t in range(32)])
    return groups


def shards(tracers, courant, neighbours, owner_map, gain, w_in, b_in, w_mid, b_mid, w_out):
    species = tracers.shape[0]
    me = lax.axis_index("spec")
    tile = lax.axis_index("tile")
    rows = tracers.reshape(-1, CY)

    west, east = pack_halo(rows, courant, neighbours)
    west = lax.ppermute(west, "tile", [(i, i + 1) for i in range(31)])
    east = lax.ppermute(east, "tile", [(i + 1, i) for i in range(31)])

    owner = owner_map[0]
    owner_spec, owner_tile = owner // 32, owner % 32
    worker = owner_spec ^ (((owner_tile ^ tile) & 1) * 2)
    place = (worker ^ me) * 32 + owner_tile
    group = jnp.arange(4, dtype=i32) ^ me

    adv, *pieces = transport(place, rows, courant, neighbours, west, east)

    def swap(parts):
        got = [lax.ppermute(parts[k], "spec", [(i, i ^ k) for i in range(4)]) for k in (2, 3, 1)]
        return [parts[0], got[2], got[0], got[1]]

    arrived = swap(pieces)
    w1 = (w_in * 0.5).T
    w2 = (w_mid * 0.5).T
    w3 = w_out.T
    own, *back = chemistry(
        group, gain[:, None], w1, 0.5 * b_in[:, None], w2, 0.5 * b_mid[:, None], w3, arrived
    )
    returned = swap(back)
    owned = lax.all_to_all(own, AXES, 0, 0, axis_index_groups=sides(), tiled=True)
    owned = owned.transpose(1, 0, 2).reshape(1, 4 * species, 32 * CY)
    out = finish(place, adv, returned)
    return out.reshape(tracers.shape), owned


def solution(mesh):
    return jax.shard_map(
        shards,
        mesh=mesh,
        in_specs=(
            P("spec", None, "tile", None),
            P(None, "tile", None),
            P(None, "tile", None),
            P("tile", None),
            P(),
            P(),
            P(),
            P(),
            P(),
            P(),
        ),
        out_specs=(P("spec", None, "tile", None), P(AXES, None, None)),
        check_vma=False,
    )
```

time: 477 us -> 212 us (0.44); the launches traced: 469 us -> 212 us
  other arithmetic: 237 us -> 2.53 us
  Pallas kernels: 0 us -> 113 us
  blocking collectives: 45.9 us -> 0 us
  local copies, waits for them, and re-layouts: 55 us -> 16.4 us
  matrix products: 36.6 us -> 0 us
  waiting for transfers between devices: 74.6 us -> 56.7 us
    pallas_call x0 -> x4, Pallas kernels: none -> 113 us  [the longest x1 61.1 us: transport(): pl.pallas_call(transport_kernel, grid=(n // GROUP,), in_specs=[smem(), pl...]
    concatenate x12 -> x0, other arithmetic: 111 us -> none  [padded_2(): jnp.concatenate([lax.ppermute(tail, axis, [(i, (i + 1) % count) for i in...]
    add x2 -> x1, other arithmetic: 63.6 us -> 0.02 us  [shards(): place = (worker ^ me) * 32 + owner_tile]
    convert_element_type x3 -> x0, other arithmetic: 56.6 us -> none  [the longest x1 53.5 us: shards(): chem_in = advected.astype(jnp.bfloat16)]
    all_to_all x1 -> x0, blocking collectives: 45.9 us -> none  [shards(): lax.all_to_all(by_owner.transpose(2, 0, 1, 3).reshape(devices, spec_dev,...]
    dot_general x2 -> x0, matrix products: 36.6 us -> none  [the longest x1 18.8 us: surrogate(): lax.dot_general(w_out, hidden_two, contract, preferred_element_type=jnp.f...]
    all_to_all x1, waiting for transfers between devices: 33.1 us -> 0.01 us  [shards(): lax.all_to_all(own, AXES, 0, 0, axis_index_groups=sides(), tiled=True)]
    gather x3 -> x0, local copies, waits for them, and re-layouts: 15.2 us -> none  [the longest x2 9.55 us: shards(): back_blocks = jnp.take(returned_piece, owners, axis=0)]
  transfers between devices with their start and end apart: 5 -> 9, of which waited for: 5 -> 5; matrix products, arithmetic and copies ran while one was open for 0% -> 4% of each run, Pallas kernels for 0% -> 13%
where the time goes in v1:
time: 212 us
  Pallas kernels  113 us (53%)
  waiting for transfers between devices  56.7 us (27%)
  starting transfers between devices  22.5 us (11%)
  local copies, waits for them, and re-layouts  16.4 us (8%)
  other arithmetic  2.53 us (1%)
    pallas_call x1, Pallas kernels, transport(): pl.pallas_call(transport_kernel, grid=(n // GROUP,), in_specs=[smem(), pl...  61.1 us
    ppermute x6, waiting for transfers between devices, swap(): lax.ppermute(parts[k], 'spec', [(i, i ^ k) for i in range(4)])  49.9 us
    pallas_call x1, Pallas kernels, finish(): pl.pallas_call(finish_kernel, grid=(groups,), in_specs=[smem(), pl.BlockS...  27.2 us
    pallas_call x1, Pallas kernels, chemistry(): pl.pallas_call(functools.partial(chem_kernel, slots), grid=(count // slot...  23.4 us
    unnamed x30, local copies, waits for them, and re-layouts  10.9 us
    all_to_all x1, starting transfers between devices, shards(): lax.all_to_all(own, AXES, 0, 0, axis_index_groups=sides(), tiled=True)  10.2 us
    ppermute x1, waiting for transfers between devices, shards(): east = lax.ppermute(east, 'tile', [(i + 1, i) for i in range(31)])  6.73 us
    ppermute x6, starting transfers between devices, swap(): lax.ppermute(parts[k], 'spec', [(i, i ^ k) for i in range(4)])  5.56 us
  transfers between devices with their start and end apart: 9, of which 5 were waited for; matrix products, arithmetic and copies ran while one was open for 4% of the time, Pallas kernels for 13%

profile of v1, /device:TPU:1, one launch (start us, length us, event | category | flops | bytes accessed | tf_op | source)
XLA Modules:
  0.0 211.5 jit_solution(18327625062490693703)
XLA Ops:
  0.6 2.3 %copy-done = f32[72,8,16,128]{3,2,1,0:T(8,128)S(1)} copy-done((f32[72,8,16,128]{3,2,1,0:T(8,128)S(1)}, f32[72,8,16,128]{3,2,1,0:T(8,128)}, u32[]{:S(2)}) %copy-start) | copy-done | bytes 4718616
  4.5 0.9 pack_halo.1
  5.3 5.5 %collective-permute-start = (bf16[1168,128]{1,0:T(8,128)(2,1)S(1)}, bf16[1168,128]{1,0:T(8,128)(2,1)S(1)}, u32[]{:S(2)}, u32[]{:S(2)}) collective-permute-start(bf16[1168,128]{1,0:T(8,128)(2,1)S(1)} %get-tuple-element.14), channel_id=1, source_target_pairs={{0,1},{1,2},{2,3},{3,4},{4,5},{5,6},{6,7},{7,8},{8,9},{9,10},{10,1... | collective-permute-start | bytes 897032 | tf_op jit(solution)/shard_map/ppermute | solution.py:330
  10.8 1.3 collective-permute-start.1
  12.8 1.4 copy.20
  14.2 3.9 %copy.22 = bf16[1024,1024]{0,1:T(8,128)(2,1)} copy(bf16[1024,1024]{1,0:T(8,128)(2,1)} %param.17) | data formatting | bytes 4194304 | tf_op args[7]
  18.2 6.7 %collective-permute-done.1.east = bf16[1168,128]{1,0:T(8,128)(2,1)S(1)} collective-permute-done((bf16[1168,128]{1,0:T(8,128)(2,1)S(1)}, bf16[1168,128]{1,0:T(8,128)(2,1)S(1)}, u32[]{:S(2)}, u32[]{:S(2)}) %collective-permute-start.1) | collective-permute-done | bytes 299040 | tf_op jit(solution)/shard_map/ppermute | solution.py:331
  25.0 61.1 %transport.1 = (f32[9,16,8,8,128]{4,3,2,1,0:T(8,128)}, bf16[2304,128]{1,0:T(8,128)(2,1)S(1)}, bf16[2304,128]{1,0:T(8,128)(2,1)S(1)}, bf16[2304,128]{1,0:T(8,128)(2,1)S(1)}, bf16[2304,128]{1,0:T(8,128)(2,1)S(1)}) custom-call(s32[128]{0:T(128)S(1)} %multiply_add_fusion.place, f32[9216,128]{1,0:T(8,128)} %bitcast.23, f32[4,16,128]{2,1,0:T(8,128)S(1)} %copy-done.2, ...), custom_call_target="tpu_custom_call" | custom-call | flops 41943040 | bytes 13631488 | tf_op jit(solution)/shard_map/transport/pallas_call | solution.py:169
  86.0 1.5 collective-permute-start.2
  87.6 1.2 collective-permute-start.3
  89.2 1.0 multiply_bitcast_fusion.1.w1
  90.2 1.5 multiply_bitcast_fusion.w2
  91.7 10.8 %collective-permute-done.3.p2 = bf16[2304,128]{1,0:T(8,128)(2,1)S(1)} collective-permute-done((bf16[2304,128]{1,0:T(8,128)(2,1)S(1)}, bf16[2304,128]{1,0:T(8,128)(2,1)S(1)}, u32[]{:S(2)}, u32[]{:S(2)}) %collective-permute-start.3) | collective-permute-done | bytes 589856 | tf_op jit(solution)/shard_map/ppermute | solution.py:342
  102.5 12.7 %collective-permute-done.4.p3 = bf16[2304,128]{1,0:T(8,128)(2,1)S(1)} collective-permute-done((bf16[2304,128]{1,0:T(8,128)(2,1)S(1)}, bf16[2304,128]{1,0:T(8,128)(2,1)S(1)}, u32[]{:S(2)}, u32[]{:S(2)}) %collective-permute-start.4) | collective-permute-done | bytes 589856 | tf_op jit(solution)/shard_map/ppermute | solution.py:342
  115.3 0.8 copy-done.13
  116.1 23.4 %chemistry.1 = (bf16[32,288,128]{2,1,0:T(8,128)(2,1)}, bf16[2304,128]{1,0:T(8,128)(2,1)S(1)}, bf16[2304,128]{1,0:T(8,128)(2,1)S(1)}, bf16[2304,128]{1,0:T(8,128)(2,1)S(1)}, bf16[2304,128]{1,0:T(8,128)(2,1)S(1)}) custom-call(s32[4]{0:T(128)S(1)} %iota_xor_fusion.group, f32[288,1]{1,0:T(8,128)S(1)} %broadcast_in_dim.6.gain, ...), custom_call_target="tpu_custom_call" | custom-call | flops 13421772800 | bytes 11534336 | tf_op jit(solution)/shard_map/chemistry/pallas_call | solution.py:251
  139.5 0.8 copy-done.6
  140.3 10.2 %all-to-all-start = ((bf16[32,288,128]{2,1,0:T(8,128)(2,1)}), bf16[32,288,128]{2,1,0:T(8,128)(2,1)}, u32[]{:S(2)}, u32[]{:S(2)}) async-start(bf16[32,288,128]{2,1,0:T(8,128)(2,1)} %get-tuple-element.25), calls=%async_computation | async-start | bytes 4718592 | tf_op jit(solution)/shard_map/all_to_all | solution.py:353
  151.2 1.7 collective-permute-start.7
  152.9 13.3 %collective-permute-done.6.r2 = bf16[2304,128]{1,0:T(8,128)(2,1)S(1)} collective-permute-done((bf16[2304,128]{1,0:T(8,128)(2,1)S(1)}, bf16[2304,128]{1,0:T(8,128)(2,1)S(1)}, u32[]{:S(2)}, u32[]{:S(2)}) %collective-permute-start.6) | collective-permute-done | bytes 589856 | tf_op jit(solution)/shard_map/ppermute | solution.py:342
  166.2 13.1 %collective-permute-done.7.r3 = bf16[2304,128]{1,0:T(8,128)(2,1)S(1)} collective-permute-done((bf16[2304,128]{1,0:T(8,128)(2,1)S(1)}, bf16[2304,128]{1,0:T(8,128)(2,1)S(1)}, u32[]{:S(2)}, u32[]{:S(2)}) %collective-permute-start.7) | collective-permute-done | bytes 589856 | tf_op jit(solution)/shard_map/ppermute | solution.py:342
  179.3 27.2 %finish.1 = f32[9216,128]{1,0:T(8,128)} custom-call(s32[128]{0:T(128)S(1)} %multiply_add_fusion.place, f32[9,16,8,8,128]{4,3,2,1,0:T(8,128)} %get-tuple-element.16.adv, bf16[2304,128]{1,0:T(8,128)(2,1)S(1)} %get-tuple-element.21.r0, bf16[2304,128]{1,0:T(8,128)(2,1)S(1)} %collective-permute-done.5.r1, bf16[2304,128]{1,0:T(8,128)(2,1)S(1)} %collective-permute-done.6.r2, ...), custom_call_target="tpu_custom_call" | custom-call | flops 4194304 | bytes 13631488 | tf_op jit(solution)/shard_map/finish/pallas_call | solution.py:301
  206.5 2.6 %copy.26 = bf16[288,32,128]{2,1,0:T(8,128)(2,1)S(1)} copy(bf16[288,32,128]{2,0,1:T(8,128)(2,1)} %bitcast.8) | data formatting | bytes 4718592 | tf_op jit(solution)/shard_map/transpose | solution.py:354
  209.1 2.4 %reshape.17 = bf16[1,288,4096]{2,1,0:T(8,128)(2,1)} reshape(bf16[288,32,128]{2,1,0:T(8,128)(2,1)S(1)} %copy.26) | data formatting | bytes 4718592 | tf_op jit(solution)/shard_map/reshape | solution.py:354
  (39 shorter events, 3.2 us)
Async XLA Ops:
  0.6 2.3 %copy-start = (f32[72,8,16,128]{3,2,1,0:T(8,128)S(1)}, f32[72,8,16,128]{3,2,1,0:T(8,128)}, u32[]{:S(2)}) copy-start(f32[72,8,16,128]{3,2,1,0:T(8,128)} %param.10) | copy-start | bytes 14155780
  3.0 0.8 copy-start.1
  3.7 0.7 copy-start.3
  4.4 7.7 %copy-start.9 = (f32[1024]{0:T(1024)S(1)}, f32[1024]{0:T(1024)}, u32[]{:S(2)}) copy-start(f32[1024]{0:T(1024)} %param.16) | copy-start | bytes 12292
  4.4 7.7 %copy-start.10 = (f32[1024]{0:T(1024)S(1)}, f32[1024]{0:T(1024)}, u32[]{:S(2)}) copy-start(f32[1024]{0:T(1024)} %param.18) | copy-start | bytes 12292
  4.5 7.7 %copy-start.11 = (f32[288]{0:T(512)S(1)}, f32[288]{0:T(512)}, u32[]{:S(2)}) copy-start(f32[288]{0:T(512)} %param.14) | copy-start | bytes 3460
  5.3 12.9 %collective-permute-start = (bf16[1168,128]{1,0:T(8,128)(2,1)S(1)}, bf16[1168,128]{1,0:T(8,128)(2,1)S(1)}, u32[]{:S(2)}, u32[]{:S(2)}) collective-permute-start(bf16[1168,128]{1,0:T(8,128)(2,1)S(1)} %get-tuple-element.14), channel_id=1, source_target_pairs={{0,1},{1,2},{2,3},{3,4},{4,5},{5,6},{6,7},{7,8},{8,9},{9,10},{10,1... | collective-permute-start | bytes 897032 | tf_op jit(solution)/shard_map/ppermute | solution.py:330
  10.8 14.1 %collective-permute-start.1 = (bf16[1168,128]{1,0:T(8,128)(2,1)S(1)}, bf16[1168,128]{1,0:T(8,128)(2,1)S(1)}, u32[]{:S(2)}, u32[]{:S(2)}) collective-permute-start(bf16[1168,128]{1,0:T(8,128)(2,1)S(1)} %get-tuple-element.15), channel_id=1, source_target_pairs={{1,0},{2,1},{3,2},{4,3},{5,4},{6,5},{7,6},{8,7},{9,8},{10,9},{11,1... | collective-permute-start | bytes 897032 | tf_op jit(solution)/shard_map/ppermute | solution.py:331
  14.2 4.0 %copy-start.12 = (s32[1,128]{1,0:T(1,128)S(1)}, s32[1,128]{1,0:T(1,128)}, u32[]{:S(2)}) copy-start(s32[1,128]{1,0:T(1,128)} %param.13) | copy-start | bytes 1540
  14.2 10.7 %copy-start.2 = (f32[4,16,128]{2,1,0:T(8,128)S(1)}, f32[4,16,128]{2,1,0:T(8,128)}, u32[]{:S(2)}) copy-start(f32[4,16,128]{2,1,0:T(8,128)} %courant.3) | copy-start | bytes 98308
  14.2 10.7 %copy-start.4 = (s32[2,16,128]{2,1,0:T(8,128)S(1)}, s32[2,16,128]{2,1,0:T(8,128)}, u32[]{:S(2)}) copy-start(s32[2,16,128]{2,1,0:T(8,128)} %nbr.3) | copy-start | bytes 49156
  18.2 72.0 %copy-start.8 = (bf16[1024,1024]{0,1:T(8,128)(2,1)S(1)}, bf16[1024,1024]{0,1:T(8,128)(2,1)}, u32[]{:S(2)}) copy-start(bf16[1024,1024]{0,1:T(8,128)(2,1)} %copy.22) | copy-start | bytes 6291460
  86.0 5.7 %collective-permute-start.2 = (bf16[2304,128]{1,0:T(8,128)(2,1)S(1)}, bf16[2304,128]{1,0:T(8,128)(2,1)S(1)}, u32[]{:S(2)}, u32[]{:S(2)}) collective-permute-start(bf16[2304,128]{1,0:T(8,128)(2,1)S(1)} %get-tuple-element.18), channel_id=1, source_target_pairs={{0,32},{32,0},{64,96},{96,64},{1,33},{33,1},{65,97},{97,65},{2,34}... | collective-permute-start | bytes 1769480 | tf_op jit(solution)/shard_map/ppermute | solution.py:342
  87.6 15.0 %collective-permute-start.3 = (bf16[2304,128]{1,0:T(8,128)(2,1)S(1)}, bf16[2304,128]{1,0:T(8,128)(2,1)S(1)}, u32[]{:S(2)}, u32[]{:S(2)}) collective-permute-start(bf16[2304,128]{1,0:T(8,128)(2,1)S(1)} %get-tuple-element.19), channel_id=1, source_target_pairs={{0,64},{32,96},{64,0},{96,32},{1,65},{33,97},{65,1},{97,33},{2,66}... | collective-permute-start | bytes 1769480 | tf_op jit(solution)/shard_map/ppermute | solution.py:342
  88.8 26.5 %collective-permute-start.4 = (bf16[2304,128]{1,0:T(8,128)(2,1)S(1)}, bf16[2304,128]{1,0:T(8,128)(2,1)S(1)}, u32[]{:S(2)}, u32[]{:S(2)}) collective-permute-start(bf16[2304,128]{1,0:T(8,128)(2,1)S(1)} %get-tuple-element.20), channel_id=1, source_target_pairs={{0,96},{32,64},{64,32},{96,0},{1,97},{33,65},{65,33},{97,1},{2,98}... | collective-permute-start | bytes 1769480 | tf_op jit(solution)/shard_map/ppermute | solution.py:342
  90.2 25.9 %copy-start.5 = (bf16[1024,288]{0,1:T(8,128)(2,1)S(1)}, bf16[1024,288]{0,1:T(8,128)(2,1)}, u32[]{:S(2)}) copy-start(bf16[1024,288]{0,1:T(8,128)(2,1)} %param.19) | copy-start | bytes 1769476
  115.3 0.8 copy-start.13
  139.5 0.8 copy-start.6
  140.3 10.2 %copy-start.7 = (bf16[2304,128]{1,0:T(8,128)(2,1)S(1)}, bf16[2304,128]{1,0:T(8,128)(2,1)}, u32[]{:S(2)}) copy-start(bf16[2304,128]{1,0:T(8,128)(2,1)} %copy-done.6) | copy-start | bytes 1769476
  140.3 66.2 %all-to-all-start = ((bf16[32,288,128]{2,1,0:T(8,128)(2,1)}), bf16[32,288,128]{2,1,0:T(8,128)(2,1)}, u32[]{:S(2)}, u32[]{:S(2)}) async-start(bf16[32,288,128]{2,1,0:T(8,128)(2,1)} %get-tuple-element.25), calls=%async_computation | async-start | bytes 4718592 | tf_op jit(solution)/shard_map/all_to_all | solution.py:353
  150.5 2.4 %collective-permute-start.5 = (bf16[2304,128]{1,0:T(8,128)(2,1)S(1)}, bf16[2304,128]{1,0:T(8,128)(2,1)S(1)}, u32[]{:S(2)}, u32[]{:S(2)}) collective-permute-start(bf16[2304,128]{1,0:T(8,128)(2,1)S(1)} %copy-done.7), channel_id=1, source_target_pairs={{0,32},{32,0},{64,96},{96,64},{1,33},{33,1},{65,97},{97,65},{2,34}... | collective-permute-start | bytes 1769480 | tf_op jit(solution)/shard_map/ppermute | solution.py:342
  151.2 15.0 %collective-permute-start.6 = (bf16[2304,128]{1,0:T(8,128)(2,1)S(1)}, bf16[2304,128]{1,0:T(8,128)(2,1)S(1)}, u32[]{:S(2)}, u32[]{:S(2)}) collective-permute-start(bf16[2304,128]{1,0:T(8,128)(2,1)S(1)} %get-tuple-element.23), channel_id=1, source_target_pairs={{0,64},{32,96},{64,0},{96,32},{1,65},{33,97},{65,1},{97,33},{2,66}... | collective-permute-start | bytes 1769480 | tf_op jit(solution)/shard_map/ppermute | solution.py:342
  151.2 28.1 %collective-permute-start.7 = (bf16[2304,128]{1,0:T(8,128)(2,1)S(1)}, bf16[2304,128]{1,0:T(8,128)(2,1)S(1)}, u32[]{:S(2)}, u32[]{:S(2)}) collective-permute-start(bf16[2304,128]{1,0:T(8,128)(2,1)S(1)} %get-tuple-element.24), channel_id=1, source_target_pairs={{0,96},{32,64},{64,32},{96,0},{1,97},{33,65},{65,33},{97,1},{2,98}... | collective-permute-start | bytes 1769480 | tf_op jit(solution)/shard_map/ppermute | solution.py:342

commit v2 on v1

v2 whole, which is shorter than its diff:
```python
import functools

import jax
import jax.numpy as jnp
from jax import lax
from jax.experimental import pallas as pl
from jax.experimental.pallas import tpu as pltpu
from jax.sharding import PartitionSpec as P

LEV = 8
COLS = 16
CY = 128
BLOCK = 16
GROUP = 8
EXTRA = 16
CHUNKS = (12, 12, 8)
HOME = ((0,), (1, 2))
MIB = 1024 * 1024
AXES = ("spec", "tile")
f32, bf16, i32 = jnp.float32, jnp.bfloat16, jnp.int32


def whole(shape):
    return pl.BlockSpec(shape, lambda *_: (0,) * len(shape))


def smem():
    return pl.BlockSpec(memory_space=pltpu.SMEM)


def anywhere():
    return pl.BlockSpec(memory_space=pl.ANY)


def resident():
    return pl.BlockSpec(memory_space=pltpu.VMEM)


def hbm(a):
    return pltpu.with_memory_space_constraint(a, pltpu.HBM)


def fetch_rows(rows, buf, sems, groups):
    per = GROUP * LEV * COLS
    copies = [
        pltpu.make_async_copy(rows.at[pl.ds(c * per, per), :], buf.at[pl.ds(c * per, per), :], sems.at[c])
        for c in range(groups)
    ]
    for copy in copies:
        copy.start()
    return copies


def pack_kernel(rows, courant, nbr, west, east, buf, cour, near, edge, extra, sems):
    species = 72
    groups = species // GROUP
    copies = fetch_rows(rows, buf, sems, groups)
    small = [
        pltpu.make_async_copy(courant, cour, sems.at[groups]),
        pltpu.make_async_copy(nbr, near, sems.at[groups + 1]),
    ]
    for copy in small:
        copy.start()
    for c in range(groups):
        copies[c].wait()
        for side, cols in ((0, (14, 15)), (1, (0, 1))):
            for j, x in enumerate(cols):
                for l in range(LEV):
                    at = (j * LEV + l) * species + c * GROUP
                    start = c * GROUP * LEV * COLS + l * COLS + x
                    edge[side, at : at + GROUP, :] = buf[pl.ds(start, GROUP, stride=LEV * COLS), :]
    for copy in small:
        copy.wait()
    n = 2 * LEV * species
    for side, x, out in ((0, 15, west), (1, 0, east)):
        extra[...] = jnp.zeros_like(extra)
        for i in range(4):
            v = cour[i, x : x + 1, :]
            high = v.astype(bf16).astype(f32)
            extra[i : i + 1, :] = high
            extra[4 + i : 5 + i, :] = v - high
        for i in range(2):
            extra[8 + i : 9 + i, :] = near[i, x : x + 1, :].astype(f32)
        out[0:n, :] = edge[side].astype(bf16)
        out[n : n + EXTRA, :] = extra[...].astype(bf16)


def pack_halo(rows, courant, nbr):
    n = rows.shape[0] // (LEV * COLS)
    total = 2 * LEV * n + EXTRA
    return pl.pallas_call(
        pack_kernel,
        grid=(1,),
        in_specs=[anywhere()] * 3,
        out_specs=[whole((total, CY))] * 2,
        out_shape=[pltpu.HBM((total, CY), bf16)] * 2,
        scratch_shapes=[
            pltpu.VMEM(rows.shape, f32),
            pltpu.VMEM(courant.shape, f32),
            pltpu.VMEM(nbr.shape, i32),
            pltpu.VMEM((2, 2 * LEV * n, CY), f32),
            pltpu.VMEM((EXTRA, CY), f32),
            pltpu.SemaphoreType.DMA((n // GROUP + 2,)),
        ],
        compiler_params=pltpu.CompilerParams(vmem_limit_bytes=32 * MIB),
        cost_estimate=pl.CostEstimate(flops=0, bytes_accessed=6 * MIB, transcendentals=0),
        name="pack_halo",
    )(hbm(rows), hbm(courant), hbm(nbr))


def lane_block():
    return lax.broadcasted_iota(i32, (GROUP, CY), 1) // BLOCK


def swap_blocks(tiles):
    place = lane_block()
    n = len(tiles)
    cur = [t if a == 0 else pltpu.roll(t, a * BLOCK, 1) for a, t in enumerate(tiles)]
    for bit in (1, 2, 4):
        mask = (place & bit) != 0
        cur = [jnp.where(mask, cur[(i + bit) % n], cur[i]) for i in range(n)]
    out = []
    for k in range(n):
        v = cur[(-k) % n]
        out.append(v if k == 0 else pltpu.roll(v, CY - k * BLOCK, 1))
    return out


def weights(c, ind):
    source = lax.broadcasted_iota(i32, (CY, CY), 0)
    target = lax.broadcasted_iota(i32, (CY, CY), 1)
    zero = jnp.zeros((CY, CY), f32)
    north = source == (target + 1) % CY
    south = source == (target + CY - 1) % CY
    before, after = source == ind[0], source == ind[1]
    high = [v.astype(bf16).astype(f32) for v in c]
    low = [v - h for v, h in zip(c, high)]
    stacks = []
    for pick in (
        lambda p: jnp.where(before, p[0], zero),
        lambda p: jnp.where(north, p[2], zero) + jnp.where(south, p[3], zero),
        lambda p: jnp.where(after, p[1], zero),
    ):
        h, l = pick(high).astype(bf16), pick(low).astype(bf16)
        stacks.append(jnp.concatenate([jnp.concatenate([h, l], axis=1), jnp.concatenate([h, zero.astype(bf16)], axis=1)], axis=0))
    return stacks


def split(v):
    high = v.astype(bf16)
    return jnp.concatenate([high, (v - high.astype(f32)).astype(bf16)], axis=1)


def move(cells, centre, stacks, c):
    lhs = jnp.concatenate(cells, axis=1)
    rhs = jnp.concatenate([m[: v.shape[1]] for m, v in zip(stacks, cells)], axis=0)
    both = jnp.dot(lhs, rhs, preferred_element_type=f32)
    own = 1.0 - (c[0] + c[1] + c[2] + c[3])
    return centre * own + (both[:, :CY] + both[:, CY:])


def column_weights(courant, nbr, x):
    return [courant[i, x : x + 1, :] for i in range(4)], [nbr[i, x : x + 1, :] for i in range(2)]


def put_blocks(place, msg, x, field, species):
    for c in range(species // GROUP):
        tiles = [field[l * species + c * GROUP : l * species + (c + 1) * GROUP, :] for l in range(LEV)]
        for b, v in enumerate(swap_blocks(tiles)):
            msg[place[x * 8 + b], c * GROUP : (c + 1) * GROUP, :] = v


def interior_kernel(place, rows, courant, nbr, adv, edge, filled, buf, cour, near, field, parts, mid, midparts, moved, msg, sems, out_sems, row_sems):
    species = 72
    per = LEV * COLS
    groups = species // GROUP
    copies = fetch_rows(rows, buf, sems, groups)
    small = [
        pltpu.make_async_copy(courant, cour, sems.at[groups]),
        pltpu.make_async_copy(nbr, near, sems.at[groups + 1]),
    ]
    for copy in small:
        copy.start()
    for c in range(groups):
        copies[c].wait()
        for l in range(LEV):
            for x in range(COLS):
                at = l * species + c * GROUP
                field[x, at : at + GROUP, :] = buf[pl.ds(c * GROUP * per + l * COLS + x, GROUP, stride=per), :]
    for copy in small:
        copy.wait()
    for x in range(COLS):
        parts[x] = split(field[x])
    for i, x in enumerate((0, 1, 14, 15)):
        edge[i] = field[x]
    matrices = {}
    leaving = []
    for x in range(1, COLS - 1):
        c, ind = column_weights(cour, near, x)
        matrices[x] = weights(c, ind)
        v = move([parts[x - 1], parts[x], parts[x + 1]], field[x], matrices[x], c)
        mid[x] = v
        midparts[x] = split(v)
        if x in (1, 2, 13, 14):
            edge[{1: 4, 2: 5, 13: 6, 14: 7}[x]] = v
        if x >= 3:
            y = x - 1
            c, _ = column_weights(cour, near, y)
            moved[y - 2] = move([midparts[y - 1], midparts[y], midparts[y + 1]], mid[y], matrices.pop(y), c)
            leaving.append(pltpu.make_async_copy(moved.at[y - 2], adv.at[y - 2], out_sems.at[y - 2]))
            leaving[-1].start()
            put_blocks(place, msg, y, moved.at[y - 2], species)
            for b in range(8):
                at = place[y * 8 + b]
                leaving.append(pltpu.make_async_copy(msg.at[at], filled.at[at], row_sems.at[(y - 2) * 8 + b]))
                leaving[-1].start()
    for copy in leaving:
        copy.wait()


def interior(place, rows, courant, nbr):
    n = rows.shape[0] // (LEV * COLS)
    size = (LEV * n, CY)
    wide = (LEV * n, 2 * CY)
    return pl.pallas_call(
        interior_kernel,
        in_specs=[smem()] + [anywhere()] * 3,
        out_specs=[anywhere(), whole((8,) + size), anywhere()],
        out_shape=[
            pltpu.HBM((12,) + size, f32),
            jax.ShapeDtypeStruct((8,) + size, f32),
            pltpu.HBM((128, n, CY), f32),
        ],
        scratch_shapes=[
            pltpu.VMEM(rows.shape, f32),
            pltpu.VMEM(courant.shape, f32),
            pltpu.VMEM(nbr.shape, i32),
            pltpu.VMEM((COLS,) + size, f32),
            pltpu.VMEM((COLS,) + wide, bf16),
            pltpu.VMEM((COLS,) + size, f32),
            pltpu.VMEM((COLS,) + wide, bf16),
            pltpu.VMEM((12,) + size, f32),
            pltpu.VMEM((128, n, CY), f32),
            pltpu.SemaphoreType.DMA((n // GROUP + 2,)),
            pltpu.SemaphoreType.DMA((12,)),
            pltpu.SemaphoreType.DMA((96,)),
        ],
        compiler_params=pltpu.CompilerParams(vmem_limit_bytes=48 * MIB),
        cost_estimate=pl.CostEstimate(flops=9 * 10**9, bytes_accessed=16 * MIB, transcendentals=0),
        name="interior",
    )(place, hbm(rows), hbm(courant), hbm(nbr))


def border_kernel(chunks, place, courant, nbr, west_in, east_in, edge, filled, adv, *rest):
    outs, (msg, cour, near_ind, west, east, moved, buf, sems, adv_sems, out_sems) = rest[:-10], rest[-10:]
    species = 72
    n = 2 * LEV * species
    size = LEV * species
    copies = [
        pltpu.make_async_copy(src, dst, sems.at[i])
        for i, (src, dst) in enumerate(
            ((courant, cour), (nbr, near_ind), (west_in, west), (east_in, east), (filled, msg))
        )
    ]
    for copy in copies:
        copy.start()
    for copy in copies[:4]:
        copy.wait()

    def halo_weights(halo):
        e = halo[n : n + EXTRA, :].astype(f32)
        c = [e[i : i + 1, :] + e[4 + i : 5 + i, :] for i in range(4)]
        ind = [e[8 + i : 9 + i, :].astype(i32) for i in range(2)]
        return c, ind

    leaving = []

    def place_column(i, v):
        moved[i] = v
        leaving.append(pltpu.make_async_copy(moved.at[i], adv.at[i], adv_sems.at[i]))
        leaving[-1].start()

    def parts(i):
        return split(edge[i])

    far, near = west[0:size, :], west[size:n, :]
    c, ind = halo_weights(west)
    a = split(move([far, near, parts(0)], near.astype(f32), weights(c, ind), c))
    c0, ind0 = column_weights(cour, near_ind, 0)
    m0 = weights(c0, ind0)
    b = move([near, parts(0), parts(1)], edge[0], m0, c0)
    place_column(0, move([a, split(b), parts(4)], b, m0, c0))
    c1, ind1 = column_weights(cour, near_ind, 1)
    place_column(1, move([split(b), parts(4), parts(5)], edge[4], weights(c1, ind1), c1))
    near, far = east[0:size, :], east[size:n, :]
    c, ind = halo_weights(east)
    a = split(move([parts(3), near, far], near.astype(f32), weights(c, ind), c))
    c0, ind0 = column_weights(cour, near_ind, 15)
    m0 = weights(c0, ind0)
    b = move([parts(2), parts(3), near], edge[3], m0, c0)
    place_column(3, move([parts(7), split(b), a], b, m0, c0))
    c1, ind1 = column_weights(cour, near_ind, 14)
    place_column(2, move([parts(6), parts(7), split(b)], edge[7], weights(c1, ind1), c1))

    copies[4].wait()
    for i, x in enumerate((0, 1, 14, 15)):
        put_blocks(place, msg, x, moved.at[i], species)
    first = 0
    for j, count in enumerate(chunks):
        for k in (2, 3, 1, 0):
            for i in range(first, first + count, 2):
                pair = jnp.concatenate([msg[k * 32 + i], msg[k * 32 + i + 1]], axis=0)
                buf[k, i * species : (i + 2) * species, :] = pair.astype(bf16)
            part = buf.at[k, pl.ds(first * species, count * species), :]
            leaving.append(pltpu.make_async_copy(part, outs[j * 4 + k], out_sems.at[j * 4 + k]))
            leaving[-1].start()
        first += count
    for copy in leaving:
        copy.wait()


def border(chunks, place, courant, nbr, west, east, edge, filled):
    n = filled.shape[1]
    size = (LEV * n, CY)
    pieces = [pltpu.HBM((count * n, CY), bf16) for count in chunks for _ in range(4)]
    return pl.pallas_call(
        functools.partial(border_kernel, chunks),
        in_specs=[smem()] + [anywhere()] * 4 + [whole(edge.shape), anywhere()],
        out_specs=[anywhere()] * (1 + len(pieces)),
        out_shape=[pltpu.HBM((4,) + size, f32)] + pieces,
        scratch_shapes=[
            pltpu.VMEM(filled.shape, f32),
            pltpu.VMEM(courant.shape, f32),
            pltpu.VMEM(nbr.shape, i32),
            pltpu.VMEM(west.shape, bf16),
            pltpu.VMEM(east.shape, bf16),
            pltpu.VMEM((4,) + size, f32),
            pltpu.VMEM((4, 32 * n, CY), bf16),
            pltpu.SemaphoreType.DMA((5,)),
            pltpu.SemaphoreType.DMA((4,)),
            pltpu.SemaphoreType.DMA((len(pieces),)),
        ],
        compiler_params=pltpu.CompilerParams(vmem_limit_bytes=40 * MIB),
        cost_estimate=pl.CostEstimate(flops=3 * 10**9, bytes_accessed=11 * MIB, transcendentals=0),
        name="border",
    )(place, hbm(courant), hbm(nbr), hbm(west), hbm(east), edge, hbm(filled))


def turn_kernel(gain, w_in, b_in, w_mid, b_mid, w_out, w1, w2, w3, b1, b2, g):
    half = jnp.asarray(0.5, bf16)
    w1[...] = (w_in[...] * half).T
    w2[...] = (w_mid[...] * half).T
    w3[...] = w_out[...].T
    b1[...] = jnp.broadcast_to(0.5 * b_in[...], (CY, b_in.shape[1])).T
    b2[...] = jnp.broadcast_to(0.5 * b_mid[...], (CY, b_mid.shape[1])).T
    g[...] = jnp.broadcast_to(gain[...], (CY, gain.shape[1])).T


def turn_weights(gain, w_in, b_in, w_mid, b_mid, w_out):
    species, hidden = w_in.shape
    args = (gain[None], w_in, b_in[None], w_mid, b_mid[None], w_out)
    return pl.pallas_call(
        turn_kernel,
        out_shape=[
            jax.ShapeDtypeStruct((hidden, species), bf16),
            jax.ShapeDtypeStruct((hidden, hidden), bf16),
            jax.ShapeDtypeStruct((species, hidden), bf16),
            jax.ShapeDtypeStruct((hidden, CY), f32),
            jax.ShapeDtypeStruct((hidden, CY), f32),
            jax.ShapeDtypeStruct((species, CY), f32),
        ],
        compiler_params=pltpu.CompilerParams(vmem_limit_bytes=32 * MIB),
        cost_estimate=pl.CostEstimate(flops=0, bytes_accessed=8 * MIB, transcendentals=0),
        name="turn_weights",
    )(*args)


def chem_kernel(slots, group, gain, w1, b1, w2, b2, w3, p0, p1, p2, p3, *rest):
    own, r0, r1, r2, r3, x, xn, h1, h2, y = rest[-10:]
    species = 72
    total = 4 * species

    for k, piece in enumerate((p0, p1, p2, p3)):
        at = pl.multiple_of(group[k] * species, GROUP)
        for i in range(slots // 2):
            pair = piece[2 * i * species : 2 * (i + 1) * species, :].astype(f32)
            x[pl.ds(at, species), 2 * i * CY : (2 * i + 1) * CY] = pair[:species]
            x[pl.ds(at, species), (2 * i + 1) * CY : (2 * i + 2) * CY] = pair[species:]
    for i in range(slots):
        lanes = slice(i * CY, (i + 1) * CY)
        v = x[:, lanes]
        scale = lax.rsqrt(jnp.sum(v * v, axis=0, keepdims=True) * (1.0 / total) + 1e-6)
        xn[:, lanes] = (v * scale * gain[...]).astype(bf16)

    def layer(w, src, dst, bias):
        hidden = w.shape[0]
        part = 256
        for m in range(0, hidden, part):
            u = jnp.dot(w[m : m + part, :], src[...], preferred_element_type=f32)
            for i in range(slots):
                lanes = slice(i * CY, (i + 1) * CY)
                v = u[:, lanes] + bias[m : m + part, :]
                dst[m : m + part, lanes] = (v + v * jnp.tanh(v)).astype(bf16)

    layer(w1, xn, h1, b1)
    layer(w2, h1, h2, b2)
    y[...] = jnp.dot(w3[...], h2[...], preferred_element_type=f32)
    for i in range(slots):
        own[i] = y[:, i * CY : (i + 1) * CY].astype(bf16)
    for k, piece in enumerate((r0, r1, r2, r3)):
        at = pl.multiple_of(group[k] * species, GROUP)
        for i in range(slots // 2):
            a = y[pl.ds(at, species), 2 * i * CY : (2 * i + 1) * CY]
            b = y[pl.ds(at, species), (2 * i + 1) * CY : (2 * i + 2) * CY]
            piece[2 * i * species : 2 * (i + 1) * species, :] = jnp.concatenate([a, b], axis=0).astype(bf16)


def chemistry(first, home, group, prepared, pieces, own, back, slots=4):
    w1, w2, w3, b1, b2, gain = prepared
    species = 72
    total = 4 * species
    count = pieces[0].shape[0] // species
    hidden = w1.shape[0]
    cells = slots * CY
    start, home_count = home
    piece_in = pl.BlockSpec((slots * species, CY), lambda c: (c, 0))
    piece_out = pl.BlockSpec((slots * species, CY), lambda c: ((first - start) // slots + c, 0))
    flops = 2 * count * CY * (hidden * hidden + 2 * hidden * total)
    fixed = [gain, w1, b1, w2, b2, w3]
    aliases = {}
    if own is not None:
        aliases[11] = 0
    for i in range(len(back)):
        aliases[11 + len(aliases)] = 1 + i
    handed = ([] if own is None else [own]) + list(back)
    own, *back = pl.pallas_call(
        functools.partial(chem_kernel, slots),
        grid=(count // slots,),
        in_specs=[smem()] + [resident()] * len(fixed) + [piece_in] * 4 + [anywhere()] * len(handed),
        out_specs=[pl.BlockSpec((slots, total, CY), lambda c: (first // slots + c, 0, 0))] + [piece_out] * 4,
        out_shape=[pltpu.HBM((32, total, CY), bf16)] + [pltpu.HBM((home_count * species, CY), bf16)] * 4,
        input_output_aliases=aliases,
        scratch_shapes=[
            pltpu.VMEM((total, cells), f32),
            pltpu.VMEM((total, cells), bf16),
            pltpu.VMEM((hidden, cells), bf16),
            pltpu.VMEM((hidden, cells), bf16),
            pltpu.VMEM((total, cells), f32),
        ],
        compiler_params=pltpu.CompilerParams(vmem_limit_bytes=36 * MIB),
        cost_estimate=pl.CostEstimate(flops=flops, bytes_accessed=8 * MIB, transcendentals=2 * hidden * count * CY),
        name="chemistry",
    )(group, *fixed, *[hbm(p) for p in pieces], *[hbm(a) for a in handed])
    return own, back


def finish_kernel(wide, place, middle, border, *rest):
    pieces, (out, tend) = rest[:-2], rest[-2:]
    step = pl.program_id(0)
    species = 72

    @pl.when(step == 0)
    def _():
        first = 0
        for j in range(0, len(pieces), 4):
            count = pieces[j].shape[0] // species
            for k in range(4):
                for i in range(0, count, 2):
                    pair = pieces[j + k][i * species : (i + 2) * species, :].astype(f32)
                    tend[k * 32 + first + i] = pair[:species]
                    tend[k * 32 + first + i + 1] = pair[species:]
            first += count

    for x in range(COLS):
        src, y = (middle, x - 2) if 2 <= x < 14 else (border, x if x < 2 else x - 12)
        for c in range(wide // GROUP):
            at = pl.multiple_of(step * wide + c * GROUP, GROUP)
            tiles = [tend[place[x * 8 + b], pl.ds(at, GROUP), :] for b in range(8)]
            for l, v in enumerate(swap_blocks(tiles)):
                v = v + src[y, l, c * GROUP : (c + 1) * GROUP, :]
                out[pl.ds(c * GROUP * LEV * COLS + l * COLS + x, GROUP, stride=LEV * COLS), :] = v


def finish(place, middle, border, pieces, wide=8):
    n = middle.shape[1] // LEV
    middle, border = (a.reshape(a.shape[0], LEV, n, CY) for a in (middle, border))

    def columns(a):
        return pl.BlockSpec((a.shape[0], LEV, wide, CY), lambda c: (0, 0, c, 0))

    return pl.pallas_call(
        functools.partial(finish_kernel, wide),
        grid=(n // wide,),
        in_specs=[smem(), columns(middle), columns(border)] + [whole(p.shape) for p in pieces],
        out_specs=pl.BlockSpec((wide * LEV * COLS, CY), lambda c: (c, 0)),
        out_shape=pltpu.HBM((n * LEV * COLS, CY), f32),
        scratch_shapes=[pltpu.VMEM((128, n, CY), f32)],
        compiler_params=pltpu.CompilerParams(vmem_limit_bytes=48 * MIB),
        cost_estimate=pl.CostEstimate(flops=4 * MIB, bytes_accessed=13 * MIB, transcendentals=0),
        name="finish",
    )(place, hbm(middle), hbm(border), *[hbm(p) for p in pieces])


def deliver_kernel(got, out):
    for i in range(got.shape[0]):
        out[0, :, i * CY : (i + 1) * CY] = got[i]


def deliver(got, tiles=8):
    count, total, _ = got.shape
    return pl.pallas_call(
        deliver_kernel,
        grid=(count // tiles,),
        in_specs=[pl.BlockSpec((tiles, total, CY), lambda c: (c, 0, 0))],
        out_specs=pl.BlockSpec((1, total, tiles * CY), lambda c: (0, 0, c)),
        out_shape=pltpu.HBM((1, total, count * CY), bf16),
        compiler_params=pltpu.CompilerParams(vmem_limit_bytes=32 * MIB),
        cost_estimate=pl.CostEstimate(flops=0, bytes_accessed=5 * MIB, transcendentals=0),
        name="deliver",
    )(got)


def sides():
    groups = []
    for core in range(2):
        for side in range(2):
            groups.append([(((t % 2) ^ side) * 2 + core) * 32 + t for t in range(32)])
    return groups


def shards(tracers, courant, neighbours, owner_map, gain, w_in, b_in, w_mid, b_mid, w_out):
    species = tracers.shape[0]
    me = lax.axis_index("spec")
    tile = lax.axis_index("tile")
    rows = tracers.reshape(-1, CY)

    west, east = pack_halo(rows, courant, neighbours)
    west = lax.ppermute(west, "tile", [(i, i + 1) for i in range(31)])
    east = lax.ppermute(east, "tile", [(i + 1, i) for i in range(31)])

    owner = owner_map[0]
    owner_spec, owner_tile = owner // 32, owner % 32
    worker = owner_spec ^ (((owner_tile ^ tile) & 1) * 2)
    place = (worker ^ me) * 32 + owner_tile
    group = jnp.arange(4, dtype=i32) ^ me

    middle, edge, filled = interior(place, rows, courant, neighbours)
    border_cols, *pieces = border(CHUNKS, place, courant, neighbours, west, east, edge, filled)

    def swap(parts):
        got = [lax.ppermute(parts[k], "spec", [(i, i ^ k) for i in range(4)]) for k in (2, 3, 1)]
        return [parts[0], got[2], got[0], got[1]]

    given = lax.optimization_barrier((gain, w_in, b_in, w_mid, b_mid, w_out, border_cols))[:-1]
    prepared = turn_weights(*given)
    own, returned = None, []
    for members in HOME:
        start, home_count = sum(CHUNKS[: members[0]]), sum(CHUNKS[j] for j in members)
        back = []
        for j in members:
            arrived = swap(pieces[4 * j : 4 * j + 4])
            own, back = chemistry(sum(CHUNKS[:j]), (start, home_count), group, prepared, arrived, own, back)
        returned.append(swap(back))
    own, returned[0] = lax.optimization_barrier((own, returned[0]))
    returned = [p for part in returned for p in part]
    owned = lax.all_to_all(own, AXES, 0, 0, axis_index_groups=sides(), tiled=True)
    out = finish(place, middle, border_cols, returned)
    return out.reshape(tracers.shape), deliver(owned)


def solution(mesh):
    return jax.shard_map(
        shards,
        mesh=mesh,
        in_specs=(
            P("spec", None, "tile", None),
            P(None, "tile", None),
            P(None, "tile", None),
            P("tile", None),
            P(),
            P(),
            P(),
            P(),
            P(),
            P(),
        ),
        out_specs=(P("spec", None, "tile", None), P(AXES, None, None)),
        check_vma=False,
    )
```

time: 212 us -> 125 us (0.59)
  Pallas kernels: 113 us -> 66 us
  waiting for transfers between devices: 56.7 us -> 23.1 us
  local copies, waits for them, and re-layouts: 16.4 us -> 4.43 us
  starting transfers between devices: 22.5 us -> 30.1 us
  other arithmetic: 2.53 us -> 0.02 us
    pallas_call x3 -> x6, Pallas kernels: 89.2 us -> 40 us  [the longest x1 12.7 us: interior(): pl.pallas_call(interior_kernel, in_specs=[smem()] + [anywhere()] * 3, out...]
    ppermute x6 -> x15, waiting for transfers between devices: 49.9 us -> 22.2 us  [swap(): lax.ppermute(parts[k], 'spec', [(i, i ^ k) for i in range(4)])]
    unnamed x30 -> x48, local copies, waits for them, and re-layouts: 10.9 us -> 3.01 us
    ppermute x6 -> x15, starting transfers between devices: 5.56 us -> 12.8 us  [swap(): lax.ppermute(parts[k], 'spec', [(i, i ^ k) for i in range(4)])]
    ppermute x1, waiting for transfers between devices: 6.73 us -> 0.29 us  [shards(): east = lax.ppermute(east, 'tile', [(i + 1, i) for i in range(31)])]
    pallas_call x1 -> x3, Pallas kernels: 23.4 us -> 26 us  [chemistry(): pl.pallas_call(functools.partial(chem_kernel, slots), grid=(count // slot...]
    transpose x1 -> x0, local copies, waits for them, and re-layouts: 2.58 us -> none  [shards(): owned = owned.transpose(1, 0, 2).reshape(1, 4 * species, 32 * CY)]
    transpose x2 -> x0, other arithmetic: 2.5 us -> none  [the longest x1 1.5 us: shards(): w2 = (w_mid * 0.5).T]
  transfers between devices with their start and end apart: 9 -> 18, of which waited for: 5 -> 7; matrix products, arithmetic and copies ran while one was open for 4% -> 1% of each run, Pallas kernels for 13% -> 42%
where the time goes in v2:
time: 125 us
  Pallas kernels  66 us (53%)
  starting transfers between devices  30.1 us (24%)
  waiting for transfers between devices  23.1 us (18%)
  local copies, waits for them, and re-layouts  4.43 us (4%)
    pallas_call x3, Pallas kernels, chemistry(): pl.pallas_call(functools.partial(chem_kernel, slots), grid=(count // slot...  26 us
    ppermute x15, waiting for transfers between devices, swap(): lax.ppermute(parts[k], 'spec', [(i, i ^ k) for i in range(4)])  22.2 us
    ppermute x15, starting transfers between devices, swap(): lax.ppermute(parts[k], 'spec', [(i, i ^ k) for i in range(4)])  12.8 us
    pallas_call x1, Pallas kernels, interior(): pl.pallas_call(interior_kernel, in_specs=[smem()] + [anywhere()] * 3, out...  12.7 us
    pallas_call x1, Pallas kernels, finish(): pl.pallas_call(functools.partial(finish_kernel, wide), grid=(n // wide,),...  12.6 us
    all_to_all x1, starting transfers between devices, shards(): lax.all_to_all(own, AXES, 0, 0, axis_index_groups=sides(), tiled=True)  10.4 us
    pallas_call x1, Pallas kernels, border(): pl.pallas_call(functools.partial(border_kernel, chunks), in_specs=[smem()...  7.88 us
    ppermute x1, starting transfers between devices, shards(): west = lax.ppermute(west, 'tile', [(i, i + 1) for i in range(31)])  5.5 us
  transfers between devices with their start and end apart: 18, of which 7 were waited for; matrix products, arithmetic and copies ran while one was open for 1% of the time, Pallas kernels for 42%

profile of v2, /device:TPU:1, one launch (start us, length us, event | category | flops | bytes accessed | tf_op | source)
XLA Modules:
  0.0 124.5 jit_solution(10160357397328971482)
XLA Ops:
  0.6 3.3 %pack_halo.1 = (bf16[1168,128]{1,0:T(8,128)(2,1)}, bf16[1168,128]{1,0:T(8,128)(2,1)}) custom-call(f32[9216,128]{1,0:T(8,128)} %bitcast.21, f32[4,16,128]{2,1,0:T(8,128)} %courant.5, s32[2,16,128]{2,1,0:T(8,128)} %nbr.5), custom_call_target="tpu_custom_call" | custom-call | bytes 6291456 | tf_op jit(solution)/shard_map/pack_halo/pallas_call | solution.py:91
  4.0 5.5 %collective-permute-start = (bf16[1168,128]{1,0:T(8,128)(2,1)}, bf16[1168,128]{1,0:T(8,128)(2,1)S(1)}, u32[]{:S(2)}, u32[]{:S(2)}) collective-permute-start(bf16[1168,128]{1,0:T(8,128)(2,1)} %get-tuple-element.53), channel_id=1, source_target_pairs={{0,1},{1,2},{2,3},{3,4},{4,5},{5,6},{6,7},{7,8},{8,9},{9,10},{10,1... | collective-permute-start | bytes 897032 | tf_op jit(solution)/shard_map/ppermute | solution.py:538
  9.5 1.3 %collective-permute-start.1 = (bf16[1168,128]{1,0:T(8,128)(2,1)}, bf16[1168,128]{1,0:T(8,128)(2,1)S(1)}, u32[]{:S(2)}, u32[]{:S(2)}) collective-permute-start(bf16[1168,128]{1,0:T(8,128)(2,1)} %get-tuple-element.54), channel_id=1, source_target_pairs={{1,0},{2,1},{3,2},{4,3},{5,4},{6,5},{7,6},{8,7},{9,8},{10,9},{11,1... | collective-permute-start | bytes 897032 | tf_op jit(solution)/shard_map/ppermute | solution.py:539
  10.8 12.7 %interior.1 = (f32[12,576,128]{2,1,0:T(8,128)}, f32[8,576,128]{2,1,0:T(8,128)S(1)}, f32[128,72,128]{2,1,0:T(8,128)}) custom-call(s32[128]{0:T(128)S(1)} %multiply_add_fusion.place, f32[9216,128]{1,0:T(8,128)} %bitcast.22, f32[4,16,128]{2,1,0:T(8,128)} %courant.5, s32[2,16,128]{2,1,0:T(8,128)} %nbr.5), custom_call_target="tpu_custom_call" | custom-call | flops 8999999488 | bytes 16777216 | tf_op jit(solution)/shard_map/interior/pallas_call | solution.py:225
  24.6 7.9 %border.1 = (f32[4,576,128]{2,1,0:T(8,128)}, bf16[864,128]{1,0:T(8,128)(2,1)}, bf16[864,128]{1,0:T(8,128)(2,1)}, bf16[864,128]{1,0:T(8,128)(2,1)}, bf16[864,128]...) custom-call(s32[128]{0:T(128)S(1)} %multiply_add_fusion.place, ...), custom_call_target="tpu_custom_call" | custom-call | flops 3000000000 | bytes 11534336 | tf_op jit(solution)/shard_map/border/pallas_call | solution.py:326
  32.5 1.6 %collective-permute-start.8 = (bf16[864,128]{1,0:T(8,128)(2,1)}, bf16[864,128]{1,0:T(8,128)(2,1)}, u32[]{:S(2)}, u32[]{:S(2)}) collective-permute-start(bf16[864,128]{1,0:T(8,128)(2,1)} %get-tuple-element.79), channel_id=1, source_target_pairs={{0,32},{32,0},{64,96},{96,64},{1,33},{33,1},{65,97},{97,65},{2,34}... | collective-permute-start | bytes 663560 | tf_op jit(solution)/shard_map/ppermute | solution.py:551
  34.1 1.2 collective-permute-start.9
  36.1 1.2 collective-permute-start.3
  37.3 1.4 %copy.18.w_out = bf16[1024,288]{1,0:T(8,128)(2,1)S(1)} copy(bf16[1024,288]{0,1:T(8,128)(2,1)} %param.19) | data formatting | bytes 1179648 | tf_op jit(solution)/shard_map/optimization_barrier | solution.py:554
  38.8 1.4 %turn_weights.1 = (bf16[1024,288]{1,0:T(8,128)(2,1)S(1)}, bf16[1024,1024]{1,0:T(8,128)(2,1)S(1)}, bf16[288,1024]{1,0:T(8,128)(2,1)S(1)}, f32[1024,128]{1,0:T(8,1...) custom-call(f32[1,288]{1,0:T(1,128)S(1)} %broadcast_in_dim.9.gain, bf16[288,1024]{1,0:T(8,128)(2,1)S(1)} %copy-done.1, ...), custom_call_target="tpu_custom_call" | custom-call | bytes 8388608 | tf_op jit(solution)/shard_map/turn_weights/pallas_call | solution.py:362
  41.4 1.2 collective-permute-start.6
  42.6 4.2 %collective-permute-done.10.p3 = bf16[864,128]{1,0:T(8,128)(2,1)} collective-permute-done((bf16[864,128]{1,0:T(8,128)(2,1)}, bf16[864,128]{1,0:T(8,128)(2,1)}, u32[]{:S(2)}, u32[]{:S(2)}) %collective-permute-start.10) | collective-permute-done | bytes 221216 | tf_op jit(solution)/shard_map/ppermute | solution.py:551
  46.8 0.8 collective-permute-start.7
  47.6 9.5 %chemistry.3 = (bf16[32,288,128]{2,1,0:T(8,128)(2,1)}, bf16[864,128]{1,0:T(8,128)(2,1)}, bf16[864,128]{1,0:T(8,128)(2,1)}, bf16[864,128]{1,0:T(8,128)(2,1)}, bf16[864,128]{1,0:T(8,128)(2,1)}) custom-call(s32[4]{0:T(128)S(1)} %iota_xor_fusion.group, f32[288,128]{1,0:T(8,128)S(1)} %get-tuple-element.64.gain, bf16[1024,288]{1,0:T(8,128)(2,1)S(1)} %get-tuple-element.65.w1, ...), custom_call_target="tpu_custom_call" | custom-call | flops 5033164800 | bytes 8388608 | tf_op jit(solution)/shard_map/chemistry/pallas_call | solution.py:436
  57.2 1.0 collective-permute-start.4
  58.9 1.2 collective-permute-start.12
  60.1 9.6 %chemistry.4 = (bf16[32,288,128]{2,1,0:T(8,128)(2,1)}, bf16[1440,128]{1,0:T(8,128)(2,1)}, bf16[1440,128]{1,0:T(8,128)(2,1)}, bf16[1440,128]{1,0:T(8,128)(2,1)}, bf16[1440,128]{1,0:T(8,128)(2,1)}) custom-call(s32[4]{0:T(128)S(1)} %iota_xor_fusion.group, f32[288,128]{1,0:T(8,128)S(1)} %get-tuple-element.64.gain, ...), custom_call_target="tpu_custom_call", output_to_operand_aliasing={{0}: (11, {})} | custom-call | flops 5033164800 | bytes 8388608 | tf_op jit(solution)/shard_map/chemistry/pallas_call | solution.py:436
  71.2 6.9 %chemistry.5 = (bf16[32,288,128]{2,1,0:T(8,128)(2,1)}, bf16[1440,128]{1,0:T(8,128)(2,1)}, bf16[1440,128]{1,0:T(8,128)(2,1)}, bf16[1440,128]{1,0:T(8,128)(2,1)}, bf16[1440,128]{1,0:T(8,128)(2,1)}) custom-call(s32[4]{0:T(128)S(1)} %iota_xor_fusion.group, ...), custom_call_target="tpu_custom_call", output_to_operand_aliasing={{0}: (11, {}), {1}: (12, {}), {2}: (13, {}), {3}: (14, {}),... | custom-call | flops 3355443200 | bytes 8388608 | tf_op jit(solution)/shard_map/chemistry/pallas_call | solution.py:436
  78.9 10.4 %all-to-all-start = ((bf16[32,288,128]{2,1,0:T(8,128)(2,1)}), bf16[32,288,128]{2,1,0:T(8,128)(2,1)S(1)}, u32[]{:S(2)}, u32[]{:S(2)}) async-start(bf16[32,288,128]{2,1,0:T(8,128)(2,1)} %get-tuple-element.101), calls=%async_computation | async-start | bytes 4718592 | tf_op jit(solution)/shard_map/all_to_all | solution.py:566
  89.8 1.8 %collective-permute-start.16 = (bf16[1440,128]{1,0:T(8,128)(2,1)}, bf16[1440,128]{1,0:T(8,128)(2,1)S(1)}, u32[]{:S(2)}, u32[]{:S(2)}) collective-permute-start(bf16[1440,128]{1,0:T(8,128)(2,1)} %get-tuple-element.100), channel_id=1, source_target_pairs={{0,96},{32,64},{64,32},{96,0},{1,97},{33,65},{65,33},{97,1},{2,98}... | collective-permute-start | bytes 1105928 | tf_op jit(solution)/shard_map/ppermute | solution.py:551
  91.6 8.3 %collective-permute-done.15.rest_6_ = bf16[1440,128]{1,0:T(8,128)(2,1)S(1)} collective-permute-done((bf16[1440,128]{1,0:T(8,128)(2,1)}, bf16[1440,128]{1,0:T(8,128)(2,1)S(1)}, u32[]{:S(2)}, u32[]{:S(2)}) %collective-permute-start.15) | collective-permute-done | bytes 368672 | tf_op jit(solution)/shard_map/ppermute | solution.py:551
  99.9 8.6 %collective-permute-done.16.rest_7_ = bf16[1440,128]{1,0:T(8,128)(2,1)S(1)} collective-permute-done((bf16[1440,128]{1,0:T(8,128)(2,1)}, bf16[1440,128]{1,0:T(8,128)(2,1)S(1)}, u32[]{:S(2)}, u32[]{:S(2)}) %collective-permute-start.16) | collective-permute-done | bytes 368672 | tf_op jit(solution)/shard_map/ppermute | solution.py:551
  109.2 12.6 %finish.1 = f32[9216,128]{1,0:T(8,128)} custom-call(s32[128]{0:T(128)S(1)} %multiply_add_fusion.place, f32[12,8,72,128]{3,2,1,0:T(8,128)} %bitcast.24, f32[4,8,72,128]{3,2,1,0:T(8,128)} %bitcast.25, bf16[864,128]{1,0:T(8,128)(2,1)} %get-tuple-element.93.rest_0_, bf16[864,128]{1,0:T(8,128)(2,1)} %copy-done.7, bf16[864,128]{1,0:T(8,128)(2,1)} %copy-done.8, ...), custom_call_target="tpu_custom_call" | custom-call | flops 4194304 | bytes 13631488 | tf_op jit(solution)/shard_map/finish/pallas_call | solution.py:491
  122.4 2.2 %deliver.1 = bf16[1,288,4096]{2,1,0:T(8,128)(2,1)} custom-call(bf16[32,288,128]{2,1,0:T(8,128)(2,1)S(1)} %all-to-all-done.got), custom_call_target="tpu_custom_call" | custom-call | bytes 5242880 | tf_op jit(solution)/shard_map/deliver/pallas_call | solution.py:511
  (73 shorter events, 7.8 us)
Async XLA Ops:
  4.0 19.5 %collective-permute-start = (bf16[1168,128]{1,0:T(8,128)(2,1)}, bf16[1168,128]{1,0:T(8,128)(2,1)S(1)}, u32[]{:S(2)}, u32[]{:S(2)}) collective-permute-start(bf16[1168,128]{1,0:T(8,128)(2,1)} %get-tuple-element.53), channel_id=1, source_target_pairs={{0,1},{1,2},{2,3},{3,4},{4,5},{5,6},{6,7},{7,8},{8,9},{9,10},{10,1... | collective-permute-start | bytes 897032 | tf_op jit(solution)/shard_map/ppermute | solution.py:538
  9.5 14.3 %collective-permute-start.1 = (bf16[1168,128]{1,0:T(8,128)(2,1)}, bf16[1168,128]{1,0:T(8,128)(2,1)S(1)}, u32[]{:S(2)}, u32[]{:S(2)}) collective-permute-start(bf16[1168,128]{1,0:T(8,128)(2,1)} %get-tuple-element.54), channel_id=1, source_target_pairs={{1,0},{2,1},{3,2},{4,3},{5,4},{6,5},{7,6},{8,7},{9,8},{10,9},{11,1... | collective-permute-start | bytes 897032 | tf_op jit(solution)/shard_map/ppermute | solution.py:539
  24.6 11.3 %copy-start.10 = (f32[288]{0:T(512)S(1)}, f32[288]{0:T(512)}, u32[]{:S(2)}) copy-start(f32[288]{0:T(512)} %param.14) | copy-start | bytes 3460
  24.6 14.2 %copy-start = (bf16[1024,1024]{1,0:T(8,128)(2,1)S(1)}, bf16[1024,1024]{1,0:T(8,128)(2,1)}, u32[]{:S(2)}) copy-start(bf16[1024,1024]{1,0:T(8,128)(2,1)} %w_mid) | copy-start | bytes 6291460
  24.6 14.2 %copy-start.1 = (bf16[288,1024]{1,0:T(8,128)(2,1)S(1)}, bf16[288,1024]{1,0:T(8,128)(2,1)}, u32[]{:S(2)}) copy-start(bf16[288,1024]{1,0:T(8,128)(2,1)} %w_in) | copy-start | bytes 1769476
  24.6 14.2 %copy-start.2 = (f32[1024]{0:T(1024)S(1)}, f32[1024]{0:T(1024)}, u32[]{:S(2)}) copy-start(f32[1024]{0:T(1024)} %param.16) | copy-start | bytes 12292
  24.6 14.2 %copy-start.3 = (f32[1024]{0:T(1024)S(1)}, f32[1024]{0:T(1024)}, u32[]{:S(2)}) copy-start(f32[1024]{0:T(1024)} %param.18) | copy-start | bytes 12292
  32.5 7.7 %collective-permute-start.8 = (bf16[864,128]{1,0:T(8,128)(2,1)}, bf16[864,128]{1,0:T(8,128)(2,1)}, u32[]{:S(2)}, u32[]{:S(2)}) collective-permute-start(bf16[864,128]{1,0:T(8,128)(2,1)} %get-tuple-element.79), channel_id=1, source_target_pairs={{0,32},{32,0},{64,96},{96,64},{1,33},{33,1},{65,97},{97,65},{2,34}... | collective-permute-start | bytes 663560 | tf_op jit(solution)/shard_map/ppermute | solution.py:551
  34.1 7.3 %collective-permute-start.9 = (bf16[864,128]{1,0:T(8,128)(2,1)}, bf16[864,128]{1,0:T(8,128)(2,1)}, u32[]{:S(2)}, u32[]{:S(2)}) collective-permute-start(bf16[864,128]{1,0:T(8,128)(2,1)} %get-tuple-element.80), channel_id=1, source_target_pairs={{0,64},{32,96},{64,0},{96,32},{1,65},{33,97},{65,1},{97,33},{2,66}... | collective-permute-start | bytes 663560 | tf_op jit(solution)/shard_map/ppermute | solution.py:551
  35.3 11.5 %collective-permute-start.10 = (bf16[864,128]{1,0:T(8,128)(2,1)}, bf16[864,128]{1,0:T(8,128)(2,1)}, u32[]{:S(2)}, u32[]{:S(2)}) collective-permute-start(bf16[864,128]{1,0:T(8,128)(2,1)} %get-tuple-element.81), channel_id=1, source_target_pairs={{0,96},{32,64},{64,32},{96,0},{1,97},{33,65},{65,33},{97,1},{2,98}... | collective-permute-start | bytes 663560 | tf_op jit(solution)/shard_map/ppermute | solution.py:551
  35.8 33.8 %collective-permute-start.2 = (bf16[576,128]{1,0:T(8,128)(2,1)}, bf16[576,128]{1,0:T(8,128)(2,1)}, u32[]{:S(2)}, u32[]{:S(2)}) collective-permute-start(bf16[576,128]{1,0:T(8,128)(2,1)} %get-tuple-element.71), channel_id=1, source_target_pairs={{0,32},{32,0},{64,96},{96,64},{1,33},{33,1},{65,97},{97,65},{2,34}... | collective-permute-start | bytes 442376 | tf_op jit(solution)/shard_map/ppermute | solution.py:551
  36.1 34.4 %collective-permute-start.3 = (bf16[576,128]{1,0:T(8,128)(2,1)}, bf16[576,128]{1,0:T(8,128)(2,1)}, u32[]{:S(2)}, u32[]{:S(2)}) collective-permute-start(bf16[576,128]{1,0:T(8,128)(2,1)} %get-tuple-element.72), channel_id=1, source_target_pairs={{0,64},{32,96},{64,0},{96,32},{1,65},{33,97},{65,1},{97,33},{2,66}... | collective-permute-start | bytes 442376 | tf_op jit(solution)/shard_map/ppermute | solution.py:551
  40.2 17.0 %collective-permute-start.5 = (bf16[864,128]{1,0:T(8,128)(2,1)S(1)}, bf16[864,128]{1,0:T(8,128)(2,1)S(1)}, u32[]{:S(2)}, u32[]{:S(2)}) collective-permute-start(bf16[864,128]{1,0:T(8,128)(2,1)S(1)} %copy-done.18), channel_id=1, source_target_pairs={{0,32},{32,0},{64,96},{96,64},{1,33},{33,1},{65,97},{97,65},{2,34}... | collective-permute-start | bytes 663560 | tf_op jit(solution)/shard_map/ppermute | solution.py:551
  41.4 16.8 %collective-permute-start.6 = (bf16[864,128]{1,0:T(8,128)(2,1)S(1)}, bf16[864,128]{1,0:T(8,128)(2,1)S(1)}, u32[]{:S(2)}, u32[]{:S(2)}) collective-permute-start(bf16[864,128]{1,0:T(8,128)(2,1)S(1)} %copy-done.17), channel_id=1, source_target_pairs={{0,64},{32,96},{64,0},{96,32},{1,65},{33,97},{65,1},{97,33},{2,66}... | collective-permute-start | bytes 663560 | tf_op jit(solution)/shard_map/ppermute | solution.py:551
  46.8 12.1 %collective-permute-start.7 = (bf16[864,128]{1,0:T(8,128)(2,1)S(1)}, bf16[864,128]{1,0:T(8,128)(2,1)S(1)}, u32[]{:S(2)}, u32[]{:S(2)}) collective-permute-start(bf16[864,128]{1,0:T(8,128)(2,1)S(1)} %copy-done.15), channel_id=1, source_target_pairs={{0,96},{32,64},{64,32},{96,0},{1,97},{33,65},{65,33},{97,1},{2,98}... | collective-permute-start | bytes 663560 | tf_op jit(solution)/shard_map/ppermute | solution.py:551
  57.2 13.3 %collective-permute-start.4 = (bf16[576,128]{1,0:T(8,128)(2,1)S(1)}, bf16[576,128]{1,0:T(8,128)(2,1)S(1)}, u32[]{:S(2)}, u32[]{:S(2)}) collective-permute-start(bf16[576,128]{1,0:T(8,128)(2,1)S(1)} %copy-done.22), channel_id=1, source_target_pairs={{0,96},{32,64},{64,32},{96,0},{1,97},{33,65},{65,33},{97,1},{2,98}... | collective-permute-start | bytes 442376 | tf_op jit(solution)/shard_map/ppermute | solution.py:551
  58.2 19.9 %collective-permute-start.11 = (bf16[864,128]{1,0:T(8,128)(2,1)}, bf16[864,128]{1,0:T(8,128)(2,1)S(1)}, u32[]{:S(2)}, u32[]{:S(2)}) collective-permute-start(bf16[864,128]{1,0:T(8,128)(2,1)} %get-tuple-element.90), channel_id=1, source_target_pairs={{0,32},{32,0},{64,96},{96,64},{1,33},{33,1},{65,97},{97,65},{2,34}... | collective-permute-start | bytes 663560 | tf_op jit(solution)/shard_map/ppermute | solution.py:551
  58.9 19.2 %collective-permute-start.12 = (bf16[864,128]{1,0:T(8,128)(2,1)}, bf16[864,128]{1,0:T(8,128)(2,1)S(1)}, u32[]{:S(2)}, u32[]{:S(2)}) collective-permute-start(bf16[864,128]{1,0:T(8,128)(2,1)} %get-tuple-element.91), channel_id=1, source_target_pairs={{0,64},{32,96},{64,0},{96,32},{1,65},{33,97},{65,1},{97,33},{2,66}... | collective-permute-start | bytes 663560 | tf_op jit(solution)/shard_map/ppermute | solution.py:551
  69.7 8.4 %collective-permute-start.13 = (bf16[864,128]{1,0:T(8,128)(2,1)S(1)}, bf16[864,128]{1,0:T(8,128)(2,1)S(1)}, u32[]{:S(2)}, u32[]{:S(2)}) collective-permute-start(bf16[864,128]{1,0:T(8,128)(2,1)S(1)} %copy-done.16), channel_id=1, source_target_pairs={{0,96},{32,64},{64,32},{96,0},{1,97},{33,65},{65,33},{97,1},{2,98}... | collective-permute-start | bytes 663560 | tf_op jit(solution)/shard_map/ppermute | solution.py:551
  78.9 43.4 %all-to-all-start = ((bf16[32,288,128]{2,1,0:T(8,128)(2,1)}), bf16[32,288,128]{2,1,0:T(8,128)(2,1)S(1)}, u32[]{:S(2)}, u32[]{:S(2)}) async-start(bf16[32,288,128]{2,1,0:T(8,128)(2,1)} %get-tuple-element.101), calls=%async_computation | async-start | bytes 4718592 | tf_op jit(solution)/shard_map/all_to_all | solution.py:566
  89.4 2.2 %collective-permute-start.14 = (bf16[1440,128]{1,0:T(8,128)(2,1)S(1)}, bf16[1440,128]{1,0:T(8,128)(2,1)S(1)}, u32[]{:S(2)}, u32[]{:S(2)}) collective-permute-start(bf16[1440,128]{1,0:T(8,128)(2,1)S(1)} %copy-done.12), channel_id=1, source_target_pairs={{0,32},{32,0},{64,96},{96,64},{1,33},{33,1},{65,97},{97,65},{2,34}... | collective-permute-start | bytes 1105928 | tf_op jit(solution)/shard_map/ppermute | solution.py:551
  89.8 10.2 %collective-permute-start.15 = (bf16[1440,128]{1,0:T(8,128)(2,1)}, bf16[1440,128]{1,0:T(8,128)(2,1)S(1)}, u32[]{:S(2)}, u32[]{:S(2)}) collective-permute-start(bf16[1440,128]{1,0:T(8,128)(2,1)} %get-tuple-element.99), channel_id=1, source_target_pairs={{0,64},{32,96},{64,0},{96,32},{1,65},{33,97},{65,1},{97,33},{2,66}... | collective-permute-start | bytes 1105928 | tf_op jit(solution)/shard_map/ppermute | solution.py:551
  89.8 18.6 %collective-permute-start.16 = (bf16[1440,128]{1,0:T(8,128)(2,1)}, bf16[1440,128]{1,0:T(8,128)(2,1)S(1)}, u32[]{:S(2)}, u32[]{:S(2)}) collective-permute-start(bf16[1440,128]{1,0:T(8,128)(2,1)} %get-tuple-element.100), channel_id=1, source_target_pairs={{0,96},{32,64},{64,32},{96,0},{1,97},{33,65},{65,33},{97,1},{2,98}... | collective-permute-start | bytes 1105928 | tf_op jit(solution)/shard_map/ppermute | solution.py:551
  91.6 16.9 %copy-start.4 = (bf16[1440,128]{1,0:T(8,128)(2,1)}, bf16[1440,128]{1,0:T(8,128)(2,1)S(1)}, u32[]{:S(2)}) copy-start(bf16[1440,128]{1,0:T(8,128)(2,1)S(1)} %collective-permute-done.14.rest_5_) | copy-start | bytes 1105924
  (18 other events, 72.5 us)

commit v3 on v2

--- a/solution.py
+++ b/solution.py
@@ -13,8 +13,8 @@
 BLOCK = 16
 GROUP = 8
 EXTRA = 16
-CHUNKS = (12, 12, 8)
-HOME = ((0,), (1, 2))
+CHUNKS = (16, 16)
+HOME = ((0,), (1,))
 MIB = 1024 * 1024
 AXES = ("spec", "tile")
 f32, bf16, i32 = jnp.float32, jnp.bfloat16, jnp.int32
@@ -264,8 +264,8 @@
     ]
     for copy in copies:
         copy.start()
-    for copy in copies[:4]:
-        copy.wait()
+    copies[0].wait()
+    copies[1].wait()
 
     def halo_weights(halo):
         e = halo[n : n + EXTRA, :].astype(f32)
@@ -283,28 +283,32 @@
     def parts(i):
         return split(edge[i])
 
+    inner = {}
+    for x in (0, 1, 15, 14):
+        c, ind = column_weights(cour, near_ind, x)
+        inner[x] = weights(c, ind), c
+    kept = [parts(i) for i in range(8)]
+    copies[2].wait()
     far, near = west[0:size, :], west[size:n, :]
     c, ind = halo_weights(west)
-    a = split(move([far, near, parts(0)], near.astype(f32), weights(c, ind), c))
-    c0, ind0 = column_weights(cour, near_ind, 0)
-    m0 = weights(c0, ind0)
-    b = move([near, parts(0), parts(1)], edge[0], m0, c0)
-    place_column(0, move([a, split(b), parts(4)], b, m0, c0))
-    c1, ind1 = column_weights(cour, near_ind, 1)
-    place_column(1, move([split(b), parts(4), parts(5)], edge[4], weights(c1, ind1), c1))
+    b = move([near, kept[0], kept[1]], edge[0], *inner[0])
+    a = split(move([far, near, kept[0]], near.astype(f32), weights(c, ind), c))
+    low = split(b)
+    place_column(1, move([low, kept[4], kept[5]], edge[4], *inner[1]))
+    place_column(0, move([a, low, kept[4]], b, *inner[0]))
+    copies[4].wait()
+    for i in range(2):
+        put_blocks(place, msg, i, moved.at[i], species)
+    copies[3].wait()
     near, far = east[0:size, :], east[size:n, :]
     c, ind = halo_weights(east)
-    a = split(move([parts(3), near, far], near.astype(f32), weights(c, ind), c))
-    c0, ind0 = column_weights(cour, near_ind, 15)
-    m0 = weights(c0, ind0)
-    b = move([parts(2), parts(3), near], edge[3], m0, c0)
-    place_column(3, move([parts(7), split(b), a], b, m0, c0))
-    c1, ind1 = column_weights(cour, near_ind, 14)
-    place_column(2, move([parts(6), parts(7), split(b)], edge[7], weights(c1, ind1), c1))
-
-    copies[4].wait()
-    for i, x in enumerate((0, 1, 14, 15)):
-        put_blocks(place, msg, x, moved.at[i], species)
+    b = move([kept[2], kept[3], near], edge[3], *inner[15])
+    a = split(move([kept[3], near, far], near.astype(f32), weights(c, ind), c))
+    low = split(b)
+    place_column(2, move([kept[6], kept[7], low], edge[7], *inner[14]))
+    place_column(3, move([kept[7], low, a], b, *inner[15]))
+    for i in range(2, 4):
+        put_blocks(place, msg, i + 12, moved.at[i], species)
     first = 0
     for j, count in enumerate(chunks):
         for k in (2, 3, 1, 0):
@@ -343,7 +347,7 @@
         compiler_params=pltpu.CompilerParams(vmem_limit_bytes=40 * MIB),
         cost_estimate=pl.CostEstimate(flops=3 * 10**9, bytes_accessed=11 * MIB, transcendentals=0),
         name="border",
-    )(place, hbm(courant), hbm(nbr), hbm(west), hbm(east), edge, hbm(filled))
+    )(place, hbm(courant), hbm(nbr), west, east, edge, hbm(filled))
 
 
 def turn_kernel(gain, w_in, b_in, w_mid, b_mid, w_out, w1, w2, w3, b1, b2, g):
@@ -450,17 +454,22 @@
         compiler_params=pltpu.CompilerParams(vmem_limit_bytes=36 * MIB),
         cost_estimate=pl.CostEstimate(flops=flops, bytes_accessed=8 * MIB, transcendentals=2 * hidden * count * CY),
         name="chemistry",
-    )(group, *fixed, *[hbm(p) for p in pieces], *[hbm(a) for a in handed])
+    )(group, *fixed, *pieces, *[hbm(a) for a in handed])
     return own, back
 
 
 def finish_kernel(wide, place, middle, border, *rest):
-    pieces, (out, tend) = rest[:-2], rest[-2:]
+    pieces, (out, tend, cells, turn, turned) = rest[:-5], rest[-5:]
     step = pl.program_id(0)
     species = 72
 
     @pl.when(step == 0)
     def _():
+        source = lax.broadcasted_iota(i32, (CY, LEV * CY), 0)
+        target = lax.broadcasted_iota(i32, (CY, LEV * CY), 1)
+        for b in range(8):
+            hit = target == source // BLOCK * CY + b * BLOCK + source % BLOCK
+            turn[b * CY : (b + 1) * CY, :] = jnp.where(hit, 1.0, 0.0).astype(bf16)
         first = 0
         for j in range(0, len(pieces), 4):
             count = pieces[j].shape[0] // species
@@ -471,17 +480,22 @@
                     tend[k * 32 + first + i + 1] = pair[species:]
             first += count
 
+    at = pl.multiple_of(step * wide, GROUP)
+    for x in range(0, COLS, 2):
+        for b in range(8):
+            pair = [tend[place[(x + i) * 8 + b], pl.ds(at, wide), :] for i in range(2)]
+            cells[x * wide : (x + 2) * wide, b * CY : (b + 1) * CY] = jnp.concatenate(pair, axis=0).astype(bf16)
+    turned[...] = jnp.dot(cells[...], turn[...], preferred_element_type=f32)
     for x in range(COLS):
         src, y = (middle, x - 2) if 2 <= x < 14 else (border, x if x < 2 else x - 12)
         for c in range(wide // GROUP):
-            at = pl.multiple_of(step * wide + c * GROUP, GROUP)
-            tiles = [tend[place[x * 8 + b], pl.ds(at, GROUP), :] for b in range(8)]
-            for l, v in enumerate(swap_blocks(tiles)):
+            for l in range(LEV):
+                v = turned[x * wide + c * GROUP : x * wide + (c + 1) * GROUP, l * CY : (l + 1) * CY]
                 v = v + src[y, l, c * GROUP : (c + 1) * GROUP, :]
                 out[pl.ds(c * GROUP * LEV * COLS + l * COLS + x, GROUP, stride=LEV * COLS), :] = v
 
 
-def finish(place, middle, border, pieces, wide=8):
+def finish(place, middle, border, pieces, wide=24):
     n = middle.shape[1] // LEV
     middle, border = (a.reshape(a.shape[0], LEV, n, CY) for a in (middle, border))
 
@@ -494,11 +508,16 @@
         in_specs=[smem(), columns(middle), columns(border)] + [whole(p.shape) for p in pieces],
         out_specs=pl.BlockSpec((wide * LEV * COLS, CY), lambda c: (c, 0)),
         out_shape=pltpu.HBM((n * LEV * COLS, CY), f32),
-        scratch_shapes=[pltpu.VMEM((128, n, CY), f32)],
+        scratch_shapes=[
+            pltpu.VMEM((128, n, CY), f32),
+            pltpu.VMEM((COLS * wide, LEV * CY), bf16),
+            pltpu.VMEM((LEV * CY, LEV * CY), bf16),
+            pltpu.VMEM((COLS * wide, LEV * CY), f32),
+        ],
         compiler_params=pltpu.CompilerParams(vmem_limit_bytes=48 * MIB),
         cost_estimate=pl.CostEstimate(flops=4 * MIB, bytes_accessed=13 * MIB, transcendentals=0),
         name="finish",
-    )(place, hbm(middle), hbm(border), *[hbm(p) for p in pieces])
+    )(place, hbm(middle), hbm(border), *pieces)
 
 
 def deliver_kernel(got, out):

time: 125 us -> 122 us (0.976)
  waiting for transfers between devices: 23.1 us -> 30.7 us
  Pallas kernels: 66 us -> 60.5 us
  starting transfers between devices: 30.1 us -> 27.5 us
  local copies, waits for them, and re-layouts: 4.43 us -> 2.43 us
    all_to_all x1, waiting for transfers between devices: 0.57 us -> 6.54 us  [shards(): lax.all_to_all(own, AXES, 0, 0, axis_index_groups=sides(), tiled=True)]
    ppermute x15 -> x12, starting transfers between devices: 12.8 us -> 10.1 us  [swap(): lax.ppermute(parts[k], 'spec', [(i, i ^ k) for i in range(4)])]
    pallas_call x1, Pallas kernels: 12.6 us -> 9.84 us  [finish(): pl.pallas_call(functools.partial(finish_kernel, wide), grid=(n // wide,),...]
    unnamed x48 -> x22, local copies, waits for them, and re-layouts: 3.01 us -> 1.01 us
    pallas_call x3 -> x2, Pallas kernels: 26 us -> 24.1 us  [chemistry(): pl.pallas_call(functools.partial(chem_kernel, slots), grid=(count // slot...]
    ppermute x15 -> x12, waiting for transfers between devices: 22.2 us -> 23.8 us  [swap(): lax.ppermute(parts[k], 'spec', [(i, i ^ k) for i in range(4)])]
  transfers between devices with their start and end apart: 18 -> 15, of which waited for: 7 -> 7; matrix products, arithmetic and copies ran while one was open for 1% -> 1% of each run, Pallas kernels for 42% -> 39%
where the time goes in v3:
time: 122 us
  Pallas kernels  60.5 us (50%)
  waiting for transfers between devices  30.7 us (25%)
  starting transfers between devices  27.5 us (23%)
  local copies, waits for them, and re-layouts  2.43 us (2%)
    pallas_call x2, Pallas kernels, chemistry(): pl.pallas_call(functools.partial(chem_kernel, slots), grid=(count // slot...  24.1 us
    ppermute x12, waiting for transfers between devices, swap(): lax.ppermute(parts[k], 'spec', [(i, i ^ k) for i in range(4)])  23.8 us
    pallas_call x1, Pallas kernels, interior(): pl.pallas_call(interior_kernel, in_specs=[smem()] + [anywhere()] * 3, out...  12.7 us
    all_to_all x1, starting transfers between devices, shards(): lax.all_to_all(own, AXES, 0, 0, axis_index_groups=sides(), tiled=True)  10.6 us
    ppermute x12, starting transfers between devices, swap(): lax.ppermute(parts[k], 'spec', [(i, i ^ k) for i in range(4)])  10.1 us
    pallas_call x1, Pallas kernels, finish(): pl.pallas_call(functools.partial(finish_kernel, wide), grid=(n // wide,),...  9.84 us
    pallas_call x1, Pallas kernels, border(): pl.pallas_call(functools.partial(border_kernel, chunks), in_specs=[smem()...  7.03 us
    all_to_all x1, waiting for transfers between devices, shards(): lax.all_to_all(own, AXES, 0, 0, axis_index_groups=sides(), tiled=True)  6.54 us
  transfers between devices with their start and end apart: 15, of which 7 were waited for; matrix products, arithmetic and copies ran while one was open for 1% of the time, Pallas kernels for 39%

profile of v3, /device:TPU:1, one launch (start us, length us, event | category | flops | bytes accessed | tf_op | source)
XLA Modules:
  0.0 121.9 jit_solution(10416428277260706948)
XLA Ops:
  0.6 3.3 %pack_halo.1 = (bf16[1168,128]{1,0:T(8,128)(2,1)}, bf16[1168,128]{1,0:T(8,128)(2,1)}) custom-call(f32[9216,128]{1,0:T(8,128)} %bitcast.21, f32[4,16,128]{2,1,0:T(8,128)} %courant.5, s32[2,16,128]{2,1,0:T(8,128)} %nbr.5), custom_call_target="tpu_custom_call" | custom-call | bytes 6291456 | tf_op jit(solution)/shard_map/pack_halo/pallas_call | solution.py:91
  4.0 5.5 %collective-permute-start = (bf16[1168,128]{1,0:T(8,128)(2,1)}, bf16[1168,128]{1,0:T(8,128)(2,1)S(1)}, u32[]{:S(2)}, u32[]{:S(2)}) collective-permute-start(bf16[1168,128]{1,0:T(8,128)(2,1)} %get-tuple-element.44), channel_id=1, source_target_pairs={{0,1},{1,2},{2,3},{3,4},{4,5},{5,6},{6,7},{7,8},{8,9},{9,10},{10,1... | collective-permute-start | bytes 897032 | tf_op jit(solution)/shard_map/ppermute | solution.py:557
  9.5 1.3 %collective-permute-start.1 = (bf16[1168,128]{1,0:T(8,128)(2,1)}, bf16[1168,128]{1,0:T(8,128)(2,1)S(1)}, u32[]{:S(2)}, u32[]{:S(2)}) collective-permute-start(bf16[1168,128]{1,0:T(8,128)(2,1)} %get-tuple-element.45), channel_id=1, source_target_pairs={{1,0},{2,1},{3,2},{4,3},{5,4},{6,5},{7,6},{8,7},{9,8},{10,9},{11,1... | collective-permute-start | bytes 897032 | tf_op jit(solution)/shard_map/ppermute | solution.py:558
  10.8 12.7 %interior.1 = (f32[12,576,128]{2,1,0:T(8,128)}, f32[8,576,128]{2,1,0:T(8,128)S(1)}, f32[128,72,128]{2,1,0:T(8,128)}) custom-call(s32[128]{0:T(128)S(1)} %multiply_add_fusion.place, f32[9216,128]{1,0:T(8,128)} %bitcast.22, f32[4,16,128]{2,1,0:T(8,128)} %courant.5, s32[2,16,128]{2,1,0:T(8,128)} %nbr.5), custom_call_target="tpu_custom_call" | custom-call | flops 8999999488 | bytes 16777216 | tf_op jit(solution)/shard_map/interior/pallas_call | solution.py:225
  23.8 7.0 %border.1 = (f32[4,576,128]{2,1,0:T(8,128)}, bf16[1152,128]{1,0:T(8,128)(2,1)}, bf16[1152,128]{1,0:T(8,128)(2,1)}, bf16[1152,128]{1,0:T(8,128)(2,1)}, bf16[1152,...) custom-call(s32[128]{0:T(128)S(1)} %multiply_add_fusion.place, ...), custom_call_target="tpu_custom_call" | custom-call | flops 3000000000 | bytes 11534336 | tf_op jit(solution)/shard_map/border/pallas_call | solution.py:330
  30.8 1.6 %collective-permute-start.5 = (bf16[1152,128]{1,0:T(8,128)(2,1)}, bf16[1152,128]{1,0:T(8,128)(2,1)}, u32[]{:S(2)}, u32[]{:S(2)}) collective-permute-start(bf16[1152,128]{1,0:T(8,128)(2,1)} %get-tuple-element.66), channel_id=1, source_target_pairs={{0,32},{32,0},{64,96},{96,64},{1,33},{33,1},{65,97},{97,65},{2,34}... | collective-permute-start | bytes 884744 | tf_op jit(solution)/shard_map/ppermute | solution.py:570
  32.5 1.2 %collective-permute-start.6 = (bf16[1152,128]{1,0:T(8,128)(2,1)}, bf16[1152,128]{1,0:T(8,128)(2,1)}, u32[]{:S(2)}, u32[]{:S(2)}) collective-permute-start(bf16[1152,128]{1,0:T(8,128)(2,1)} %get-tuple-element.67), channel_id=1, source_target_pairs={{0,64},{32,96},{64,0},{96,32},{1,65},{33,97},{65,1},{97,33},{2,66}... | collective-permute-start | bytes 884744 | tf_op jit(solution)/shard_map/ppermute | solution.py:570
  34.4 1.2 collective-permute-start.3
  35.6 1.4 %copy.13.w_out = bf16[1024,288]{1,0:T(8,128)(2,1)S(1)} copy(bf16[1024,288]{0,1:T(8,128)(2,1)} %param.19) | data formatting | bytes 1179648 | tf_op jit(solution)/shard_map/optimization_barrier | solution.py:573
  37.1 1.4 %turn_weights.1 = (bf16[1024,288]{1,0:T(8,128)(2,1)S(1)}, bf16[1024,1024]{1,0:T(8,128)(2,1)S(1)}, bf16[288,1024]{1,0:T(8,128)(2,1)S(1)}, f32[1024,128]{1,0:T(8,1...) custom-call(f32[1,288]{1,0:T(1,128)S(1)} %broadcast_in_dim.9.gain, bf16[288,1024]{1,0:T(8,128)(2,1)S(1)} %copy-done.1, ...), custom_call_target="tpu_custom_call" | custom-call | bytes 8388608 | tf_op jit(solution)/shard_map/turn_weights/pallas_call | solution.py:366
  39.4 1.9 %collective-permute-done.6.p2 = bf16[1152,128]{1,0:T(8,128)(2,1)} collective-permute-done((bf16[1152,128]{1,0:T(8,128)(2,1)}, bf16[1152,128]{1,0:T(8,128)(2,1)}, u32[]{:S(2)}, u32[]{:S(2)}) %collective-permute-start.6) | collective-permute-done | bytes 294944 | tf_op jit(solution)/shard_map/ppermute | solution.py:570
  41.4 7.0 %collective-permute-done.7.p3 = bf16[1152,128]{1,0:T(8,128)(2,1)} collective-permute-done((bf16[1152,128]{1,0:T(8,128)(2,1)}, bf16[1152,128]{1,0:T(8,128)(2,1)}, u32[]{:S(2)}, u32[]{:S(2)}) %collective-permute-start.7) | collective-permute-done | bytes 294944 | tf_op jit(solution)/shard_map/ppermute | solution.py:570
  48.3 12.1 %chemistry.2 = (bf16[32,288,128]{2,1,0:T(8,128)(2,1)}, bf16[1152,128]{1,0:T(8,128)(2,1)}, bf16[1152,128]{1,0:T(8,128)(2,1)}, bf16[1152,128]{1,0:T(8,128)(2,1)}, bf16[1152,128]{1,0:T(8,128)(2,1)}) custom-call(s32[4]{0:T(128)S(1)} %iota_xor_fusion.group, f32[288,128]{1,0:T(8,128)S(1)} %get-tuple-element.55.gain, bf16[1024,288]{1,0:T(8,128)(2,1)S(1)} %get-tuple-element.56.w1, ...), custom_call_target="tpu_custom_call" | custom-call | flops 6710886400 | bytes 8388608 | tf_op jit(solution)/shard_map/chemistry/pallas_call | solution.py:440
  60.5 1.3 %collective-permute-start.9 = (bf16[1152,128]{1,0:T(8,128)(2,1)}, bf16[1152,128]{1,0:T(8,128)(2,1)S(1)}, u32[]{:S(2)}, u32[]{:S(2)}) collective-permute-start(bf16[1152,128]{1,0:T(8,128)(2,1)} %get-tuple-element.73), channel_id=1, source_target_pairs={{0,64},{32,96},{64,0},{96,32},{1,65},{33,97},{65,1},{97,33},{2,66}... | collective-permute-start | bytes 884744 | tf_op jit(solution)/shard_map/ppermute | solution.py:570
  62.6 12.0 %chemistry.3 = (bf16[32,288,128]{2,1,0:T(8,128)(2,1)}, bf16[1152,128]{1,0:T(8,128)(2,1)}, bf16[1152,128]{1,0:T(8,128)(2,1)}, bf16[1152,128]{1,0:T(8,128)(2,1)}, bf16[1152,128]{1,0:T(8,128)(2,1)}) custom-call(s32[4]{0:T(128)S(1)} %iota_xor_fusion.group, f32[288,128]{1,0:T(8,128)S(1)} %get-tuple-element.55.gain, ...), custom_call_target="tpu_custom_call", output_to_operand_aliasing={{0}: (11, {})} | custom-call | flops 6710886400 | bytes 8388608 | tf_op jit(solution)/shard_map/chemistry/pallas_call | solution.py:440
  74.6 1.2 collective-permute-done.10.rest_3_
  75.8 10.6 %all-to-all-start = ((bf16[32,288,128]{2,1,0:T(8,128)(2,1)}), bf16[32,288,128]{2,1,0:T(8,128)(2,1)S(1)}, u32[]{:S(2)}, u32[]{:S(2)}) async-start(bf16[32,288,128]{2,1,0:T(8,128)(2,1)} %get-tuple-element.83), calls=%async_computation | async-start | bytes 4718592 | tf_op jit(solution)/shard_map/all_to_all | solution.py:585
  86.9 1.8 %collective-permute-start.13 = (bf16[1152,128]{1,0:T(8,128)(2,1)}, bf16[1152,128]{1,0:T(8,128)(2,1)S(1)}, u32[]{:S(2)}, u32[]{:S(2)}) collective-permute-start(bf16[1152,128]{1,0:T(8,128)(2,1)} %get-tuple-element.82), channel_id=1, source_target_pairs={{0,96},{32,64},{64,32},{96,0},{1,97},{33,65},{65,33},{97,1},{2,98}... | collective-permute-start | bytes 884744 | tf_op jit(solution)/shard_map/ppermute | solution.py:570
  88.7 6.8 %collective-permute-done.12.rest_6_ = bf16[1152,128]{1,0:T(8,128)(2,1)S(1)} collective-permute-done((bf16[1152,128]{1,0:T(8,128)(2,1)}, bf16[1152,128]{1,0:T(8,128)(2,1)S(1)}, u32[]{:S(2)}, u32[]{:S(2)}) %collective-permute-start.12) | collective-permute-done | bytes 294944 | tf_op jit(solution)/shard_map/ppermute | solution.py:570
  95.5 6.9 %collective-permute-done.13.rest_7_ = bf16[1152,128]{1,0:T(8,128)(2,1)S(1)} collective-permute-done((bf16[1152,128]{1,0:T(8,128)(2,1)}, bf16[1152,128]{1,0:T(8,128)(2,1)S(1)}, u32[]{:S(2)}, u32[]{:S(2)}) %collective-permute-start.13) | collective-permute-done | bytes 294944 | tf_op jit(solution)/shard_map/ppermute | solution.py:570
  102.4 1.0 copy-done.3
  103.4 9.8 %finish.1 = f32[9216,128]{1,0:T(8,128)} custom-call(s32[128]{0:T(128)S(1)} %multiply_add_fusion.place, f32[12,8,72,128]{3,2,1,0:T(8,128)} %bitcast.24, f32[4,8,72,128]{3,2,1,0:T(8,128)} %bitcast.25, bf16[1152,128]{1,0:T(8,128)(2,1)S(1)} %copy-done.2, bf16[1152,128]{1,0:T(8,128)(2,1)S(1)} %collective-permute-done.8.rest_1_, ...), custom_call_target="tpu_custom_call" | custom-call | flops 4194304 | bytes 13631488 | tf_op jit(solution)/shard_map/finish/pallas_call | solution.py:505
  113.2 6.5 %all-to-all-done.got = bf16[32,288,128]{2,1,0:T(8,128)(2,1)S(1)} async-done(((bf16[32,288,128]{2,1,0:T(8,128)(2,1)}), bf16[32,288,128]{2,1,0:T(8,128)(2,1)S(1)}, u32[]{:S(2)}, u32[]{:S(2)}) %all-to-all-start) | async-done | bytes 2359328 | tf_op jit(solution)/shard_map/all_to_all | solution.py:585
  119.8 2.2 %deliver.1 = bf16[1,288,4096]{2,1,0:T(8,128)(2,1)} custom-call(bf16[32,288,128]{2,1,0:T(8,128)(2,1)S(1)} %all-to-all-done.got), custom_call_target="tpu_custom_call" | custom-call | bytes 5242880 | tf_op jit(solution)/shard_map/deliver/pallas_call | solution.py:530
  (40 shorter events, 3.3 us)
Async XLA Ops:
  0.6 10.1 %copy-start.9 = (s32[1,128]{1,0:T(1,128)S(1)}, s32[1,128]{1,0:T(1,128)}, u32[]{:S(2)}) copy-start(s32[1,128]{1,0:T(1,128)} %param.13) | copy-start | bytes 1540
  4.0 19.5 %collective-permute-start = (bf16[1168,128]{1,0:T(8,128)(2,1)}, bf16[1168,128]{1,0:T(8,128)(2,1)S(1)}, u32[]{:S(2)}, u32[]{:S(2)}) collective-permute-start(bf16[1168,128]{1,0:T(8,128)(2,1)} %get-tuple-element.44), channel_id=1, source_target_pairs={{0,1},{1,2},{2,3},{3,4},{4,5},{5,6},{6,7},{7,8},{8,9},{9,10},{10,1... | collective-permute-start | bytes 897032 | tf_op jit(solution)/shard_map/ppermute | solution.py:557
  9.5 14.3 %collective-permute-start.1 = (bf16[1168,128]{1,0:T(8,128)(2,1)}, bf16[1168,128]{1,0:T(8,128)(2,1)S(1)}, u32[]{:S(2)}, u32[]{:S(2)}) collective-permute-start(bf16[1168,128]{1,0:T(8,128)(2,1)} %get-tuple-element.45), channel_id=1, source_target_pairs={{1,0},{2,1},{3,2},{4,3},{5,4},{6,5},{7,6},{8,7},{9,8},{10,9},{11,1... | collective-permute-start | bytes 897032 | tf_op jit(solution)/shard_map/ppermute | solution.py:558
  23.8 10.4 %copy-start.8 = (f32[288]{0:T(512)S(1)}, f32[288]{0:T(512)}, u32[]{:S(2)}) copy-start(f32[288]{0:T(512)} %param.14) | copy-start | bytes 3460
  23.8 13.3 %copy-start = (bf16[1024,1024]{1,0:T(8,128)(2,1)S(1)}, bf16[1024,1024]{1,0:T(8,128)(2,1)}, u32[]{:S(2)}) copy-start(bf16[1024,1024]{1,0:T(8,128)(2,1)} %w_mid) | copy-start | bytes 6291460
  23.8 13.3 %copy-start.1 = (bf16[288,1024]{1,0:T(8,128)(2,1)S(1)}, bf16[288,1024]{1,0:T(8,128)(2,1)}, u32[]{:S(2)}) copy-start(bf16[288,1024]{1,0:T(8,128)(2,1)} %w_in) | copy-start | bytes 1769476
  23.8 13.3 %copy-start.4 = (f32[1024]{0:T(1024)S(1)}, f32[1024]{0:T(1024)}, u32[]{:S(2)}) copy-start(f32[1024]{0:T(1024)} %param.16) | copy-start | bytes 12292
  23.8 13.3 %copy-start.5 = (f32[1024]{0:T(1024)S(1)}, f32[1024]{0:T(1024)}, u32[]{:S(2)}) copy-start(f32[1024]{0:T(1024)} %param.18) | copy-start | bytes 12292
  30.8 7.7 %collective-permute-start.5 = (bf16[1152,128]{1,0:T(8,128)(2,1)}, bf16[1152,128]{1,0:T(8,128)(2,1)}, u32[]{:S(2)}, u32[]{:S(2)}) collective-permute-start(bf16[1152,128]{1,0:T(8,128)(2,1)} %get-tuple-element.66), channel_id=1, source_target_pairs={{0,32},{32,0},{64,96},{96,64},{1,33},{33,1},{65,97},{97,65},{2,34}... | collective-permute-start | bytes 884744 | tf_op jit(solution)/shard_map/ppermute | solution.py:570
  32.5 8.9 %collective-permute-start.6 = (bf16[1152,128]{1,0:T(8,128)(2,1)}, bf16[1152,128]{1,0:T(8,128)(2,1)}, u32[]{:S(2)}, u32[]{:S(2)}) collective-permute-start(bf16[1152,128]{1,0:T(8,128)(2,1)} %get-tuple-element.67), channel_id=1, source_target_pairs={{0,64},{32,96},{64,0},{96,32},{1,65},{33,97},{65,1},{97,33},{2,66}... | collective-permute-start | bytes 884744 | tf_op jit(solution)/shard_map/ppermute | solution.py:570
  33.7 14.6 %collective-permute-start.7 = (bf16[1152,128]{1,0:T(8,128)(2,1)}, bf16[1152,128]{1,0:T(8,128)(2,1)}, u32[]{:S(2)}, u32[]{:S(2)}) collective-permute-start(bf16[1152,128]{1,0:T(8,128)(2,1)} %get-tuple-element.68), channel_id=1, source_target_pairs={{0,96},{32,64},{64,32},{96,0},{1,97},{33,65},{65,33},{97,1},{2,98}... | collective-permute-start | bytes 884744 | tf_op jit(solution)/shard_map/ppermute | solution.py:570
  34.2 27.6 %collective-permute-start.2 = (bf16[1152,128]{1,0:T(8,128)(2,1)}, bf16[1152,128]{1,0:T(8,128)(2,1)}, u32[]{:S(2)}, u32[]{:S(2)}) collective-permute-start(bf16[1152,128]{1,0:T(8,128)(2,1)} %get-tuple-element.62), channel_id=1, source_target_pairs={{0,32},{32,0},{64,96},{96,64},{1,33},{33,1},{65,97},{97,65},{2,34}... | collective-permute-start | bytes 884744 | tf_op jit(solution)/shard_map/ppermute | solution.py:570
  34.4 28.2 %collective-permute-start.3 = (bf16[1152,128]{1,0:T(8,128)(2,1)}, bf16[1152,128]{1,0:T(8,128)(2,1)}, u32[]{:S(2)}, u32[]{:S(2)}) collective-permute-start(bf16[1152,128]{1,0:T(8,128)(2,1)} %get-tuple-element.63), channel_id=1, source_target_pairs={{0,64},{32,96},{64,0},{96,32},{1,65},{33,97},{65,1},{97,33},{2,66}... | collective-permute-start | bytes 884744 | tf_op jit(solution)/shard_map/ppermute | solution.py:570
  37.1 11.2 %copy-start.7 = (bf16[1152,128]{1,0:T(8,128)(2,1)S(1)}, bf16[1152,128]{1,0:T(8,128)(2,1)}, u32[]{:S(2)}) copy-start(bf16[1152,128]{1,0:T(8,128)(2,1)} %get-tuple-element.65.p0) | copy-start | bytes 884740
  38.5 24.1 %collective-permute-start.4 = (bf16[1152,128]{1,0:T(8,128)(2,1)S(1)}, bf16[1152,128]{1,0:T(8,128)(2,1)S(1)}, u32[]{:S(2)}, u32[]{:S(2)}) collective-permute-start(bf16[1152,128]{1,0:T(8,128)(2,1)S(1)} %copy-done.10), channel_id=1, source_target_pairs={{0,96},{32,64},{64,32},{96,0},{1,97},{33,65},{65,33},{97,1},{2,98}... | collective-permute-start | bytes 884744 | tf_op jit(solution)/shard_map/ppermute | solution.py:570
  48.3 14.3 %copy-start.6 = (bf16[1152,128]{1,0:T(8,128)(2,1)S(1)}, bf16[1152,128]{1,0:T(8,128)(2,1)}, u32[]{:S(2)}) copy-start(bf16[1152,128]{1,0:T(8,128)(2,1)} %get-tuple-element.61.p0) | copy-start | bytes 884740
  60.4 14.2 %collective-permute-start.8 = (bf16[1152,128]{1,0:T(8,128)(2,1)}, bf16[1152,128]{1,0:T(8,128)(2,1)S(1)}, u32[]{:S(2)}, u32[]{:S(2)}) collective-permute-start(bf16[1152,128]{1,0:T(8,128)(2,1)} %get-tuple-element.72), channel_id=1, source_target_pairs={{0,32},{32,0},{64,96},{96,64},{1,33},{33,1},{65,97},{97,65},{2,34}... | collective-permute-start | bytes 884744 | tf_op jit(solution)/shard_map/ppermute | solution.py:570
  60.5 14.2 %collective-permute-start.9 = (bf16[1152,128]{1,0:T(8,128)(2,1)}, bf16[1152,128]{1,0:T(8,128)(2,1)S(1)}, u32[]{:S(2)}, u32[]{:S(2)}) collective-permute-start(bf16[1152,128]{1,0:T(8,128)(2,1)} %get-tuple-element.73), channel_id=1, source_target_pairs={{0,64},{32,96},{64,0},{96,32},{1,65},{33,97},{65,1},{97,33},{2,66}... | collective-permute-start | bytes 884744 | tf_op jit(solution)/shard_map/ppermute | solution.py:570
  61.8 14.1 %collective-permute-start.10 = (bf16[1152,128]{1,0:T(8,128)(2,1)}, bf16[1152,128]{1,0:T(8,128)(2,1)S(1)}, u32[]{:S(2)}, u32[]{:S(2)}) collective-permute-start(bf16[1152,128]{1,0:T(8,128)(2,1)} %get-tuple-element.74), channel_id=1, source_target_pairs={{0,96},{32,64},{64,32},{96,0},{1,97},{33,65},{65,33},{97,1},{2,98}... | collective-permute-start | bytes 884744 | tf_op jit(solution)/shard_map/ppermute | solution.py:570
  75.8 26.6 %copy-start.2 = (bf16[1152,128]{1,0:T(8,128)(2,1)S(1)}, bf16[1152,128]{1,0:T(8,128)(2,1)}, u32[]{:S(2)}) copy-start(bf16[1152,128]{1,0:T(8,128)(2,1)} %get-tuple-element.75.rest_0_) | copy-start | bytes 884740
  75.8 43.9 %all-to-all-start = ((bf16[32,288,128]{2,1,0:T(8,128)(2,1)}), bf16[32,288,128]{2,1,0:T(8,128)(2,1)S(1)}, u32[]{:S(2)}, u32[]{:S(2)}) async-start(bf16[32,288,128]{2,1,0:T(8,128)(2,1)} %get-tuple-element.83), calls=%async_computation | async-start | bytes 4718592 | tf_op jit(solution)/shard_map/all_to_all | solution.py:585
  86.5 2.2 %collective-permute-start.11 = (bf16[1152,128]{1,0:T(8,128)(2,1)}, bf16[1152,128]{1,0:T(8,128)(2,1)S(1)}, u32[]{:S(2)}, u32[]{:S(2)}) collective-permute-start(bf16[1152,128]{1,0:T(8,128)(2,1)} %get-tuple-element.80), channel_id=1, source_target_pairs={{0,32},{32,0},{64,96},{96,64},{1,33},{33,1},{65,97},{97,65},{2,34}... | collective-permute-start | bytes 884744 | tf_op jit(solution)/shard_map/ppermute | solution.py:570
  86.6 8.8 %collective-permute-start.12 = (bf16[1152,128]{1,0:T(8,128)(2,1)}, bf16[1152,128]{1,0:T(8,128)(2,1)S(1)}, u32[]{:S(2)}, u32[]{:S(2)}) collective-permute-start(bf16[1152,128]{1,0:T(8,128)(2,1)} %get-tuple-element.81), channel_id=1, source_target_pairs={{0,64},{32,96},{64,0},{96,32},{1,65},{33,97},{65,1},{97,33},{2,66}... | collective-permute-start | bytes 884744 | tf_op jit(solution)/shard_map/ppermute | solution.py:570
  86.9 15.5 %collective-permute-start.13 = (bf16[1152,128]{1,0:T(8,128)(2,1)}, bf16[1152,128]{1,0:T(8,128)(2,1)S(1)}, u32[]{:S(2)}, u32[]{:S(2)}) collective-permute-start(bf16[1152,128]{1,0:T(8,128)(2,1)} %get-tuple-element.82), channel_id=1, source_target_pairs={{0,96},{32,64},{64,32},{96,0},{1,97},{33,65},{65,33},{97,1},{2,98}... | collective-permute-start | bytes 884744 | tf_op jit(solution)/shard_map/ppermute | solution.py:570
  (2 other events, 2.4 us)

commit v4 on v3

--- a/solution.py
+++ b/solution.py
@@ -13,8 +13,8 @@
 BLOCK = 16
 GROUP = 8
 EXTRA = 16
-CHUNKS = (16, 16)
-HOME = ((0,), (1,))
+CHUNKS = (8, 8, 16)
+HOME = ((0, 1), (2,))
 MIB = 1024 * 1024
 AXES = ("spec", "tile")
 f32, bf16, i32 = jnp.float32, jnp.bfloat16, jnp.int32

time: 122 us -> 119 us (0.975)
  waiting for transfers between devices: 30.7 us -> 24.1 us
  starting transfers between devices: 27.5 us -> 29.2 us
  Pallas kernels: 60.5 us -> 61.8 us
    ppermute x12 -> x15, waiting for transfers between devices: 23.8 us -> 18.3 us  [swap(): lax.ppermute(parts[k], 'spec', [(i, i ^ k) for i in range(4)])]
    ppermute x12 -> x15, starting transfers between devices: 10.1 us -> 11.8 us  [swap(): lax.ppermute(parts[k], 'spec', [(i, i ^ k) for i in range(4)])]
    pallas_call x2 -> x3, Pallas kernels: 24.1 us -> 25.3 us  [chemistry(): pl.pallas_call(functools.partial(chem_kernel, slots), grid=(count // slot...]
  transfers between devices with their start and end apart: 15 -> 18, of which waited for: 7 -> 7; matrix products, arithmetic and copies ran while one was open for 1% -> 1% of each run, Pallas kernels for 39% -> 42%
where the time goes in v4:
time: 119 us; the launch traced here: 118 us
  Pallas kernels  61.8 us (52%)
  starting transfers between devices  29.2 us (25%)
  waiting for transfers between devices  24.1 us (20%)
  local copies, waits for them, and re-layouts  2.44 us (2%)
    pallas_call x3, Pallas kernels, chemistry(): pl.pallas_call(functools.partial(chem_kernel, slots), grid=(count // slot...  25.3 us
    ppermute x15, waiting for transfers between devices, swap(): lax.ppermute(parts[k], 'spec', [(i, i ^ k) for i in range(4)])  18.3 us
    pallas_call x1, Pallas kernels, interior(): pl.pallas_call(interior_kernel, in_specs=[smem()] + [anywhere()] * 3, out...  12.7 us
    ppermute x15, starting transfers between devices, swap(): lax.ppermute(parts[k], 'spec', [(i, i ^ k) for i in range(4)])  11.8 us
    all_to_all x1, starting transfers between devices, shards(): lax.all_to_all(own, AXES, 0, 0, axis_index_groups=sides(), tiled=True)  10.6 us
    pallas_call x1, Pallas kernels, finish(): pl.pallas_call(functools.partial(finish_kernel, wide), grid=(n // wide,),...  9.82 us
    pallas_call x1, Pallas kernels, border(): pl.pallas_call(functools.partial(border_kernel, chunks), in_specs=[smem()...  7.11 us
    ppermute x1, starting transfers between devices, shards(): west = lax.ppermute(west, 'tile', [(i, i + 1) for i in range(31)])  5.5 us
  transfers between devices with their start and end apart: 18, of which 7 were waited for; matrix products, arithmetic and copies ran while one was open for 1% of the time, Pallas kernels for 42%

profile of v4, /device:TPU:1, one launch (start us, length us, event | category | flops | bytes accessed | tf_op | source)
XLA Modules:
  0.0 118.4 jit_solution(4725041642944389651)
XLA Ops:
  0.6 3.3 %pack_halo.1 = (bf16[1168,128]{1,0:T(8,128)(2,1)}, bf16[1168,128]{1,0:T(8,128)(2,1)}) custom-call(f32[9216,128]{1,0:T(8,128)} %bitcast.21, f32[4,16,128]{2,1,0:T(8,128)} %courant.5, s32[2,16,128]{2,1,0:T(8,128)} %nbr.5), custom_call_target="tpu_custom_call" | custom-call | bytes 6291456 | tf_op jit(solution)/shard_map/pack_halo/pallas_call | solution.py:91
  4.0 5.5 %collective-permute-start = (bf16[1168,128]{1,0:T(8,128)(2,1)}, bf16[1168,128]{1,0:T(8,128)(2,1)S(1)}, u32[]{:S(2)}, u32[]{:S(2)}) collective-permute-start(bf16[1168,128]{1,0:T(8,128)(2,1)} %get-tuple-element.53), channel_id=1, source_target_pairs={{0,1},{1,2},{2,3},{3,4},{4,5},{5,6},{6,7},{7,8},{8,9},{9,10},{10,1... | collective-permute-start | bytes 897032 | tf_op jit(solution)/shard_map/ppermute | solution.py:557
  9.5 1.3 %collective-permute-start.1 = (bf16[1168,128]{1,0:T(8,128)(2,1)}, bf16[1168,128]{1,0:T(8,128)(2,1)S(1)}, u32[]{:S(2)}, u32[]{:S(2)}) collective-permute-start(bf16[1168,128]{1,0:T(8,128)(2,1)} %get-tuple-element.54), channel_id=1, source_target_pairs={{1,0},{2,1},{3,2},{4,3},{5,4},{6,5},{7,6},{8,7},{9,8},{10,9},{11,1... | collective-permute-start | bytes 897032 | tf_op jit(solution)/shard_map/ppermute | solution.py:558
  10.8 12.7 %interior.1 = (f32[12,576,128]{2,1,0:T(8,128)}, f32[8,576,128]{2,1,0:T(8,128)S(1)}, f32[128,72,128]{2,1,0:T(8,128)}) custom-call(s32[128]{0:T(128)S(1)} %multiply_add_fusion.place, f32[9216,128]{1,0:T(8,128)} %bitcast.22, f32[4,16,128]{2,1,0:T(8,128)} %courant.5, s32[2,16,128]{2,1,0:T(8,128)} %nbr.5), custom_call_target="tpu_custom_call" | custom-call | flops 8999999488 | bytes 16777216 | tf_op jit(solution)/shard_map/interior/pallas_call | solution.py:225
  23.8 7.1 %border.1 = (f32[4,576,128]{2,1,0:T(8,128)}, bf16[576,128]{1,0:T(8,128)(2,1)}, bf16[576,128]{1,0:T(8,128)(2,1)}, bf16[576,128]{1,0:T(8,128)(2,1)}, bf16[576,128]...) custom-call(s32[128]{0:T(128)S(1)} %multiply_add_fusion.place, ...), custom_call_target="tpu_custom_call" | custom-call | flops 3000000000 | bytes 11534336 | tf_op jit(solution)/shard_map/border/pallas_call | solution.py:330
  30.9 1.6 %collective-permute-start.8 = (bf16[576,128]{1,0:T(8,128)(2,1)}, bf16[576,128]{1,0:T(8,128)(2,1)}, u32[]{:S(2)}, u32[]{:S(2)}) collective-permute-start(bf16[576,128]{1,0:T(8,128)(2,1)} %get-tuple-element.79), channel_id=1, source_target_pairs={{0,32},{32,0},{64,96},{96,64},{1,33},{33,1},{65,97},{97,65},{2,34}... | collective-permute-start | bytes 442376 | tf_op jit(solution)/shard_map/ppermute | solution.py:570
  32.6 1.2 %collective-permute-start.9 = (bf16[576,128]{1,0:T(8,128)(2,1)}, bf16[576,128]{1,0:T(8,128)(2,1)}, u32[]{:S(2)}, u32[]{:S(2)}) collective-permute-start(bf16[576,128]{1,0:T(8,128)(2,1)} %get-tuple-element.80), channel_id=1, source_target_pairs={{0,64},{32,96},{64,0},{96,32},{1,65},{33,97},{65,1},{97,33},{2,66}... | collective-permute-start | bytes 442376 | tf_op jit(solution)/shard_map/ppermute | solution.py:570
  34.5 1.2 %collective-permute-start.6 = (bf16[576,128]{1,0:T(8,128)(2,1)}, bf16[576,128]{1,0:T(8,128)(2,1)}, u32[]{:S(2)}, u32[]{:S(2)}) collective-permute-start(bf16[576,128]{1,0:T(8,128)(2,1)} %get-tuple-element.76), channel_id=1, source_target_pairs={{0,64},{32,96},{64,0},{96,32},{1,65},{33,97},{65,1},{97,33},{2,66}... | collective-permute-start | bytes 442376 | tf_op jit(solution)/shard_map/ppermute | solution.py:570
  35.7 1.4 %copy.18.w_out = bf16[1024,288]{1,0:T(8,128)(2,1)S(1)} copy(bf16[1024,288]{0,1:T(8,128)(2,1)} %param.19) | data formatting | bytes 1179648 | tf_op jit(solution)/shard_map/optimization_barrier | solution.py:573
  37.3 1.4 %turn_weights.1 = (bf16[1024,288]{1,0:T(8,128)(2,1)S(1)}, bf16[1024,1024]{1,0:T(8,128)(2,1)S(1)}, bf16[288,1024]{1,0:T(8,128)(2,1)S(1)}, f32[1024,128]{1,0:T(8,1...) custom-call(f32[1,288]{1,0:T(1,128)S(1)} %broadcast_in_dim.9.gain, bf16[288,1024]{1,0:T(8,128)(2,1)S(1)} %copy-done.1, ...), custom_call_target="tpu_custom_call" | custom-call | bytes 8388608 | tf_op jit(solution)/shard_map/turn_weights/pallas_call | solution.py:366
  39.6 2.5 %collective-permute-done.10.p3 = bf16[576,128]{1,0:T(8,128)(2,1)} collective-permute-done((bf16[576,128]{1,0:T(8,128)(2,1)}, bf16[576,128]{1,0:T(8,128)(2,1)}, u32[]{:S(2)}, u32[]{:S(2)}) %collective-permute-start.10) | collective-permute-done | bytes 147488 | tf_op jit(solution)/shard_map/ppermute | solution.py:570
  42.1 1.2 %collective-permute-start.3 = (bf16[1152,128]{1,0:T(8,128)(2,1)S(1)}, bf16[1152,128]{1,0:T(8,128)(2,1)S(1)}, u32[]{:S(2)}, u32[]{:S(2)}) collective-permute-start(bf16[1152,128]{1,0:T(8,128)(2,1)S(1)} %copy-done.12), channel_id=1, source_target_pairs={{0,64},{32,96},{64,0},{96,32},{1,65},{33,97},{65,1},{97,33},{2,66}... | collective-permute-start | bytes 884744 | tf_op jit(solution)/shard_map/ppermute | solution.py:570
  43.3 6.9 %chemistry.3 = (bf16[32,288,128]{2,1,0:T(8,128)(2,1)}, bf16[1152,128]{1,0:T(8,128)(2,1)}, bf16[1152,128]{1,0:T(8,128)(2,1)}, bf16[1152,128]{1,0:T(8,128)(2,1)}, bf16[1152,128]{1,0:T(8,128)(2,1)}) custom-call(s32[4]{0:T(128)S(1)} %iota_xor_fusion.group, f32[288,128]{1,0:T(8,128)S(1)} %get-tuple-element.64.gain, bf16[1024,288]{1,0:T(8,128)(2,1)S(1)} %get-tuple-element.65.w1, ...), custom_call_target="tpu_custom_call" | custom-call | flops 3355443200 | bytes 8388608 | tf_op jit(solution)/shard_map/chemistry/pallas_call | solution.py:440
  50.5 6.9 %chemistry.4 = (bf16[32,288,128]{2,1,0:T(8,128)(2,1)}, bf16[1152,128]{1,0:T(8,128)(2,1)}, bf16[1152,128]{1,0:T(8,128)(2,1)}, bf16[1152,128]{1,0:T(8,128)(2,1)}, bf16[1152,128]{1,0:T(8,128)(2,1)}) custom-call(s32[4]{0:T(128)S(1)} %iota_xor_fusion.group, ...), custom_call_target="tpu_custom_call", output_to_operand_aliasing={{0}: (11, {}), {1}: (12, {}), {2}: (13, {}), {3}: (14, {}),... | custom-call | flops 3355443200 | bytes 8388608 | tf_op jit(solution)/shard_map/chemistry/pallas_call | solution.py:440
  57.9 1.2 %collective-permute-start.12 = (bf16[1152,128]{1,0:T(8,128)(2,1)}, bf16[1152,128]{1,0:T(8,128)(2,1)S(1)}, u32[]{:S(2)}, u32[]{:S(2)}) collective-permute-start(bf16[1152,128]{1,0:T(8,128)(2,1)} %get-tuple-element.91), channel_id=1, source_target_pairs={{0,64},{32,96},{64,0},{96,32},{1,65},{33,97},{65,1},{97,33},{2,66}... | collective-permute-start | bytes 884744 | tf_op jit(solution)/shard_map/ppermute | solution.py:570
  60.5 11.5 %chemistry.5 = (bf16[32,288,128]{2,1,0:T(8,128)(2,1)}, bf16[1152,128]{1,0:T(8,128)(2,1)}, bf16[1152,128]{1,0:T(8,128)(2,1)}, bf16[1152,128]{1,0:T(8,128)(2,1)}, bf16[1152,128]{1,0:T(8,128)(2,1)}) custom-call(s32[4]{0:T(128)S(1)} %iota_xor_fusion.group, f32[288,128]{1,0:T(8,128)S(1)} %get-tuple-element.64.gain, ...), custom_call_target="tpu_custom_call", output_to_operand_aliasing={{0}: (11, {})} | custom-call | flops 6710886400 | bytes 8388608 | tf_op jit(solution)/shard_map/chemistry/pallas_call | solution.py:440
  72.0 1.2 collective-permute-done.13.rest_3_
  73.2 10.6 %all-to-all-start = ((bf16[32,288,128]{2,1,0:T(8,128)(2,1)}), bf16[32,288,128]{2,1,0:T(8,128)(2,1)S(1)}, u32[]{:S(2)}, u32[]{:S(2)}) async-start(bf16[32,288,128]{2,1,0:T(8,128)(2,1)} %get-tuple-element.101), calls=%async_computation | async-start | bytes 4718592 | tf_op jit(solution)/shard_map/all_to_all | solution.py:585
  84.4 1.7 %collective-permute-start.16 = (bf16[1152,128]{1,0:T(8,128)(2,1)}, bf16[1152,128]{1,0:T(8,128)(2,1)S(1)}, u32[]{:S(2)}, u32[]{:S(2)}) collective-permute-start(bf16[1152,128]{1,0:T(8,128)(2,1)} %get-tuple-element.100), channel_id=1, source_target_pairs={{0,96},{32,64},{64,32},{96,0},{1,97},{33,65},{65,33},{97,1},{2,98}... | collective-permute-start | bytes 884744 | tf_op jit(solution)/shard_map/ppermute | solution.py:570
  86.2 7.0 %collective-permute-done.15.rest_6_ = bf16[1152,128]{1,0:T(8,128)(2,1)S(1)} collective-permute-done((bf16[1152,128]{1,0:T(8,128)(2,1)}, bf16[1152,128]{1,0:T(8,128)(2,1)S(1)}, u32[]{:S(2)}, u32[]{:S(2)}) %collective-permute-start.15) | collective-permute-done | bytes 294944 | tf_op jit(solution)/shard_map/ppermute | solution.py:570
  93.2 6.8 %collective-permute-done.16.rest_7_ = bf16[1152,128]{1,0:T(8,128)(2,1)S(1)} collective-permute-done((bf16[1152,128]{1,0:T(8,128)(2,1)}, bf16[1152,128]{1,0:T(8,128)(2,1)S(1)}, u32[]{:S(2)}, u32[]{:S(2)}) %collective-permute-start.16) | collective-permute-done | bytes 294944 | tf_op jit(solution)/shard_map/ppermute | solution.py:570
  101.0 9.8 %finish.1 = f32[9216,128]{1,0:T(8,128)} custom-call(s32[128]{0:T(128)S(1)} %multiply_add_fusion.place, f32[12,8,72,128]{3,2,1,0:T(8,128)} %bitcast.24, f32[4,8,72,128]{3,2,1,0:T(8,128)} %bitcast.25, bf16[1152,128]{1,0:T(8,128)(2,1)S(1)} %copy-done.3, bf16[1152,128]{1,0:T(8,128)(2,1)S(1)} %collective-permute-done.11.rest_1_, ...), custom_call_target="tpu_custom_call" | custom-call | flops 4194304 | bytes 13631488 | tf_op jit(solution)/shard_map/finish/pallas_call | solution.py:505
  110.8 5.5 %all-to-all-done.got = bf16[32,288,128]{2,1,0:T(8,128)(2,1)S(1)} async-done(((bf16[32,288,128]{2,1,0:T(8,128)(2,1)}), bf16[32,288,128]{2,1,0:T(8,128)(2,1)S(1)}, u32[]{:S(2)}, u32[]{:S(2)}) %all-to-all-start) | async-done | bytes 2359328 | tf_op jit(solution)/shard_map/all_to_all | solution.py:585
  116.3 2.2 %deliver.1 = bf16[1,288,4096]{2,1,0:T(8,128)(2,1)} custom-call(bf16[32,288,128]{2,1,0:T(8,128)(2,1)S(1)} %all-to-all-done.got), custom_call_target="tpu_custom_call" | custom-call | bytes 5242880 | tf_op jit(solution)/shard_map/deliver/pallas_call | solution.py:530
  (55 shorter events, 5.8 us)
Async XLA Ops:
  4.0 19.5 %collective-permute-start = (bf16[1168,128]{1,0:T(8,128)(2,1)}, bf16[1168,128]{1,0:T(8,128)(2,1)S(1)}, u32[]{:S(2)}, u32[]{:S(2)}) collective-permute-start(bf16[1168,128]{1,0:T(8,128)(2,1)} %get-tuple-element.53), channel_id=1, source_target_pairs={{0,1},{1,2},{2,3},{3,4},{4,5},{5,6},{6,7},{7,8},{8,9},{9,10},{10,1... | collective-permute-start | bytes 897032 | tf_op jit(solution)/shard_map/ppermute | solution.py:557
  9.5 14.3 %collective-permute-start.1 = (bf16[1168,128]{1,0:T(8,128)(2,1)}, bf16[1168,128]{1,0:T(8,128)(2,1)S(1)}, u32[]{:S(2)}, u32[]{:S(2)}) collective-permute-start(bf16[1168,128]{1,0:T(8,128)(2,1)} %get-tuple-element.54), channel_id=1, source_target_pairs={{1,0},{2,1},{3,2},{4,3},{5,4},{6,5},{7,6},{8,7},{9,8},{10,9},{11,1... | collective-permute-start | bytes 897032 | tf_op jit(solution)/shard_map/ppermute | solution.py:558
  23.8 10.5 %copy-start.9 = (f32[288]{0:T(512)S(1)}, f32[288]{0:T(512)}, u32[]{:S(2)}) copy-start(f32[288]{0:T(512)} %param.14) | copy-start | bytes 3460
  23.8 13.4 %copy-start = (bf16[1024,1024]{1,0:T(8,128)(2,1)S(1)}, bf16[1024,1024]{1,0:T(8,128)(2,1)}, u32[]{:S(2)}) copy-start(bf16[1024,1024]{1,0:T(8,128)(2,1)} %w_mid) | copy-start | bytes 6291460
  23.8 13.4 %copy-start.1 = (bf16[288,1024]{1,0:T(8,128)(2,1)S(1)}, bf16[288,1024]{1,0:T(8,128)(2,1)}, u32[]{:S(2)}) copy-start(bf16[288,1024]{1,0:T(8,128)(2,1)} %w_in) | copy-start | bytes 1769476
  23.8 13.4 %copy-start.4 = (f32[1024]{0:T(1024)S(1)}, f32[1024]{0:T(1024)}, u32[]{:S(2)}) copy-start(f32[1024]{0:T(1024)} %param.16) | copy-start | bytes 12292
  23.8 13.4 %copy-start.5 = (f32[1024]{0:T(1024)S(1)}, f32[1024]{0:T(1024)}, u32[]{:S(2)}) copy-start(f32[1024]{0:T(1024)} %param.18) | copy-start | bytes 12292
  30.9 7.7 %collective-permute-start.8 = (bf16[576,128]{1,0:T(8,128)(2,1)}, bf16[576,128]{1,0:T(8,128)(2,1)}, u32[]{:S(2)}, u32[]{:S(2)}) collective-permute-start(bf16[576,128]{1,0:T(8,128)(2,1)} %get-tuple-element.79), channel_id=1, source_target_pairs={{0,32},{32,0},{64,96},{96,64},{1,33},{33,1},{65,97},{97,65},{2,34}... | collective-permute-start | bytes 442376 | tf_op jit(solution)/shard_map/ppermute | solution.py:570
  32.6 7.0 %collective-permute-start.9 = (bf16[576,128]{1,0:T(8,128)(2,1)}, bf16[576,128]{1,0:T(8,128)(2,1)}, u32[]{:S(2)}, u32[]{:S(2)}) collective-permute-start(bf16[576,128]{1,0:T(8,128)(2,1)} %get-tuple-element.80), channel_id=1, source_target_pairs={{0,64},{32,96},{64,0},{96,32},{1,65},{33,97},{65,1},{97,33},{2,66}... | collective-permute-start | bytes 442376 | tf_op jit(solution)/shard_map/ppermute | solution.py:570
  33.8 8.3 %collective-permute-start.10 = (bf16[576,128]{1,0:T(8,128)(2,1)}, bf16[576,128]{1,0:T(8,128)(2,1)}, u32[]{:S(2)}, u32[]{:S(2)}) collective-permute-start(bf16[576,128]{1,0:T(8,128)(2,1)} %get-tuple-element.81), channel_id=1, source_target_pairs={{0,96},{32,64},{64,32},{96,0},{1,97},{33,65},{65,33},{97,1},{2,98}... | collective-permute-start | bytes 442376 | tf_op jit(solution)/shard_map/ppermute | solution.py:570
  34.3 15.9 %collective-permute-start.5 = (bf16[576,128]{1,0:T(8,128)(2,1)}, bf16[576,128]{1,0:T(8,128)(2,1)}, u32[]{:S(2)}, u32[]{:S(2)}) collective-permute-start(bf16[576,128]{1,0:T(8,128)(2,1)} %get-tuple-element.75), channel_id=1, source_target_pairs={{0,32},{32,0},{64,96},{96,64},{1,33},{33,1},{65,97},{97,65},{2,34}... | collective-permute-start | bytes 442376 | tf_op jit(solution)/shard_map/ppermute | solution.py:570
  34.5 16.0 %collective-permute-start.6 = (bf16[576,128]{1,0:T(8,128)(2,1)}, bf16[576,128]{1,0:T(8,128)(2,1)}, u32[]{:S(2)}, u32[]{:S(2)}) collective-permute-start(bf16[576,128]{1,0:T(8,128)(2,1)} %get-tuple-element.76), channel_id=1, source_target_pairs={{0,64},{32,96},{64,0},{96,32},{1,65},{33,97},{65,1},{97,33},{2,66}... | collective-permute-start | bytes 442376 | tf_op jit(solution)/shard_map/ppermute | solution.py:570
  38.7 11.8 %collective-permute-start.7 = (bf16[576,128]{1,0:T(8,128)(2,1)S(1)}, bf16[576,128]{1,0:T(8,128)(2,1)S(1)}, u32[]{:S(2)}, u32[]{:S(2)}) collective-permute-start(bf16[576,128]{1,0:T(8,128)(2,1)S(1)} %copy-done.14), channel_id=1, source_target_pairs={{0,96},{32,64},{64,32},{96,0},{1,97},{33,65},{65,33},{97,1},{2,98}... | collective-permute-start | bytes 442376 | tf_op jit(solution)/shard_map/ppermute | solution.py:570
  39.5 19.6 %collective-permute-start.2 = (bf16[1152,128]{1,0:T(8,128)(2,1)S(1)}, bf16[1152,128]{1,0:T(8,128)(2,1)S(1)}, u32[]{:S(2)}, u32[]{:S(2)}) collective-permute-start(bf16[1152,128]{1,0:T(8,128)(2,1)S(1)} %copy-done.13), channel_id=1, source_target_pairs={{0,32},{32,0},{64,96},{96,64},{1,33},{33,1},{65,97},{97,65},{2,34}... | collective-permute-start | bytes 884744 | tf_op jit(solution)/shard_map/ppermute | solution.py:570
  42.1 17.6 %collective-permute-start.3 = (bf16[1152,128]{1,0:T(8,128)(2,1)S(1)}, bf16[1152,128]{1,0:T(8,128)(2,1)S(1)}, u32[]{:S(2)}, u32[]{:S(2)}) collective-permute-start(bf16[1152,128]{1,0:T(8,128)(2,1)S(1)} %copy-done.12), channel_id=1, source_target_pairs={{0,64},{32,96},{64,0},{96,32},{1,65},{33,97},{65,1},{97,33},{2,66}... | collective-permute-start | bytes 884744 | tf_op jit(solution)/shard_map/ppermute | solution.py:570
  50.3 10.2 %collective-permute-start.4 = (bf16[1152,128]{1,0:T(8,128)(2,1)S(1)}, bf16[1152,128]{1,0:T(8,128)(2,1)S(1)}, u32[]{:S(2)}, u32[]{:S(2)}) collective-permute-start(bf16[1152,128]{1,0:T(8,128)(2,1)S(1)} %copy-done.11), channel_id=1, source_target_pairs={{0,96},{32,64},{64,32},{96,0},{1,97},{33,65},{65,33},{97,1},{2,98}... | collective-permute-start | bytes 884744 | tf_op jit(solution)/shard_map/ppermute | solution.py:570
  57.4 14.7 %collective-permute-start.11 = (bf16[1152,128]{1,0:T(8,128)(2,1)}, bf16[1152,128]{1,0:T(8,128)(2,1)S(1)}, u32[]{:S(2)}, u32[]{:S(2)}) collective-permute-start(bf16[1152,128]{1,0:T(8,128)(2,1)} %get-tuple-element.90), channel_id=1, source_target_pairs={{0,32},{32,0},{64,96},{96,64},{1,33},{33,1},{65,97},{97,65},{2,34}... | collective-permute-start | bytes 884744 | tf_op jit(solution)/shard_map/ppermute | solution.py:570
  57.9 14.1 %collective-permute-start.12 = (bf16[1152,128]{1,0:T(8,128)(2,1)}, bf16[1152,128]{1,0:T(8,128)(2,1)S(1)}, u32[]{:S(2)}, u32[]{:S(2)}) collective-permute-start(bf16[1152,128]{1,0:T(8,128)(2,1)} %get-tuple-element.91), channel_id=1, source_target_pairs={{0,64},{32,96},{64,0},{96,32},{1,65},{33,97},{65,1},{97,33},{2,66}... | collective-permute-start | bytes 884744 | tf_op jit(solution)/shard_map/ppermute | solution.py:570
  59.2 14.1 %collective-permute-start.13 = (bf16[1152,128]{1,0:T(8,128)(2,1)}, bf16[1152,128]{1,0:T(8,128)(2,1)S(1)}, u32[]{:S(2)}, u32[]{:S(2)}) collective-permute-start(bf16[1152,128]{1,0:T(8,128)(2,1)} %get-tuple-element.92), channel_id=1, source_target_pairs={{0,96},{32,64},{64,32},{96,0},{1,97},{33,65},{65,33},{97,1},{2,98}... | collective-permute-start | bytes 884744 | tf_op jit(solution)/shard_map/ppermute | solution.py:570
  73.2 26.8 %copy-start.2 = (bf16[1152,128]{1,0:T(8,128)(2,1)S(1)}, bf16[1152,128]{1,0:T(8,128)(2,1)}, u32[]{:S(2)}) copy-start(bf16[1152,128]{1,0:T(8,128)(2,1)} %get-tuple-element.97.rest_4_) | copy-start | bytes 884740
  73.2 43.1 %all-to-all-start = ((bf16[32,288,128]{2,1,0:T(8,128)(2,1)}), bf16[32,288,128]{2,1,0:T(8,128)(2,1)S(1)}, u32[]{:S(2)}, u32[]{:S(2)}) async-start(bf16[32,288,128]{2,1,0:T(8,128)(2,1)} %get-tuple-element.101), calls=%async_computation | async-start | bytes 4718592 | tf_op jit(solution)/shard_map/all_to_all | solution.py:585
  83.9 2.3 %collective-permute-start.14 = (bf16[1152,128]{1,0:T(8,128)(2,1)}, bf16[1152,128]{1,0:T(8,128)(2,1)S(1)}, u32[]{:S(2)}, u32[]{:S(2)}) collective-permute-start(bf16[1152,128]{1,0:T(8,128)(2,1)} %get-tuple-element.98), channel_id=1, source_target_pairs={{0,32},{32,0},{64,96},{96,64},{1,33},{33,1},{65,97},{97,65},{2,34}... | collective-permute-start | bytes 884744 | tf_op jit(solution)/shard_map/ppermute | solution.py:570
  84.4 8.8 %collective-permute-start.15 = (bf16[1152,128]{1,0:T(8,128)(2,1)}, bf16[1152,128]{1,0:T(8,128)(2,1)S(1)}, u32[]{:S(2)}, u32[]{:S(2)}) collective-permute-start(bf16[1152,128]{1,0:T(8,128)(2,1)} %get-tuple-element.99), channel_id=1, source_target_pairs={{0,64},{32,96},{64,0},{96,32},{1,65},{33,97},{65,1},{97,33},{2,66}... | collective-permute-start | bytes 884744 | tf_op jit(solution)/shard_map/ppermute | solution.py:570
  84.4 15.6 %collective-permute-start.16 = (bf16[1152,128]{1,0:T(8,128)(2,1)}, bf16[1152,128]{1,0:T(8,128)(2,1)S(1)}, u32[]{:S(2)}, u32[]{:S(2)}) collective-permute-start(bf16[1152,128]{1,0:T(8,128)(2,1)} %get-tuple-element.100), channel_id=1, source_target_pairs={{0,96},{32,64},{64,32},{96,0},{1,97},{33,65},{65,33},{97,1},{2,98}... | collective-permute-start | bytes 884744 | tf_op jit(solution)/shard_map/ppermute | solution.py:570
  (9 other events, 50.1 us)

commit v5 on v4

--- a/solution.py
+++ b/solution.py
@@ -419,7 +419,7 @@
             piece[2 * i * species : 2 * (i + 1) * species, :] = jnp.concatenate([a, b], axis=0).astype(bf16)
 
 
-def chemistry(first, home, group, prepared, pieces, own, back, slots=4):
+def chemistry(first, home, group, prepared, pieces, own, back, slots=8):
     w1, w2, w3, b1, b2, gain = prepared
     species = 72
     total = 4 * species

time: 119 us -> 119 us (level)
  transfers between devices with their start and end apart: 18 -> 18, of which waited for: 7 -> 7; matrix products, arithmetic and copies ran while one was open for 1% -> 1% of each run, Pallas kernels for 42% -> 41%
where the time goes in v5:
time: 119 us; the launch traced here: 118 us
  Pallas kernels  60.8 us (51%)
  starting transfers between devices  29.5 us (25%)
  waiting for transfers between devices  24.5 us (21%)
  local copies, waits for them, and re-layouts  2.44 us (2%)
    pallas_call x3, Pallas kernels, chemistry(): pl.pallas_call(functools.partial(chem_kernel, slots), grid=(count // slot...  24.4 us
    ppermute x15, waiting for transfers between devices, swap(): lax.ppermute(parts[k], 'spec', [(i, i ^ k) for i in range(4)])  19.1 us
    pallas_call x1, Pallas kernels, interior(): pl.pallas_call(interior_kernel, in_specs=[smem()] + [anywhere()] * 3, out...  12.7 us
    ppermute x15, starting transfers between devices, swap(): lax.ppermute(parts[k], 'spec', [(i, i ^ k) for i in range(4)])  12.1 us
    all_to_all x1, starting transfers between devices, shards(): lax.all_to_all(own, AXES, 0, 0, axis_index_groups=sides(), tiled=True)  10.6 us
    pallas_call x1, Pallas kernels, finish(): pl.pallas_call(functools.partial(finish_kernel, wide), grid=(n // wide,),...  9.84 us
    pallas_call x1, Pallas kernels, border(): pl.pallas_call(functools.partial(border_kernel, chunks), in_specs=[smem()...  7.11 us
    ppermute x1, starting transfers between devices, shards(): west = lax.ppermute(west, 'tile', [(i, i + 1) for i in range(31)])  5.5 us
  transfers between devices with their start and end apart: 18, of which 7 were waited for; matrix products, arithmetic and copies ran while one was open for 1% of the time, Pallas kernels for 41%

profile of v5, /device:TPU:1, one launch (start us, length us, event | category | flops | bytes accessed | tf_op | source)
XLA Modules:
  0.0 118.1 jit_solution(4869366781949042159)
XLA Ops:
  0.6 3.3 %pack_halo.1 = (bf16[1168,128]{1,0:T(8,128)(2,1)}, bf16[1168,128]{1,0:T(8,128)(2,1)}) custom-call(f32[9216,128]{1,0:T(8,128)} %bitcast.21, f32[4,16,128]{2,1,0:T(8,128)} %courant.5, s32[2,16,128]{2,1,0:T(8,128)} %nbr.5), custom_call_target="tpu_custom_call" | custom-call | bytes 6291456 | tf_op jit(solution)/shard_map/pack_halo/pallas_call | solution.py:91
  4.0 5.5 %collective-permute-start = (bf16[1168,128]{1,0:T(8,128)(2,1)}, bf16[1168,128]{1,0:T(8,128)(2,1)S(1)}, u32[]{:S(2)}, u32[]{:S(2)}) collective-permute-start(bf16[1168,128]{1,0:T(8,128)(2,1)} %get-tuple-element.53), channel_id=1, source_target_pairs={{0,1},{1,2},{2,3},{3,4},{4,5},{5,6},{6,7},{7,8},{8,9},{9,10},{10,1... | collective-permute-start | bytes 897032 | tf_op jit(solution)/shard_map/ppermute | solution.py:557
  9.5 1.3 %collective-permute-start.1 = (bf16[1168,128]{1,0:T(8,128)(2,1)}, bf16[1168,128]{1,0:T(8,128)(2,1)S(1)}, u32[]{:S(2)}, u32[]{:S(2)}) collective-permute-start(bf16[1168,128]{1,0:T(8,128)(2,1)} %get-tuple-element.54), channel_id=1, source_target_pairs={{1,0},{2,1},{3,2},{4,3},{5,4},{6,5},{7,6},{8,7},{9,8},{10,9},{11,1... | collective-permute-start | bytes 897032 | tf_op jit(solution)/shard_map/ppermute | solution.py:558
  10.8 12.7 %interior.1 = (f32[12,576,128]{2,1,0:T(8,128)}, f32[8,576,128]{2,1,0:T(8,128)S(1)}, f32[128,72,128]{2,1,0:T(8,128)}) custom-call(s32[128]{0:T(128)S(1)} %multiply_add_fusion.place, f32[9216,128]{1,0:T(8,128)} %bitcast.22, f32[4,16,128]{2,1,0:T(8,128)} %courant.5, s32[2,16,128]{2,1,0:T(8,128)} %nbr.5), custom_call_target="tpu_custom_call" | custom-call | flops 8999999488 | bytes 16777216 | tf_op jit(solution)/shard_map/interior/pallas_call | solution.py:225
  23.8 7.1 %border.1 = (f32[4,576,128]{2,1,0:T(8,128)}, bf16[576,128]{1,0:T(8,128)(2,1)}, bf16[576,128]{1,0:T(8,128)(2,1)}, bf16[576,128]{1,0:T(8,128)(2,1)}, bf16[576,128]...) custom-call(s32[128]{0:T(128)S(1)} %multiply_add_fusion.place, ...), custom_call_target="tpu_custom_call" | custom-call | flops 3000000000 | bytes 11534336 | tf_op jit(solution)/shard_map/border/pallas_call | solution.py:330
  30.9 1.6 %collective-permute-start.8 = (bf16[576,128]{1,0:T(8,128)(2,1)}, bf16[576,128]{1,0:T(8,128)(2,1)}, u32[]{:S(2)}, u32[]{:S(2)}) collective-permute-start(bf16[576,128]{1,0:T(8,128)(2,1)} %get-tuple-element.79), channel_id=1, source_target_pairs={{0,32},{32,0},{64,96},{96,64},{1,33},{33,1},{65,97},{97,65},{2,34}... | collective-permute-start | bytes 442376 | tf_op jit(solution)/shard_map/ppermute | solution.py:570
  32.6 1.2 %collective-permute-start.9 = (bf16[576,128]{1,0:T(8,128)(2,1)}, bf16[576,128]{1,0:T(8,128)(2,1)}, u32[]{:S(2)}, u32[]{:S(2)}) collective-permute-start(bf16[576,128]{1,0:T(8,128)(2,1)} %get-tuple-element.80), channel_id=1, source_target_pairs={{0,64},{32,96},{64,0},{96,32},{1,65},{33,97},{65,1},{97,33},{2,66}... | collective-permute-start | bytes 442376 | tf_op jit(solution)/shard_map/ppermute | solution.py:570
  34.5 1.2 %collective-permute-start.6 = (bf16[576,128]{1,0:T(8,128)(2,1)}, bf16[576,128]{1,0:T(8,128)(2,1)}, u32[]{:S(2)}, u32[]{:S(2)}) collective-permute-start(bf16[576,128]{1,0:T(8,128)(2,1)} %get-tuple-element.76), channel_id=1, source_target_pairs={{0,64},{32,96},{64,0},{96,32},{1,65},{33,97},{65,1},{97,33},{2,66}... | collective-permute-start | bytes 442376 | tf_op jit(solution)/shard_map/ppermute | solution.py:570
  35.7 1.4 %copy.18.w_out = bf16[1024,288]{1,0:T(8,128)(2,1)S(1)} copy(bf16[1024,288]{0,1:T(8,128)(2,1)} %param.19) | data formatting | bytes 1179648 | tf_op jit(solution)/shard_map/optimization_barrier | solution.py:573
  37.3 1.4 %turn_weights.1 = (bf16[1024,288]{1,0:T(8,128)(2,1)S(1)}, bf16[1024,1024]{1,0:T(8,128)(2,1)S(1)}, bf16[288,1024]{1,0:T(8,128)(2,1)S(1)}, f32[1024,128]{1,0:T(8,1...) custom-call(f32[1,288]{1,0:T(1,128)S(1)} %broadcast_in_dim.9.gain, bf16[288,1024]{1,0:T(8,128)(2,1)S(1)} %copy-done.1, ...), custom_call_target="tpu_custom_call" | custom-call | bytes 8388608 | tf_op jit(solution)/shard_map/turn_weights/pallas_call | solution.py:366
  39.6 2.5 %collective-permute-done.10.p3 = bf16[576,128]{1,0:T(8,128)(2,1)} collective-permute-done((bf16[576,128]{1,0:T(8,128)(2,1)}, bf16[576,128]{1,0:T(8,128)(2,1)}, u32[]{:S(2)}, u32[]{:S(2)}) %collective-permute-start.10) | collective-permute-done | bytes 147488 | tf_op jit(solution)/shard_map/ppermute | solution.py:570
  42.1 1.2 %collective-permute-start.3 = (bf16[1152,128]{1,0:T(8,128)(2,1)S(1)}, bf16[1152,128]{1,0:T(8,128)(2,1)S(1)}, u32[]{:S(2)}, u32[]{:S(2)}) collective-permute-start(bf16[1152,128]{1,0:T(8,128)(2,1)S(1)} %copy-done.12), channel_id=1, source_target_pairs={{0,64},{32,96},{64,0},{96,32},{1,65},{33,97},{65,1},{97,33},{2,66}... | collective-permute-start | bytes 884744 | tf_op jit(solution)/shard_map/ppermute | solution.py:570
  43.3 6.7 %chemistry.3 = (bf16[32,288,128]{2,1,0:T(8,128)(2,1)}, bf16[1152,128]{1,0:T(8,128)(2,1)}, bf16[1152,128]{1,0:T(8,128)(2,1)}, bf16[1152,128]{1,0:T(8,128)(2,1)}, bf16[1152,128]{1,0:T(8,128)(2,1)}) custom-call(s32[4]{0:T(128)S(1)} %iota_xor_fusion.group, f32[288,128]{1,0:T(8,128)S(1)} %get-tuple-element.64.gain, bf16[1024,288]{1,0:T(8,128)(2,1)S(1)} %get-tuple-element.65.w1, ...), custom_call_target="tpu_custom_call" | custom-call | flops 3355443200 | bytes 8388608 | tf_op jit(solution)/shard_map/chemistry/pallas_call | solution.py:440
  50.6 6.7 %chemistry.4 = (bf16[32,288,128]{2,1,0:T(8,128)(2,1)}, bf16[1152,128]{1,0:T(8,128)(2,1)}, bf16[1152,128]{1,0:T(8,128)(2,1)}, bf16[1152,128]{1,0:T(8,128)(2,1)}, bf16[1152,128]{1,0:T(8,128)(2,1)}) custom-call(s32[4]{0:T(128)S(1)} %iota_xor_fusion.group, ...), custom_call_target="tpu_custom_call", output_to_operand_aliasing={{0}: (11, {}), {1}: (12, {}), {2}: (13, {}), {3}: (14, {}),... | custom-call | flops 3355443200 | bytes 8388608 | tf_op jit(solution)/shard_map/chemistry/pallas_call | solution.py:440
  57.8 1.2 %collective-permute-start.12 = (bf16[1152,128]{1,0:T(8,128)(2,1)}, bf16[1152,128]{1,0:T(8,128)(2,1)S(1)}, u32[]{:S(2)}, u32[]{:S(2)}) collective-permute-start(bf16[1152,128]{1,0:T(8,128)(2,1)} %get-tuple-element.91), channel_id=1, source_target_pairs={{0,64},{32,96},{64,0},{96,32},{1,65},{33,97},{65,1},{97,33},{2,66}... | collective-permute-start | bytes 884744 | tf_op jit(solution)/shard_map/ppermute | solution.py:570
  60.5 10.9 %chemistry.5 = (bf16[32,288,128]{2,1,0:T(8,128)(2,1)}, bf16[1152,128]{1,0:T(8,128)(2,1)}, bf16[1152,128]{1,0:T(8,128)(2,1)}, bf16[1152,128]{1,0:T(8,128)(2,1)}, bf16[1152,128]{1,0:T(8,128)(2,1)}) custom-call(s32[4]{0:T(128)S(1)} %iota_xor_fusion.group, f32[288,128]{1,0:T(8,128)S(1)} %get-tuple-element.64.gain, ...), custom_call_target="tpu_custom_call", output_to_operand_aliasing={{0}: (11, {})} | custom-call | flops 6710886400 | bytes 8388608 | tf_op jit(solution)/shard_map/chemistry/pallas_call | solution.py:440
  71.5 1.7 %collective-permute-done.13.rest_3_ = bf16[1152,128]{1,0:T(8,128)(2,1)S(1)} collective-permute-done((bf16[1152,128]{1,0:T(8,128)(2,1)}, bf16[1152,128]{1,0:T(8,128)(2,1)S(1)}, u32[]{:S(2)}, u32[]{:S(2)}) %collective-permute-start.13) | collective-permute-done | bytes 294944 | tf_op jit(solution)/shard_map/ppermute | solution.py:570
  73.1 10.6 %all-to-all-start = ((bf16[32,288,128]{2,1,0:T(8,128)(2,1)}), bf16[32,288,128]{2,1,0:T(8,128)(2,1)S(1)}, u32[]{:S(2)}, u32[]{:S(2)}) async-start(bf16[32,288,128]{2,1,0:T(8,128)(2,1)} %get-tuple-element.101), calls=%async_computation | async-start | bytes 4718592 | tf_op jit(solution)/shard_map/all_to_all | solution.py:585
  84.5 1.7 %collective-permute-start.16 = (bf16[1152,128]{1,0:T(8,128)(2,1)}, bf16[1152,128]{1,0:T(8,128)(2,1)S(1)}, u32[]{:S(2)}, u32[]{:S(2)}) collective-permute-start(bf16[1152,128]{1,0:T(8,128)(2,1)} %get-tuple-element.100), channel_id=1, source_target_pairs={{0,96},{32,64},{64,32},{96,0},{1,97},{33,65},{65,33},{97,1},{2,98}... | collective-permute-start | bytes 884744 | tf_op jit(solution)/shard_map/ppermute | solution.py:570
  86.3 7.0 %collective-permute-done.15.rest_6_ = bf16[1152,128]{1,0:T(8,128)(2,1)S(1)} collective-permute-done((bf16[1152,128]{1,0:T(8,128)(2,1)}, bf16[1152,128]{1,0:T(8,128)(2,1)S(1)}, u32[]{:S(2)}, u32[]{:S(2)}) %collective-permute-start.15) | collective-permute-done | bytes 294944 | tf_op jit(solution)/shard_map/ppermute | solution.py:570
  93.3 6.8 %collective-permute-done.16.rest_7_ = bf16[1152,128]{1,0:T(8,128)(2,1)S(1)} collective-permute-done((bf16[1152,128]{1,0:T(8,128)(2,1)}, bf16[1152,128]{1,0:T(8,128)(2,1)S(1)}, u32[]{:S(2)}, u32[]{:S(2)}) %collective-permute-start.16) | collective-permute-done | bytes 294944 | tf_op jit(solution)/shard_map/ppermute | solution.py:570
  101.1 9.8 %finish.1 = f32[9216,128]{1,0:T(8,128)} custom-call(s32[128]{0:T(128)S(1)} %multiply_add_fusion.place, f32[12,8,72,128]{3,2,1,0:T(8,128)} %bitcast.24, f32[4,8,72,128]{3,2,1,0:T(8,128)} %bitcast.25, bf16[1152,128]{1,0:T(8,128)(2,1)S(1)} %copy-done.3, bf16[1152,128]{1,0:T(8,128)(2,1)S(1)} %collective-permute-done.11.rest_1_, ...), custom_call_target="tpu_custom_call" | custom-call | flops 4194304 | bytes 13631488 | tf_op jit(solution)/shard_map/finish/pallas_call | solution.py:505
  110.9 5.1 %all-to-all-done.got = bf16[32,288,128]{2,1,0:T(8,128)(2,1)S(1)} async-done(((bf16[32,288,128]{2,1,0:T(8,128)(2,1)}), bf16[32,288,128]{2,1,0:T(8,128)(2,1)S(1)}, u32[]{:S(2)}, u32[]{:S(2)}) %all-to-all-start) | async-done | bytes 2359328 | tf_op jit(solution)/shard_map/all_to_all | solution.py:585
  116.0 2.2 %deliver.1 = bf16[1,288,4096]{2,1,0:T(8,128)(2,1)} custom-call(bf16[32,288,128]{2,1,0:T(8,128)(2,1)S(1)} %all-to-all-done.got), custom_call_target="tpu_custom_call" | custom-call | bytes 5242880 | tf_op jit(solution)/shard_map/deliver/pallas_call | solution.py:530
  (55 shorter events, 6.4 us)
Async XLA Ops:
  4.0 19.5 %collective-permute-start = (bf16[1168,128]{1,0:T(8,128)(2,1)}, bf16[1168,128]{1,0:T(8,128)(2,1)S(1)}, u32[]{:S(2)}, u32[]{:S(2)}) collective-permute-start(bf16[1168,128]{1,0:T(8,128)(2,1)} %get-tuple-element.53), channel_id=1, source_target_pairs={{0,1},{1,2},{2,3},{3,4},{4,5},{5,6},{6,7},{7,8},{8,9},{9,10},{10,1... | collective-permute-start | bytes 897032 | tf_op jit(solution)/shard_map/ppermute | solution.py:557
  9.5 14.3 %collective-permute-start.1 = (bf16[1168,128]{1,0:T(8,128)(2,1)}, bf16[1168,128]{1,0:T(8,128)(2,1)S(1)}, u32[]{:S(2)}, u32[]{:S(2)}) collective-permute-start(bf16[1168,128]{1,0:T(8,128)(2,1)} %get-tuple-element.54), channel_id=1, source_target_pairs={{1,0},{2,1},{3,2},{4,3},{5,4},{6,5},{7,6},{8,7},{9,8},{10,9},{11,1... | collective-permute-start | bytes 897032 | tf_op jit(solution)/shard_map/ppermute | solution.py:558
  23.8 10.5 %copy-start.9 = (f32[288]{0:T(512)S(1)}, f32[288]{0:T(512)}, u32[]{:S(2)}) copy-start(f32[288]{0:T(512)} %param.14) | copy-start | bytes 3460
  23.8 13.4 %copy-start = (bf16[1024,1024]{1,0:T(8,128)(2,1)S(1)}, bf16[1024,1024]{1,0:T(8,128)(2,1)}, u32[]{:S(2)}) copy-start(bf16[1024,1024]{1,0:T(8,128)(2,1)} %w_mid) | copy-start | bytes 6291460
  23.8 13.4 %copy-start.1 = (bf16[288,1024]{1,0:T(8,128)(2,1)S(1)}, bf16[288,1024]{1,0:T(8,128)(2,1)}, u32[]{:S(2)}) copy-start(bf16[288,1024]{1,0:T(8,128)(2,1)} %w_in) | copy-start | bytes 1769476
  23.8 13.4 %copy-start.4 = (f32[1024]{0:T(1024)S(1)}, f32[1024]{0:T(1024)}, u32[]{:S(2)}) copy-start(f32[1024]{0:T(1024)} %param.16) | copy-start | bytes 12292
  23.8 13.4 %copy-start.5 = (f32[1024]{0:T(1024)S(1)}, f32[1024]{0:T(1024)}, u32[]{:S(2)}) copy-start(f32[1024]{0:T(1024)} %param.18) | copy-start | bytes 12292
  30.9 7.7 %collective-permute-start.8 = (bf16[576,128]{1,0:T(8,128)(2,1)}, bf16[576,128]{1,0:T(8,128)(2,1)}, u32[]{:S(2)}, u32[]{:S(2)}) collective-permute-start(bf16[576,128]{1,0:T(8,128)(2,1)} %get-tuple-element.79), channel_id=1, source_target_pairs={{0,32},{32,0},{64,96},{96,64},{1,33},{33,1},{65,97},{97,65},{2,34}... | collective-permute-start | bytes 442376 | tf_op jit(solution)/shard_map/ppermute | solution.py:570
  32.6 7.0 %collective-permute-start.9 = (bf16[576,128]{1,0:T(8,128)(2,1)}, bf16[576,128]{1,0:T(8,128)(2,1)}, u32[]{:S(2)}, u32[]{:S(2)}) collective-permute-start(bf16[576,128]{1,0:T(8,128)(2,1)} %get-tuple-element.80), channel_id=1, source_target_pairs={{0,64},{32,96},{64,0},{96,32},{1,65},{33,97},{65,1},{97,33},{2,66}... | collective-permute-start | bytes 442376 | tf_op jit(solution)/shard_map/ppermute | solution.py:570
  33.8 8.3 %collective-permute-start.10 = (bf16[576,128]{1,0:T(8,128)(2,1)}, bf16[576,128]{1,0:T(8,128)(2,1)}, u32[]{:S(2)}, u32[]{:S(2)}) collective-permute-start(bf16[576,128]{1,0:T(8,128)(2,1)} %get-tuple-element.81), channel_id=1, source_target_pairs={{0,96},{32,64},{64,32},{96,0},{1,97},{33,65},{65,33},{97,1},{2,98}... | collective-permute-start | bytes 442376 | tf_op jit(solution)/shard_map/ppermute | solution.py:570
  34.3 15.8 %collective-permute-start.5 = (bf16[576,128]{1,0:T(8,128)(2,1)}, bf16[576,128]{1,0:T(8,128)(2,1)}, u32[]{:S(2)}, u32[]{:S(2)}) collective-permute-start(bf16[576,128]{1,0:T(8,128)(2,1)} %get-tuple-element.75), channel_id=1, source_target_pairs={{0,32},{32,0},{64,96},{96,64},{1,33},{33,1},{65,97},{97,65},{2,34}... | collective-permute-start | bytes 442376 | tf_op jit(solution)/shard_map/ppermute | solution.py:570
  34.5 16.0 %collective-permute-start.6 = (bf16[576,128]{1,0:T(8,128)(2,1)}, bf16[576,128]{1,0:T(8,128)(2,1)}, u32[]{:S(2)}, u32[]{:S(2)}) collective-permute-start(bf16[576,128]{1,0:T(8,128)(2,1)} %get-tuple-element.76), channel_id=1, source_target_pairs={{0,64},{32,96},{64,0},{96,32},{1,65},{33,97},{65,1},{97,33},{2,66}... | collective-permute-start | bytes 442376 | tf_op jit(solution)/shard_map/ppermute | solution.py:570
  38.7 11.9 %collective-permute-start.7 = (bf16[576,128]{1,0:T(8,128)(2,1)S(1)}, bf16[576,128]{1,0:T(8,128)(2,1)S(1)}, u32[]{:S(2)}, u32[]{:S(2)}) collective-permute-start(bf16[576,128]{1,0:T(8,128)(2,1)S(1)} %copy-done.14), channel_id=1, source_target_pairs={{0,96},{32,64},{64,32},{96,0},{1,97},{33,65},{65,33},{97,1},{2,98}... | collective-permute-start | bytes 442376 | tf_op jit(solution)/shard_map/ppermute | solution.py:570
  39.5 19.4 %collective-permute-start.2 = (bf16[1152,128]{1,0:T(8,128)(2,1)S(1)}, bf16[1152,128]{1,0:T(8,128)(2,1)S(1)}, u32[]{:S(2)}, u32[]{:S(2)}) collective-permute-start(bf16[1152,128]{1,0:T(8,128)(2,1)S(1)} %copy-done.13), channel_id=1, source_target_pairs={{0,32},{32,0},{64,96},{96,64},{1,33},{33,1},{65,97},{97,65},{2,34}... | collective-permute-start | bytes 884744 | tf_op jit(solution)/shard_map/ppermute | solution.py:570
  42.1 17.3 %collective-permute-start.3 = (bf16[1152,128]{1,0:T(8,128)(2,1)S(1)}, bf16[1152,128]{1,0:T(8,128)(2,1)S(1)}, u32[]{:S(2)}, u32[]{:S(2)}) collective-permute-start(bf16[1152,128]{1,0:T(8,128)(2,1)S(1)} %copy-done.12), channel_id=1, source_target_pairs={{0,64},{32,96},{64,0},{96,32},{1,65},{33,97},{65,1},{97,33},{2,66}... | collective-permute-start | bytes 884744 | tf_op jit(solution)/shard_map/ppermute | solution.py:570
  50.1 10.4 %collective-permute-start.4 = (bf16[1152,128]{1,0:T(8,128)(2,1)S(1)}, bf16[1152,128]{1,0:T(8,128)(2,1)S(1)}, u32[]{:S(2)}, u32[]{:S(2)}) collective-permute-start(bf16[1152,128]{1,0:T(8,128)(2,1)S(1)} %copy-done.11), channel_id=1, source_target_pairs={{0,96},{32,64},{64,32},{96,0},{1,97},{33,65},{65,33},{97,1},{2,98}... | collective-permute-start | bytes 884744 | tf_op jit(solution)/shard_map/ppermute | solution.py:570
  57.2 14.2 %collective-permute-start.11 = (bf16[1152,128]{1,0:T(8,128)(2,1)}, bf16[1152,128]{1,0:T(8,128)(2,1)S(1)}, u32[]{:S(2)}, u32[]{:S(2)}) collective-permute-start(bf16[1152,128]{1,0:T(8,128)(2,1)} %get-tuple-element.90), channel_id=1, source_target_pairs={{0,32},{32,0},{64,96},{96,64},{1,33},{33,1},{65,97},{97,65},{2,34}... | collective-permute-start | bytes 884744 | tf_op jit(solution)/shard_map/ppermute | solution.py:570
  57.8 13.7 %collective-permute-start.12 = (bf16[1152,128]{1,0:T(8,128)(2,1)}, bf16[1152,128]{1,0:T(8,128)(2,1)S(1)}, u32[]{:S(2)}, u32[]{:S(2)}) collective-permute-start(bf16[1152,128]{1,0:T(8,128)(2,1)} %get-tuple-element.91), channel_id=1, source_target_pairs={{0,64},{32,96},{64,0},{96,32},{1,65},{33,97},{65,1},{97,33},{2,66}... | collective-permute-start | bytes 884744 | tf_op jit(solution)/shard_map/ppermute | solution.py:570
  59.0 14.2 %collective-permute-start.13 = (bf16[1152,128]{1,0:T(8,128)(2,1)}, bf16[1152,128]{1,0:T(8,128)(2,1)S(1)}, u32[]{:S(2)}, u32[]{:S(2)}) collective-permute-start(bf16[1152,128]{1,0:T(8,128)(2,1)} %get-tuple-element.92), channel_id=1, source_target_pairs={{0,96},{32,64},{64,32},{96,0},{1,97},{33,65},{65,33},{97,1},{2,98}... | collective-permute-start | bytes 884744 | tf_op jit(solution)/shard_map/ppermute | solution.py:570
  73.1 27.0 %copy-start.2 = (bf16[1152,128]{1,0:T(8,128)(2,1)S(1)}, bf16[1152,128]{1,0:T(8,128)(2,1)}, u32[]{:S(2)}) copy-start(bf16[1152,128]{1,0:T(8,128)(2,1)} %get-tuple-element.97.rest_4_) | copy-start | bytes 884740
  73.1 42.9 %all-to-all-start = ((bf16[32,288,128]{2,1,0:T(8,128)(2,1)}), bf16[32,288,128]{2,1,0:T(8,128)(2,1)S(1)}, u32[]{:S(2)}, u32[]{:S(2)}) async-start(bf16[32,288,128]{2,1,0:T(8,128)(2,1)} %get-tuple-element.101), calls=%async_computation | async-start | bytes 4718592 | tf_op jit(solution)/shard_map/all_to_all | solution.py:585
  83.8 2.5 %collective-permute-start.14 = (bf16[1152,128]{1,0:T(8,128)(2,1)}, bf16[1152,128]{1,0:T(8,128)(2,1)S(1)}, u32[]{:S(2)}, u32[]{:S(2)}) collective-permute-start(bf16[1152,128]{1,0:T(8,128)(2,1)} %get-tuple-element.98), channel_id=1, source_target_pairs={{0,32},{32,0},{64,96},{96,64},{1,33},{33,1},{65,97},{97,65},{2,34}... | collective-permute-start | bytes 884744 | tf_op jit(solution)/shard_map/ppermute | solution.py:570
  84.5 8.8 %collective-permute-start.15 = (bf16[1152,128]{1,0:T(8,128)(2,1)}, bf16[1152,128]{1,0:T(8,128)(2,1)S(1)}, u32[]{:S(2)}, u32[]{:S(2)}) collective-permute-start(bf16[1152,128]{1,0:T(8,128)(2,1)} %get-tuple-element.99), channel_id=1, source_target_pairs={{0,64},{32,96},{64,0},{96,32},{1,65},{33,97},{65,1},{97,33},{2,66}... | collective-permute-start | bytes 884744 | tf_op jit(solution)/shard_map/ppermute | solution.py:570
  84.5 15.6 %collective-permute-start.16 = (bf16[1152,128]{1,0:T(8,128)(2,1)}, bf16[1152,128]{1,0:T(8,128)(2,1)S(1)}, u32[]{:S(2)}, u32[]{:S(2)}) collective-permute-start(bf16[1152,128]{1,0:T(8,128)(2,1)} %get-tuple-element.100), channel_id=1, source_target_pairs={{0,96},{32,64},{64,32},{96,0},{1,97},{33,65},{65,33},{97,1},{2,98}... | collective-permute-start | bytes 884744 | tf_op jit(solution)/shard_map/ppermute | solution.py:570
  (9 other events, 49.9 us)
